TPU v7x, 32 devices: a whole 2x2x4 slice. The times are simulated.
32 devices in a mesh: replica: 2 (over x), owner: 16 (over z, y, core).
Axes of the slice: x: 2, y: 2, z: 4, core: 2. Of those that a mesh axis runs over, the one named last changes fastest.
Arguments:
- hidden: bfloat16 [4096, 5120], P(('replica', 'owner')), parts along dimension 0, may hold values from -6 to 6
- base_weight: bfloat16 [5120, 1024], replicated, may hold values from -0.078125 to 0.078125
- factor_down: bfloat16 [16, 64, 5120], P('owner'), may hold values from -0.078125 to 0.078125
- factor_up: bfloat16 [16, 64, 1024], P('owner'), may hold values from -0.75 to 0.75
- group_variants: int32 [32, 4], P(('replica', 'owner')), parts along dimension 0, may hold values from 0 to 15, all different within a row
- row_choice: int32 [4096], P(('replica', 'owner')), parts along dimension 0, may hold values from 0 to 3
- slot_of: int32 [16], replicated, may hold values from 0 to 15, each once
Outputs:
- adapted: bfloat16 [4096, 1024], P(('replica', 'owner')), parts along dimension 0
There are 2 independent parts, one for each index of `replica`. A program takes and returns all parts, laid end to end along the dimension named above; an argument that names none is the same for every part. Nothing has to cross between parts.
Inputs may be any that keep to these rules, and one draw needn't show every extreme that they name: `group_variants`: each group lists 4 different variants; every variant is listed by some group of each replica. `slot_of`: each storage slot is taken by exactly one variant.
All inputs are finite; a program needn't handle non-finite values.
Results may differ from a plain program's by a relative error of at most 0.0041.
Values may be sent and summed in bfloat16 or wider, within the bound.
No kernel may reach another device: no remote copies, remote signals or barrier semaphores. Data moves between devices by JAX's collectives and lax.ppermute only.
A program may use at most 64 MiB of HBM per device.

v0:
```python
import jax
import jax.numpy as jnp
from jax import lax
from jax.sharding import PartitionSpec as P


def flat_pieces(factor, count):
    stored, first, second = factor.shape
    return factor.reshape(stored, count, first * second // count)


def body(hidden, base_weight, factor_down, factor_up, group_variants, row_choice, slot_of):
    count = lax.axis_size("owner")
    rows_here, width = hidden.shape
    rank = factor_down.shape[1]
    qwidth = factor_up.shape[2]
    listed = group_variants.shape[1]
    base = jnp.dot(hidden, base_weight, preferred_element_type=jnp.float32)
    select = (row_choice[:, None] == jnp.arange(listed, dtype=jnp.int32)[None, :]).astype(
        jnp.float32
    )
    down_store, up_store = (
        lax.all_to_all(
            flat_pieces(factor_down, count), "owner", split_axis=1, concat_axis=0, tiled=True
        ),
        lax.all_to_all(
            flat_pieces(factor_up, count), "owner", split_axis=1, concat_axis=0, tiled=True
        ),
    )
    down_store = down_store.reshape(down_store.shape[0], -1)
    up_store = up_store.reshape(up_store.shape[0], -1)
    every_list = lax.all_gather(group_variants, "owner", axis=0, tiled=True)
    slots = jnp.take(slot_of, every_list.T.reshape(-1), axis=0)
    send_down = jnp.take(down_store, slots, axis=0).reshape(listed, count, down_store.shape[1])
    send_up = jnp.take(up_store, slots, axis=0).reshape(listed, count, up_store.shape[1])
    got_down, got_up = (
        lax.all_to_all(send_down, "owner", split_axis=1, concat_axis=1, tiled=True),
        lax.all_to_all(send_up, "owner", split_axis=1, concat_axis=1, tiled=True),
    )
    down_full = got_down.reshape(listed, rank, width)
    up_full = got_up.reshape(listed, rank, qwidth)
    every_z = jnp.einsum("rd,cjd->rcj", hidden, down_full, preferred_element_type=jnp.float32)
    chosen_z = jnp.einsum("rcj,rc->rj", every_z, select)
    rounded_z = chosen_z.astype(jnp.bfloat16)
    masked = (select[:, :, None] * rounded_z.astype(jnp.float32)[:, None, :]).astype(jnp.bfloat16)
    delta = jnp.einsum("rcj,cjq->rq", masked, up_full, preferred_element_type=jnp.float32)
    return (base + delta).astype(jnp.bfloat16)


def solution(mesh):
    return jax.shard_map(
        body,
        mesh=mesh,
        in_specs=(
            P(("replica", "owner"), None),
            P(),
            P("owner", None, None),
            P("owner", None, None),
            P(("replica", "owner"), None),
            P(("replica", "owner")),
            P(),
        ),
        out_specs=P(("replica", "owner"), None),
        check_vma=False,
    )
```

profile of v0, /device:TPU:15, one launch (start us, length us, event | category | flops | bytes accessed | tf_op | source)
XLA Modules:
  0.0 166.3 jit_solution(5449860032435977614)
XLA Ops:
  0.0 0.0 copy-start
  0.0 1.1 reshape.179
  1.1 0.5 broadcast.128
  1.7 1.3 reduce.2
  3.0 0.7 reshape.180
  3.7 6.6 %all-to-all-start.2 = ((bf16[16,2,2048]{2,1,0:T(2,128)(2,1)}), bf16[16,2,2048]{2,1,0:T(2,128)(2,1)S(1)}, u32[]{:S(2)}, u32[]{:S(2)}) async-start(bf16[16,2,2048]{2,1,0:T(2,128)(2,1)} %reshape.180), calls=%async_computation.2 | async-start | bytes 262144 | tf_op jit(solution)/shard_map/all_to_all | solution.py:26
  10.3 15.7 %all-gather = s32[16,1,4]{2,1,0:T(1,128)S(1)} all-gather(s32[1,1,4]{2,1,0:T(1,128)} %bitcast.55), channel_id=1, replica_groups=mesh['replica'=2,'owner'=16] {'owner'}, dimensions={0}, use_global_device_ids=true | all-gather | bytes 272 | tf_op jit(solution)/shard_map/all_gather | solution.py:32
  25.9 0.1 copy.17
  26.0 0.1 reshape.141
  26.1 0.0 copy-start.1
  26.1 2.2 %reshape.178 = bf16[1,16,20480]{2,0,1:T(2,128)(2,1)S(1)} reshape(bf16[1,64,5120]{2,1,0:T(8,128)(2,1)} %param.9) | data formatting | bytes 1310720 | tf_op jit(solution)/shard_map/reshape | solution.py:9
  28.4 4.7 %reduce.3 = bf16[16,20480]{1,0:T(8,128)(2,1)S(1)} reduce(bf16[16,1,20480]{2,1,0:T(2,128)(2,1)S(1)} %bitcast.49, bf16[]{:T(256)} %broadcast.128), dimensions={1}, to_apply=%bitcast.38.reduce_sub_computation | reduce | bytes 1310722
  33.1 1.3 reshape.182
  34.4 0.0 copy-done.1
  34.4 0.8 gather_fusion
  35.2 0.1 gather.21
  35.3 0.1 copy.18
  35.4 0.0 all-to-all-done.2
  35.4 9.6 %all-to-all-start = ((bf16[16,2,10240]{2,1,0:T(2,128)(2,1)}), bf16[16,2,10240]{2,1,0:T(2,128)(2,1)S(1)}, u32[]{:S(2)}, u32[]{:S(2)}) async-start(bf16[16,2,10240]{2,1,0:T(2,128)(2,1)} %reshape.182), calls=%async_computation | async-start | bytes 1310720 | tf_op jit(solution)/shard_map/all_to_all | solution.py:23
  45.1 0.1 reshape.181
  45.2 0.2 copy.38
  45.4 0.9 gather_fusion.2
  46.2 1.3 copy_select_fusion.1
  47.5 14.0 %all-to-all-done = bf16[16,2,10240]{2,1,0:T(2,128)(2,1)S(1)} async-done(((bf16[16,2,10240]{2,1,0:T(2,128)(2,1)}), bf16[16,2,10240]{2,1,0:T(2,128)(2,1)S(1)}, u32[]{:S(2)}, u32[]{:S(2)}) %all-to-all-start) | async-done | bytes 655392 | tf_op jit(solution)/shard_map/all_to_all | solution.py:23
  61.5 0.0 copy-start.2
  61.5 0.8 copy-done.2
  62.3 4.9 %all-to-all-start.3 = ((bf16[4,16,4096]{2,0,1:T(4,128)(2,1)}), bf16[4,16,4096]{2,0,1:T(4,128)(2,1)}, u32[]{:S(2)}, u32[]{:S(2)}) async-start(bf16[4,16,4096]{2,0,1:T(4,128)(2,1)} %copy_select_fusion.1), calls=%async_computation.3 | async-start | bytes 1048576 | tf_op jit(solution)/shard_map/all_to_all | solution.py:38
  67.3 4.1 %reshape.183 = bf16[16,1,20480]{2,1,0:T(2,128)(2,1)S(1)} reshape(bf16[16,2,10240]{2,1,0:T(2,128)(2,1)} %copy-done.2) | data formatting | bytes 1310720
  71.4 0.7 copy.37
  72.1 3.7 %gather_fusion.1 = bf16[64,20480]{1,0:T(8,128)(2,1)} fusion(bf16[16,20480]{1,0:T(8,128)(2,1)S(1)} %bitcast.46, s32[1024]{0:T(1024)S(1)} %pad_clamp_fusion), kind=kCustom, calls=%fused_computation.1 | custom fusion | bytes 5243136 | tf_op jit(solution)/shard_map/jit(_take)/gather | solution.py:34
  75.8 6.8 %copy_select_fusion = bf16[4,16,20480]{2,0,1:T(4,128)(2,1)} fusion(bf16[4,16,20480]{2,1,0:T(8,128)(2,1)} %bitcast.48, pred[4,16]{0,1:T(8,128)(4,1)S(1)} %copy.18), kind=kLoop, calls=%fused_computation.3 | loop fusion | flops 1310720 | bytes 5242944 | tf_op jit(solution)/shard_map/jit(_take)/select_n | solution.py:34
  82.6 0.0 copy-start.3
  82.6 0.0 all-to-all-done.3
  82.6 6.2 %all-to-all-start.1 = ((bf16[4,16,20480]{2,0,1:T(4,128)(2,1)}), bf16[4,16,20480]{2,0,1:T(4,128)(2,1)}, u32[]{:S(2)}, u32[]{:S(2)}) async-start(bf16[4,16,20480]{2,0,1:T(4,128)(2,1)} %copy_select_fusion), calls=%async_computation.1 | async-start | bytes 5242880 | tf_op jit(solution)/shard_map/all_to_all | solution.py:37
  88.8 0.0 copy-done.3
  88.8 1.3 copy.25
  90.1 0.3 reshape.147
  90.5 57.1 %all-to-all-done.1 = bf16[4,16,20480]{2,0,1:T(4,128)(2,1)} async-done(((bf16[4,16,20480]{2,0,1:T(4,128)(2,1)}), bf16[4,16,20480]{2,0,1:T(4,128)(2,1)}, u32[]{:S(2)}, u32[]{:S(2)}) %all-to-all-start.1) | async-done | bytes 2621472 | tf_op jit(solution)/shard_map/all_to_all | solution.py:37
  147.5 4.7 %copy.21 = bf16[4,16,20480]{2,1,0:T(8,128)(2,1)} copy(bf16[4,16,20480]{2,0,1:T(4,128)(2,1)} %all-to-all-done.1) | data formatting | bytes 5242880 | tf_op jit(solution)/shard_map/all_to_all | solution.py:37
  152.2 5.0 %reshape.144 = bf16[4,64,5120]{2,1,0:T(8,128)(2,1)} reshape(bf16[4,16,20480]{2,1,0:T(8,128)(2,1)} %copy.21) | data formatting | bytes 5242880 | tf_op jit(solution)/shard_map/reshape | solution.py:40
  157.2 0.0 copy-done
  157.2 2.6 %fusion.9 = bf16[128,64]{0,1:T(8,128)(2,1)S(1)} fusion(bf16[4,64,5120]{2,1,0:T(8,128)(2,1)} %reshape.144, bf16[128,5120]{1,0:T(8,128)(2,1)S(1)} %copy-done, f32[128,4]{0,1:T(4,128)S(1)} %fusion.14), kind=kOutput, calls=%fused_computation.11 | convolution fusion | flops 335601664 | bytes 3950592 | tf_op jit(solution)/shard_map/rd,cjd->rcj/dot_general | solution.py:42
  159.8 0.3 convolution_bitcast_fusion
  160.0 6.2 %fusion.2 = bf16[128,1024]{1,0:T(8,128)(2,1)} fusion(f32[128,1024]{1,0:T(8,128)S(1)} %convolution_bitcast_fusion, bf16[128,5120]{1,0:T(8,128)(2,1)S(1)} %copy-done, bf16[5120,1024]{1,0:T(8,128)(2,1)} %param.8), kind=kOutput, calls=%fused_computation.8 | convolution fusion | flops 1342439424 | bytes 12582912 | tf_op jit(solution)/shard_map/dot_general | solution.py:18
  (7 shorter events, 0.1 us)
Async XLA Ops:
  0.0 157.2 %copy-start = (bf16[128,5120]{1,0:T(8,128)(2,1)S(1)}, bf16[128,5120]{1,0:T(8,128)(2,1)}, u32[]{:S(2)}) copy-start(bf16[128,5120]{1,0:T(8,128)(2,1)} %param.7) | copy-start | bytes 3932164
  3.7 31.7 %all-to-all-start.2 = ((bf16[16,2,2048]{2,1,0:T(2,128)(2,1)}), bf16[16,2,2048]{2,1,0:T(2,128)(2,1)S(1)}, u32[]{:S(2)}, u32[]{:S(2)}) async-start(bf16[16,2,2048]{2,1,0:T(2,128)(2,1)} %reshape.180), calls=%async_computation.2 | async-start | bytes 262144 | tf_op jit(solution)/shard_map/all_to_all | solution.py:26
  26.1 8.3 %copy-start.1 = (s32[16]{0:T(128)S(1)}, s32[16]{0:T(128)}, u32[]{:S(2)}) copy-start(s32[16]{0:T(128)} %param.13) | copy-start | bytes 196
  35.4 26.1 %all-to-all-start = ((bf16[16,2,10240]{2,1,0:T(2,128)(2,1)}), bf16[16,2,10240]{2,1,0:T(2,128)(2,1)S(1)}, u32[]{:S(2)}, u32[]{:S(2)}) async-start(bf16[16,2,10240]{2,1,0:T(2,128)(2,1)} %reshape.182), calls=%async_computation | async-start | bytes 1310720 | tf_op jit(solution)/shard_map/all_to_all | solution.py:23
  61.5 0.8 copy-start.2
  62.3 20.3 %all-to-all-start.3 = ((bf16[4,16,4096]{2,0,1:T(4,128)(2,1)}), bf16[4,16,4096]{2,0,1:T(4,128)(2,1)}, u32[]{:S(2)}, u32[]{:S(2)}) async-start(bf16[4,16,4096]{2,0,1:T(4,128)(2,1)} %copy_select_fusion.1), calls=%async_computation.3 | async-start | bytes 1048576 | tf_op jit(solution)/shard_map/all_to_all | solution.py:38
  82.6 6.2 %copy-start.3 = (s32[128]{0:T(128)S(1)}, s32[128]{0:T(128)}, u32[]{:S(2)}) copy-start(s32[128]{0:T(128)} %param.12) | copy-start | bytes 1540
  82.6 64.9 %all-to-all-start.1 = ((bf16[4,16,20480]{2,0,1:T(4,128)(2,1)}), bf16[4,16,20480]{2,0,1:T(4,128)(2,1)}, u32[]{:S(2)}, u32[]{:S(2)}) async-start(bf16[4,16,20480]{2,0,1:T(4,128)(2,1)} %copy_select_fusion), calls=%async_computation.1 | async-start | bytes 5242880 | tf_op jit(solution)/shard_map/all_to_all | solution.py:37
where the time goes:
time: 167 us; the launch traced here: 166 us
  waiting for transfers between devices  71.1 us (43%)
  local copies, waits for them, and re-layouts  28.9 us (17%)
  starting transfers between devices  27.3 us (16%)
  blocking collectives  15.7 us (9%)
  other arithmetic  14.2 us (9%)
  matrix products  9.06 us (5%)
    all_to_all x1, waiting for transfers between devices, body(): lax.all_to_all(send_down, 'owner', split_axis=1, concat_axis=1, tiled=True)  57.1 us
    all_gather x1, blocking collectives, body(): every_list = lax.all_gather(group_variants, 'owner', axis=0, tiled=True)  15.7 us
    all_to_all x1, waiting for transfers between devices, body(): lax.all_to_all(flat_pieces(factor_down, count), 'owner', split_axis=1, co...  14 us
    all_to_all x1, starting transfers between devices, body(): lax.all_to_all(flat_pieces(factor_down, count), 'owner', split_axis=1, co...  9.63 us
    unnamed x15, local copies, waits for them, and re-layouts  8.52 us
    select_n x2, other arithmetic, body(): jnp.take(down_store, slots, axis=0)  6.8 us
    all_to_all x1, starting transfers between devices, body(): lax.all_to_all(flat_pieces(factor_up, count), 'owner', split_axis=1, conc...  6.55 us
    dot_general x1, matrix products, body(): base = jnp.dot(hidden, base_weight, preferred_element_type=jnp.float32)  6.23 us
  transfers between devices with their start and end apart: 4, of which 2 were waited for; matrix products, arithmetic and copies ran while one was open for 17% of the time, Pallas kernels for 0%

commit v1 on v0

v1 whole, which is shorter than its diff:
```python
import jax
import jax.numpy as jnp
from jax import lax
from jax.sharding import PartitionSpec as P


def body(hidden, base_weight, factor_down, factor_up, group_variants, row_choice, slot_of):
    owners = lax.axis_size("owner")
    replicas = lax.axis_size("replica")
    assert replicas == 2 and owners % 4 == 0 and owners <= 256
    planes = owners // 4
    rows, width = hidden.shape
    rank = factor_down.shape[1]
    qwidth = factor_up.shape[2]
    half, qhalf = width // 2, qwidth // 2
    x = lax.axis_index("replica")
    here = lax.axis_index("owner")
    plane, column, core = here // 4, here // 2 % 2, here % 2

    def by_owner(value, flip):
        return lax.ppermute(value, "owner", [(i, i ^ flip) for i in range(owners)])

    def across(value, flip):
        pairs = [
            (r * owners + i, (1 - r) * owners + (i ^ flip)) for r in range(2) for i in range(owners)
        ]
        return lax.ppermute(value, ("replica", "owner"), pairs)

    def to_x(value):
        return across(value, 0)

    def to_y(value):
        return by_owner(value, 2)

    def to_d(value):
        return across(value, 2)

    def to_core(value):
        return by_owner(value, 1)

    variants = jnp.arange(slot_of.shape[0], dtype=jnp.int32)
    listed = jnp.sum(
        jnp.where(group_variants[0][:, None] == variants[None, :], slot_of[None, :], 0), axis=1
    )
    places = jnp.arange(listed.shape[0], dtype=jnp.int32)
    slot = jnp.sum(jnp.where(row_choice[:, None] == places[None, :], listed[None, :], 0), axis=1)
    tag = jnp.broadcast_to(slot.astype(jnp.bfloat16)[:, None], (rows, 128))

    unit = jnp.concatenate(
        [
            lax.dynamic_slice_in_dim(factor_down[0], x * half, half, axis=1),
            lax.dynamic_slice_in_dim(factor_up[0], x * qhalf, qhalf, axis=1),
        ],
        axis=1,
    )
    units = [unit] + [by_owner(unit, 4 * s) for s in range(1, planes)]

    mine = jnp.concatenate([lax.dynamic_slice_in_dim(hidden, x * half, half, axis=1), tag], axis=1)
    other = jnp.concatenate(
        [lax.dynamic_slice_in_dim(hidden, (1 - x) * half, half, axis=1), tag], axis=1
    )
    blocks = [mine, to_x(other), to_y(mine), to_d(other)]

    base = jnp.dot(hidden, base_weight, preferred_element_type=jnp.float32)

    downs = [u[:, :half] for u in units]
    downs_other = [to_core(d) for d in downs]
    ups = jnp.concatenate([u[:, half:] for u in units], axis=0)
    ups = [ups, to_x(ups), to_y(ups), to_d(ups)]
    ups_other = [to_core(u) for u in ups]

    hid = jnp.concatenate([b[:, :half] for b in blocks], axis=0)
    tags = jnp.concatenate([b[:, half : half + 1] for b in blocks], axis=0).astype(jnp.int32)
    part = jnp.zeros((4 * rows, rank), jnp.float32)
    for s in range(planes):
        first = (plane ^ s) * 4 + column * 2
        for pair, which in ((downs[s], core), (downs_other[s], 1 - core)):
            z = lax.dot_general(
                hid, pair, (((1,), (1,)), ((), ())), preferred_element_type=jnp.float32
            )
            part = jnp.where(tags == first + which, z, part)
    part = part.reshape(4, rows, rank)
    total = part[0] + to_x(part[1]) + to_y(part[2]) + to_d(part[3])
    z = total.astype(jnp.bfloat16)

    def spread(col, cor):
        ids = jnp.stack([(plane ^ s) * 4 + col * 2 + cor for s in range(planes)])
        keep = slot[:, None, None] == ids[None, :, None]
        return jnp.where(keep, z[:, None, :], 0).reshape(rows, planes * rank)

    own_half = jnp.zeros((rows, qhalf), jnp.float32)
    oth_half = jnp.zeros((rows, qhalf), jnp.float32)
    for held, cor in ((ups, core), (ups_other, 1 - core)):
        a, b = spread(column, cor), spread(1 - column, cor)
        own_half += jnp.dot(a, held[0], preferred_element_type=jnp.float32)
        oth_half += jnp.dot(a, held[1], preferred_element_type=jnp.float32)
        own_half += jnp.dot(b, held[2], preferred_element_type=jnp.float32)
        oth_half += jnp.dot(b, held[3], preferred_element_type=jnp.float32)
    delta = jnp.where(
        x == 0,
        jnp.concatenate([own_half, oth_half], axis=1),
        jnp.concatenate([oth_half, own_half], axis=1),
    )
    return (base + delta).astype(jnp.bfloat16)


def solution(mesh):
    return jax.shard_map(
        body,
        mesh=mesh,
        in_specs=(
            P(("replica", "owner"), None),
            P(),
            P("owner", None, None),
            P("owner", None, None),
            P(("replica", "owner"), None),
            P(("replica", "owner")),
            P(),
        ),
        out_specs=P(("replica", "owner"), None),
        check_vma=False,
    )
```

time: 167 us -> 82.5 us (0.49)
  the two profiles are of different devices: /device:TPU:15 before, /device:TPU:16 now
where the time goes in v1:
time: 82.5 us; the launch traced here: 81.9 us
  waiting for transfers between devices  34.2 us (41%)
  matrix products  17.2 us (21%)
  starting transfers between devices  16.6 us (20%)
  local copies, waits for them, and re-layouts  9.49 us (12%)
  other arithmetic  4.04 us (5%)
    ppermute x14, waiting for transfers between devices, by_owner(): return lax.ppermute(value, 'owner', [(i, i ^ flip) for i in range(owners)])  32.8 us
    ppermute x6, starting transfers between devices, across(): return lax.ppermute(value, ('replica', 'owner'), pairs)  9.14 us
    ppermute x14, starting transfers between devices, by_owner(): return lax.ppermute(value, 'owner', [(i, i ^ flip) for i in range(owners)])  7.45 us
    dot_general x8, matrix products, body(): lax.dot_general(hid, pair, (((1,), (1,)), ((), ())), preferred_element_ty...  7.26 us
    dot_general x1, matrix products, body(): base = jnp.dot(hidden, base_weight, preferred_element_type=jnp.float32)  6.24 us
    slice x3, local copies, waits for them, and re-layouts, body(): hid = jnp.concatenate([b[:, :half] for b in blocks], axis=0)  3.4 us
    slice x3, local copies, waits for them, and re-layouts, body(): b[:, half:half + 1]  2.58 us
  transfers between devices with their start and end apart: 20, of which 5 were waited for; matrix products, arithmetic and copies ran while one was open for 27% of the time, Pallas kernels for 0%

profile of v1, /device:TPU:16, one launch (start us, length us, event | category | flops | bytes accessed | tf_op | source)
XLA Modules:
  0.0 81.9 jit_solution(12648617508986666754)
XLA Ops:
  0.0 1.1 %copy-done = bf16[1,64,5120]{2,1,0:T(8,128)(2,1)S(1)} copy-done((bf16[1,64,5120]{2,1,0:T(8,128)(2,1)S(1)}, bf16[1,64,5120]{2,1,0:T(8,128)(2,1)}, u32[]{:S(2)}) %copy-start) | copy-done | bytes 655384
  1.1 0.9 %dynamic-slice_bitcast_fusion.1 = bf16[64,512]{1,0:T(8,128)(2,1)S(1)} fusion(bf16[1,64,1024]{2,1,0:T(8,128)(2,1)} %param.10, s32[]{:T(128)S(6)} %select_n.107), kind=kLoop, calls=%fused_computation.23 | loop fusion | bytes 131076 | tf_op jit(solution)/shard_map/dynamic_slice | solution.py:52
  2.0 1.6 %collective-permute-start.7 = (bf16[64,3072]{1,0:T(8,128)(2,1)S(1)}, bf16[64,3072]{1,0:T(8,128)(2,1)S(1)}, u32[]{:S(2)}, u32[]{:S(2)}) collective-permute-start(bf16[64,3072]{1,0:T(8,128)(2,1)S(1)} %pad_maximum_fusion.3), channel_id=1, source_target_pairs={{0,4},{1,5},{2,6},{3,7},{4,0},{5,1},{6,2},{7,3},{8,12},{9,13},{10,... | collective-permute-start | bytes 1179656 | tf_op jit(solution)/shard_map/ppermute | solution.py:21
  3.6 0.9 %select_reduce_fusion.1 = s32[4]{0:T(128)S(1)} fusion(s32[16]{0:T(128)} %param.13, s32[4]{0:T(128)} %bitcast.63), kind=kLoop, calls=%fused_computation.44 | loop fusion | flops 188 | bytes 96 | tf_op jit(solution)/shard_map/reduce_sum | solution.py:42
  4.5 0.7 select_reduce_fusion
  5.2 1.4 %constant_dynamic-slice_fusion = (bf16[128,2560]{1,0:T(8,128)(2,1)S(1)}, bf16[128,2560]{1,0:T(8,128)(2,1)S(1)}) fusion(bf16[128,5120]{1,0:T(8,128)(2,1)} %param.7, s32[]{:T(128)S(6)} %select_n.106, s32[]{:T(128)S(6)} %select_n.105), kind=kLoop, calls=%fused_computation.52 | loop fusion | bytes 2621448 | tf_op jit(solution)/shard_map/dynamic_slice | solution.py:58
  6.6 0.1 broadcast_in_dim.145
  6.7 1.2 %pad_maximum_fusion.1 = (bf16[128,2688]{1,0:T(8,128)(2,1)}, bf16[128,2688]{1,0:T(8,128)(2,1)}) fusion(bf16[128,128]{1,0:T(8,128)(2,1)S(1)} %broadcast_in_dim.145, bf16[128,2560]{1,0:T(8,128)(2,1)S(1)} %get-tuple-element.7, bf16[128,2560]{1,0:T(8,128)(2,1)S(1)} %get-tuple-element.8), kind=kLoop, calls=%fused_computation.15 | loop fusion | flops 2408448 | bytes 2719744 | tf_op jit(solution)/shard_map/concatenate | solution.py:58
  7.9 2.4 %collective-permute-start.2 = (bf16[128,2688]{1,0:T(8,128)(2,1)}, bf16[128,2688]{1,0:T(8,128)(2,1)}, u32[]{:S(2)}, u32[]{:S(2)}) collective-permute-start(bf16[128,2688]{1,0:T(8,128)(2,1)} %get-tuple-element.13), channel_id=1, source_target_pairs={{0,18},{1,19},{2,16},{3,17},{4,22},{5,23},{6,20},{7,21},{8,26},{9,... | collective-permute-start | bytes 2064392 | tf_op jit(solution)/shard_map/ppermute | solution.py:27
  10.3 0.5 collective-permute-start
  10.9 0.3 collective-permute-start.5
  11.2 1.6 %collective-permute-start.3 = (bf16[64,3072]{1,0:T(8,128)(2,1)S(1)}, bf16[64,3072]{1,0:T(8,128)(2,1)S(1)}, u32[]{:S(2)}, u32[]{:S(2)}) collective-permute-start(bf16[64,3072]{1,0:T(8,128)(2,1)S(1)} %pad_maximum_fusion.3), channel_id=1, source_target_pairs={{0,12},{1,13},{2,14},{3,15},{4,8},{5,9},{6,10},{7,11},{8,4},{9,5},... | collective-permute-start | bytes 1179656 | tf_op jit(solution)/shard_map/ppermute | solution.py:21
  12.8 1.3 %collective-permute-done.7 = bf16[64,3072]{1,0:T(8,128)(2,1)S(1)} collective-permute-done((bf16[64,3072]{1,0:T(8,128)(2,1)S(1)}, bf16[64,3072]{1,0:T(8,128)(2,1)S(1)}, u32[]{:S(2)}, u32[]{:S(2)}) %collective-permute-start.7) | collective-permute-done | bytes 393248 | tf_op jit(solution)/shard_map/ppermute | solution.py:21
  14.1 1.5 %collective-permute-start.1 = (bf16[128,2688]{1,0:T(8,128)(2,1)}, bf16[128,2688]{1,0:T(8,128)(2,1)}, u32[]{:S(2)}, u32[]{:S(2)}) collective-permute-start(bf16[128,2688]{1,0:T(8,128)(2,1)} %get-tuple-element.12), channel_id=1, source_target_pairs={{0,2},{1,3},{2,0},{3,1},{4,6},{5,7},{6,4},{7,5},{8,10},{9,11},{10,... | collective-permute-start | bytes 2064392 | tf_op jit(solution)/shard_map/ppermute | solution.py:21
  15.6 0.1 pad_add_fusion
  15.7 0.1 pad_add_fusion.2
  15.7 21.1 %collective-permute-done.5 = bf16[64,3072]{1,0:T(8,128)(2,1)S(1)} collective-permute-done((bf16[64,3072]{1,0:T(8,128)(2,1)S(1)}, bf16[64,3072]{1,0:T(8,128)(2,1)S(1)}, u32[]{:S(2)}, u32[]{:S(2)}) %collective-permute-start.5) | collective-permute-done | bytes 393248 | tf_op jit(solution)/shard_map/ppermute | solution.py:21
  36.9 0.0 collective-permute-start.9
  36.9 9.2 %collective-permute-done.3 = bf16[64,3072]{1,0:T(8,128)(2,1)S(1)} collective-permute-done((bf16[64,3072]{1,0:T(8,128)(2,1)S(1)}, bf16[64,3072]{1,0:T(8,128)(2,1)S(1)}, u32[]{:S(2)}, u32[]{:S(2)}) %collective-permute-start.3) | collective-permute-done | bytes 393248 | tf_op jit(solution)/shard_map/ppermute | solution.py:21
  46.1 0.7 pad_maximum_fusion.4
  46.8 0.5 collective-permute-start.13
  47.4 0.0 collective-permute-done.2
  47.4 2.5 %collective-permute-start.17 = (bf16[256,512]{1,0:T(8,128)(2,1)}, bf16[256,512]{1,0:T(8,128)(2,1)}, u32[]{:S(2)}, u32[]{:S(2)}) collective-permute-start(bf16[256,512]{1,0:T(8,128)(2,1)} %pad_maximum_fusion.4), channel_id=1, source_target_pairs={{0,18},{1,19},{2,16},{3,17},{4,22},{5,23},{6,20},{7,21},{8,26},{9,... | collective-permute-start | bytes 786440 | tf_op jit(solution)/shard_map/ppermute | solution.py:27
  49.9 0.9 %slice_reduce_fusion = bf16[128]{0:T(256)(128)(2,1)S(1)} fusion(bf16[128,2688]{1,0:T(8,128)(2,1)} %collective-permute-done.2), kind=kLoop, calls=%fused_computation.32 | loop fusion | bytes 512 | tf_op jit(solution)/shard_map/slice | solution.py:73
  50.8 0.6 collective-permute-start.16
  51.4 0.9 %slice_reduce_fusion.2 = bf16[128]{0:T(256)(128)(2,1)S(1)} fusion(bf16[128,2688]{1,0:T(8,128)(2,1)} %collective-permute-done), kind=kLoop, calls=%fused_computation.34 | loop fusion | bytes 512 | tf_op jit(solution)/shard_map/slice | solution.py:73
  52.3 0.1 collective-permute-start.8
  52.4 0.9 %slice_reduce_fusion.1 = bf16[128]{0:T(256)(128)(2,1)S(1)} fusion(bf16[128,2688]{1,0:T(8,128)(2,1)} %collective-permute-done.1), kind=kLoop, calls=%fused_computation.33 | loop fusion | bytes 512 | tf_op jit(solution)/shard_map/slice | solution.py:73
  53.3 1.1 %slice.72 = bf16[128,2560]{1,0:T(8,128)(2,1)S(1)} slice(bf16[128,2688]{1,0:T(8,128)(2,1)} %collective-permute-done), slice={[0:128], [0:2560]} | slice | bytes 1310720 | tf_op jit(solution)/shard_map/slice | solution.py:72
  54.4 1.1 %slice.74 = bf16[128,2560]{1,0:T(8,128)(2,1)S(1)} slice(bf16[128,2688]{1,0:T(8,128)(2,1)} %collective-permute-done.2), slice={[0:128], [0:2560]} | slice | bytes 1310720 | tf_op jit(solution)/shard_map/slice | solution.py:72
  55.5 1.1 %slice.73 = bf16[128,2560]{1,0:T(8,128)(2,1)S(1)} slice(bf16[128,2688]{1,0:T(8,128)(2,1)} %collective-permute-done.1), slice={[0:128], [0:2560]} | slice | bytes 1310720 | tf_op jit(solution)/shard_map/slice | solution.py:72
  56.7 0.2 pad_maximum_fusion
  56.9 0.9 %convolution_select_fusion = f32[512,64]{0,1:T(8,128)S(1)} fusion(bf16[512,2560]{1,0:T(8,128)(2,1)S(1)} %pad_maximum_fusion, bf16[64,2560]{1,0:T(8,128)(2,1)S(1)} %dynamic-slice_bitcast_fusion, pred[512]{0:T(512)(128)(4,1)S(1)} %get-tuple-element.24), kind=kOutput, calls=%fused_computation.7 | convolution fusion | flops 167804928 | bytes 3080704 | tf_op jit(solution)/shard_map/dot_general | solution.py:78
  57.8 0.6 collective-permute-start.6
  58.4 0.9 %convolution_select_fusion.1 = f32[512,64]{0,1:T(8,128)S(1)} fusion(f32[512,64]{0,1:T(8,128)S(1)} %convolution_select_fusion, bf16[512,2560]{1,0:T(8,128)(2,1)S(1)} %pad_maximum_fusion, bf16[64,2560]{1,0:T(8,128)(2,1)S(1)} %collective-permute-done.9, pred[512]{0:T(512)(128)(4,1)S(1)} %get-tuple-element.23), kind=kOutput, calls=%fused_computation.8 | convolution fusion | flops 167804928 | bytes 3211776 | tf_op jit(solution)/shard_map/dot_general | solution.py:78
  59.3 0.9 %convolution_select_fusion.2 = f32[512,64]{0,1:T(8,128)S(1)} fusion(f32[512,64]{0,1:T(8,128)S(1)} %convolution_select_fusion.1, bf16[512,2560]{1,0:T(8,128)(2,1)S(1)} %pad_maximum_fusion, pred[512]{0:T(512)(128)(4,1)S(1)} %get-tuple-element.22, bf16[64,3072]{1,0:T(8,128)(2,1)S(1)} %collective-permute-done.7), kind=kOutput, calls=%fused_computation.9 | convolution fusion | flops 167804928 | bytes 3211776 | tf_op jit(solution)/shard_map/dot_general | solution.py:78
  60.2 0.1 collective-permute-start.4
  60.3 0.9 %convolution_select_fusion.3 = f32[512,64]{0,1:T(8,128)S(1)} fusion(f32[512,64]{0,1:T(8,128)S(1)} %convolution_select_fusion.2, bf16[512,2560]{1,0:T(8,128)(2,1)S(1)} %pad_maximum_fusion, bf16[64,2560]{1,0:T(8,128)(2,1)S(1)} %collective-permute-done.8, pred[512]{0:T(512)(128)(4,1)S(1)} %get-tuple-element.21), kind=kOutput, calls=%fused_computation.10 | convolution fusion | flops 167804928 | bytes 3211776 | tf_op jit(solution)/shard_map/dot_general | solution.py:78
  61.2 0.9 %convolution_select_fusion.4 = f32[512,64]{0,1:T(8,128)S(1)} fusion(f32[512,64]{0,1:T(8,128)S(1)} %convolution_select_fusion.3, bf16[512,2560]{1,0:T(8,128)(2,1)S(1)} %pad_maximum_fusion, pred[512]{0:T(512)(128)(4,1)S(1)} %get-tuple-element.20, bf16[64,3072]{1,0:T(8,128)(2,1)S(1)} %collective-permute-done.5), kind=kOutput, calls=%fused_computation.11 | convolution fusion | flops 167804928 | bytes 3211776 | tf_op jit(solution)/shard_map/dot_general | solution.py:78
  62.1 0.0 collective-permute-done.6
  62.1 0.9 %convolution_select_fusion.5 = f32[512,64]{0,1:T(8,128)S(1)} fusion(f32[512,64]{0,1:T(8,128)S(1)} %convolution_select_fusion.4, bf16[512,2560]{1,0:T(8,128)(2,1)S(1)} %pad_maximum_fusion, bf16[64,2560]{1,0:T(8,128)(2,1)S(1)} %collective-permute-done.6, pred[512]{0:T(512)(128)(4,1)S(1)} %get-tuple-element.19), kind=kOutput, calls=%fused_computation.12 | convolution fusion | flops 167804928 | bytes 3211776 | tf_op jit(solution)/shard_map/dot_general | solution.py:78
  63.0 0.9 %convolution_select_fusion.6 = f32[512,64]{0,1:T(8,128)S(1)} fusion(f32[512,64]{0,1:T(8,128)S(1)} %convolution_select_fusion.5, bf16[512,2560]{1,0:T(8,128)(2,1)S(1)} %pad_maximum_fusion, pred[512]{0:T(512)(128)(4,1)S(1)} %get-tuple-element.18, bf16[64,3072]{1,0:T(8,128)(2,1)S(1)} %collective-permute-done.3), kind=kOutput, calls=%fused_computation.13 | convolution fusion | flops 167804928 | bytes 3211776 | tf_op jit(solution)/shard_map/dot_general | solution.py:78
  63.9 0.0 collective-permute-done.4
  64.0 0.9 %convolution_select_fusion.7 = f32[512,64]{0,1:T(8,128)S(1)} fusion(f32[512,64]{0,1:T(8,128)S(1)} %convolution_select_fusion.6, bf16[512,2560]{1,0:T(8,128)(2,1)S(1)} %pad_maximum_fusion, bf16[64,2560]{1,0:T(8,128)(2,1)S(1)} %collective-permute-done.4, pred[512]{0:T(512)(128)(4,1)S(1)} %get-tuple-element.5), kind=kOutput, calls=%fused_computation.14 | convolution fusion | flops 167804928 | bytes 3211776 | tf_op jit(solution)/shard_map/dot_general | solution.py:78
  64.9 1.6 %collective-permute-start.10 = (f32[128,64]{0,1:T(8,128)S(1)}, f32[128,64]{0,1:T(8,128)S(1)}, u32[]{:S(2)}, u32[]{:S(2)}) collective-permute-start(f32[128,64]{0,1:T(8,128)S(1)} %get-tuple-element.9), channel_id=1, source_target_pairs={{0,16},{1,17},{2,18},{3,19},{4,20},{5,21},{6,22},{7,23},{8,24},{9,... | collective-permute-start | bytes 98312 | tf_op jit(solution)/shard_map/ppermute | solution.py:27
  66.4 0.5 collective-permute-start.11
  66.9 0.0 collective-permute-done.13
  66.9 1.5 %collective-permute-start.12 = (f32[128,64]{0,1:T(8,128)S(1)}, f32[128,64]{0,1:T(8,128)S(1)}, u32[]{:S(2)}, u32[]{:S(2)}) collective-permute-start(f32[128,64]{0,1:T(8,128)S(1)} %get-tuple-element.10), channel_id=1, source_target_pairs={{0,18},{1,19},{2,16},{3,17},{4,22},{5,23},{6,20},{7,21},{8,26},{9,... | collective-permute-start | bytes 98312 | tf_op jit(solution)/shard_map/ppermute | solution.py:27
  68.4 0.1 broadcast_compare_fusion.1
  68.5 0.1 collective-permute-start.14
  68.6 0.5 collective-permute-start.15
  69.1 0.1 collective-permute-start.19
  69.2 1.2 %collective-permute-done.11 = f32[128,64]{0,1:T(8,128)S(1)} collective-permute-done((f32[128,64]{0,1:T(8,128)S(1)}, f32[128,64]{0,1:T(8,128)S(1)}, u32[]{:S(2)}, u32[]{:S(2)}) %collective-permute-start.11) | collective-permute-done | bytes 32800 | tf_op jit(solution)/shard_map/ppermute | solution.py:21
  70.4 1.4 %collective-permute-done.12 = f32[128,64]{0,1:T(8,128)S(1)} collective-permute-done((f32[128,64]{0,1:T(8,128)S(1)}, f32[128,64]{0,1:T(8,128)S(1)}, u32[]{:S(2)}, u32[]{:S(2)}) %collective-permute-start.12) | collective-permute-done | bytes 32800 | tf_op jit(solution)/shard_map/ppermute | solution.py:27
  71.8 0.2 fusion.11
  72.0 0.2 fusion.12
  72.2 0.0 copy-start.1
  72.3 0.2 fusion.1
  72.5 1.3 %fusion.13 = f32[128,512]{1,0:T(8,128)S(1)} fusion(bf16[128,256]{0,1:T(8,128)(2,1)S(1)} %bitcast.58, bf16[256,512]{1,0:T(8,128)(2,1)} %collective-permute-done.17), kind=kOutput, calls=%fused_computation.64 | convolution fusion | flops 33554432 | bytes 589824 | tf_op jit(solution)/shard_map/dot_general | solution.py:98
  73.8 1.2 %convolution_add_fusion.1 = f32[128,512]{1,0:T(8,128)S(1)} fusion(f32[128,512]{1,0:T(8,128)S(1)} %fusion.13, bf16[128,256]{0,1:T(8,128)(2,1)S(1)} %bitcast.62, bf16[256,512]{1,0:T(8,128)(2,1)} %collective-permute-done.16), kind=kOutput, calls=%fused_computation.3 | convolution fusion | flops 33619968 | bytes 851968 | tf_op jit(solution)/shard_map/dot_general | solution.py:96
  74.9 0.2 fusion.14
  75.2 0.2 convolution_add_fusion.2
  75.4 0.2 fusion
  75.6 6.2 %fusion.3 = bf16[128,1024]{1,0:T(8,128)(2,1)} fusion(f32[128,512]{1,0:T(8,128)S(1)} %fusion, f32[128,512]{1,0:T(8,128)S(1)} %convolution_add_fusion.2, pred[]{:T(512)S(6)} %eq.188, bf16[128,5120]{1,0:T(8,128)(2,1)S(1)} %copy-done.1, bf16[5120,1024]{1,0:T(8,128)(2,1)} %param.8), kind=kOutput, calls=%fused_computation.19 | convolution fusion | flops 1342832640 | bytes 12582913 | tf_op jit(solution)/shard_map/dot_general | solution.py:64
  (28 shorter events, 0.3 us)
Async XLA Ops:
  0.0 1.1 %copy-start = (bf16[1,64,5120]{2,1,0:T(8,128)(2,1)S(1)}, bf16[1,64,5120]{2,1,0:T(8,128)(2,1)}, u32[]{:S(2)}) copy-start(bf16[1,64,5120]{2,1,0:T(8,128)(2,1)} %param.9) | copy-start | bytes 1966084
  2.0 12.1 %collective-permute-start.7 = (bf16[64,3072]{1,0:T(8,128)(2,1)S(1)}, bf16[64,3072]{1,0:T(8,128)(2,1)S(1)}, u32[]{:S(2)}, u32[]{:S(2)}) collective-permute-start(bf16[64,3072]{1,0:T(8,128)(2,1)S(1)} %pad_maximum_fusion.3), channel_id=1, source_target_pairs={{0,4},{1,5},{2,6},{3,7},{4,0},{5,1},{6,2},{7,3},{8,12},{9,13},{10,... | collective-permute-start | bytes 1179656 | tf_op jit(solution)/shard_map/ppermute | solution.py:21
  7.9 39.5 %collective-permute-start.2 = (bf16[128,2688]{1,0:T(8,128)(2,1)}, bf16[128,2688]{1,0:T(8,128)(2,1)}, u32[]{:S(2)}, u32[]{:S(2)}) collective-permute-start(bf16[128,2688]{1,0:T(8,128)(2,1)} %get-tuple-element.13), channel_id=1, source_target_pairs={{0,18},{1,19},{2,16},{3,17},{4,22},{5,23},{6,20},{7,21},{8,26},{9,... | collective-permute-start | bytes 2064392 | tf_op jit(solution)/shard_map/ppermute | solution.py:27
  10.3 40.5 %collective-permute-start = (bf16[128,2688]{1,0:T(8,128)(2,1)}, bf16[128,2688]{1,0:T(8,128)(2,1)}, u32[]{:S(2)}, u32[]{:S(2)}) collective-permute-start(bf16[128,2688]{1,0:T(8,128)(2,1)} %get-tuple-element.13), channel_id=1, source_target_pairs={{0,16},{1,17},{2,18},{3,19},{4,20},{5,21},{6,22},{7,23},{8,24},{9,... | collective-permute-start | bytes 2064392 | tf_op jit(solution)/shard_map/ppermute | solution.py:27
  10.9 26.0 %collective-permute-start.5 = (bf16[64,3072]{1,0:T(8,128)(2,1)S(1)}, bf16[64,3072]{1,0:T(8,128)(2,1)S(1)}, u32[]{:S(2)}, u32[]{:S(2)}) collective-permute-start(bf16[64,3072]{1,0:T(8,128)(2,1)S(1)} %pad_maximum_fusion.3), channel_id=1, source_target_pairs={{0,8},{1,9},{2,10},{3,11},{4,12},{5,13},{6,14},{7,15},{8,0},{9,1},... | collective-permute-start | bytes 1179656 | tf_op jit(solution)/shard_map/ppermute | solution.py:21
  11.2 34.9 %collective-permute-start.3 = (bf16[64,3072]{1,0:T(8,128)(2,1)S(1)}, bf16[64,3072]{1,0:T(8,128)(2,1)S(1)}, u32[]{:S(2)}, u32[]{:S(2)}) collective-permute-start(bf16[64,3072]{1,0:T(8,128)(2,1)S(1)} %pad_maximum_fusion.3), channel_id=1, source_target_pairs={{0,12},{1,13},{2,14},{3,15},{4,8},{5,9},{6,10},{7,11},{8,4},{9,5},... | collective-permute-start | bytes 1179656 | tf_op jit(solution)/shard_map/ppermute | solution.py:21
  14.1 38.2 %collective-permute-start.1 = (bf16[128,2688]{1,0:T(8,128)(2,1)}, bf16[128,2688]{1,0:T(8,128)(2,1)}, u32[]{:S(2)}, u32[]{:S(2)}) collective-permute-start(bf16[128,2688]{1,0:T(8,128)(2,1)} %get-tuple-element.12), channel_id=1, source_target_pairs={{0,2},{1,3},{2,0},{3,1},{4,6},{5,7},{6,4},{7,5},{8,10},{9,11},{10,... | collective-permute-start | bytes 2064392 | tf_op jit(solution)/shard_map/ppermute | solution.py:21
  36.9 21.0 %collective-permute-start.9 = (bf16[64,2560]{1,0:T(8,128)(2,1)S(1)}, bf16[64,2560]{1,0:T(8,128)(2,1)S(1)}, u32[]{:S(2)}, u32[]{:S(2)}) collective-permute-start(bf16[64,2560]{1,0:T(8,128)(2,1)S(1)} %dynamic-slice_bitcast_fusion), channel_id=1, source_target_pairs={{0,1},{1,0},{2,3},{3,2},{4,5},{5,4},{6,7},{7,6},{8,9},{9,8},{10,11... | collective-permute-start | bytes 983048 | tf_op jit(solution)/shard_map/ppermute | solution.py:21
  46.8 20.1 %collective-permute-start.13 = (bf16[256,512]{1,0:T(8,128)(2,1)}, bf16[256,512]{1,0:T(8,128)(2,1)S(1)}, u32[]{:S(2)}, u32[]{:S(2)}) collective-permute-start(bf16[256,512]{1,0:T(8,128)(2,1)} %pad_maximum_fusion.4), channel_id=1, source_target_pairs={{0,2},{1,3},{2,0},{3,1},{4,6},{5,7},{6,4},{7,5},{8,10},{9,11},{10,... | collective-permute-start | bytes 786440 | tf_op jit(solution)/shard_map/ppermute | solution.py:21
  47.4 21.1 %collective-permute-start.17 = (bf16[256,512]{1,0:T(8,128)(2,1)}, bf16[256,512]{1,0:T(8,128)(2,1)}, u32[]{:S(2)}, u32[]{:S(2)}) collective-permute-start(bf16[256,512]{1,0:T(8,128)(2,1)} %pad_maximum_fusion.4), channel_id=1, source_target_pairs={{0,18},{1,19},{2,16},{3,17},{4,22},{5,23},{6,20},{7,21},{8,26},{9,... | collective-permute-start | bytes 786440 | tf_op jit(solution)/shard_map/ppermute | solution.py:27
  50.8 17.8 %collective-permute-start.16 = (bf16[256,512]{1,0:T(8,128)(2,1)}, bf16[256,512]{1,0:T(8,128)(2,1)}, u32[]{:S(2)}, u32[]{:S(2)}) collective-permute-start(bf16[256,512]{1,0:T(8,128)(2,1)} %pad_maximum_fusion.4), channel_id=1, source_target_pairs={{0,16},{1,17},{2,18},{3,19},{4,20},{5,21},{6,22},{7,23},{8,24},{9,... | collective-permute-start | bytes 786440 | tf_op jit(solution)/shard_map/ppermute | solution.py:27
  52.3 7.9 %collective-permute-start.8 = (bf16[64,2560]{1,0:T(8,128)(2,1)S(1)}, bf16[64,2560]{1,0:T(8,128)(2,1)S(1)}, u32[]{:S(2)}, u32[]{:S(2)}) collective-permute-start(bf16[64,2560]{1,0:T(8,128)(2,1)S(1)} %slice.77), channel_id=1, source_target_pairs={{0,1},{1,0},{2,3},{3,2},{4,5},{5,4},{6,7},{7,6},{8,9},{9,8},{10,11... | collective-permute-start | bytes 983048 | tf_op jit(solution)/shard_map/ppermute | solution.py:21
  57.8 4.3 %collective-permute-start.6 = (bf16[64,2560]{1,0:T(8,128)(2,1)S(1)}, bf16[64,2560]{1,0:T(8,128)(2,1)S(1)}, u32[]{:S(2)}, u32[]{:S(2)}) collective-permute-start(bf16[64,2560]{1,0:T(8,128)(2,1)S(1)} %slice.76), channel_id=1, source_target_pairs={{0,1},{1,0},{2,3},{3,2},{4,5},{5,4},{6,7},{7,6},{8,9},{9,8},{10,11... | collective-permute-start | bytes 983048 | tf_op jit(solution)/shard_map/ppermute | solution.py:21
  60.2 3.7 %collective-permute-start.4 = (bf16[64,2560]{1,0:T(8,128)(2,1)S(1)}, bf16[64,2560]{1,0:T(8,128)(2,1)S(1)}, u32[]{:S(2)}, u32[]{:S(2)}) collective-permute-start(bf16[64,2560]{1,0:T(8,128)(2,1)S(1)} %slice.75), channel_id=1, source_target_pairs={{0,1},{1,0},{2,3},{3,2},{4,5},{5,4},{6,7},{7,6},{8,9},{9,8},{10,11... | collective-permute-start | bytes 983048 | tf_op jit(solution)/shard_map/ppermute | solution.py:21
  64.9 4.2 %collective-permute-start.10 = (f32[128,64]{0,1:T(8,128)S(1)}, f32[128,64]{0,1:T(8,128)S(1)}, u32[]{:S(2)}, u32[]{:S(2)}) collective-permute-start(f32[128,64]{0,1:T(8,128)S(1)} %get-tuple-element.9), channel_id=1, source_target_pairs={{0,16},{1,17},{2,18},{3,19},{4,20},{5,21},{6,22},{7,23},{8,24},{9,... | collective-permute-start | bytes 98312 | tf_op jit(solution)/shard_map/ppermute | solution.py:27
  66.4 3.9 %collective-permute-start.11 = (f32[128,64]{0,1:T(8,128)S(1)}, f32[128,64]{0,1:T(8,128)S(1)}, u32[]{:S(2)}, u32[]{:S(2)}) collective-permute-start(f32[128,64]{0,1:T(8,128)S(1)} %get-tuple-element.11), channel_id=1, source_target_pairs={{0,2},{1,3},{2,0},{3,1},{4,6},{5,7},{6,4},{7,5},{8,10},{9,11},{10,... | collective-permute-start | bytes 98312 | tf_op jit(solution)/shard_map/ppermute | solution.py:21
  66.9 4.8 %collective-permute-start.12 = (f32[128,64]{0,1:T(8,128)S(1)}, f32[128,64]{0,1:T(8,128)S(1)}, u32[]{:S(2)}, u32[]{:S(2)}) collective-permute-start(f32[128,64]{0,1:T(8,128)S(1)} %get-tuple-element.10), channel_id=1, source_target_pairs={{0,18},{1,19},{2,16},{3,17},{4,22},{5,23},{6,20},{7,21},{8,26},{9,... | collective-permute-start | bytes 98312 | tf_op jit(solution)/shard_map/ppermute | solution.py:27
  68.5 3.5 %collective-permute-start.14 = (bf16[256,512]{1,0:T(8,128)(2,1)}, bf16[256,512]{1,0:T(8,128)(2,1)S(1)}, u32[]{:S(2)}, u32[]{:S(2)}) collective-permute-start(bf16[256,512]{1,0:T(8,128)(2,1)} %pad_maximum_fusion.4), channel_id=1, source_target_pairs={{0,1},{1,0},{2,3},{3,2},{4,5},{5,4},{6,7},{7,6},{8,9},{9,8},{10,11... | collective-permute-start | bytes 786440 | tf_op jit(solution)/shard_map/ppermute | solution.py:21
  68.6 6.5 %collective-permute-start.15 = (bf16[256,512]{1,0:T(8,128)(2,1)S(1)}, bf16[256,512]{1,0:T(8,128)(2,1)S(1)}, u32[]{:S(2)}, u32[]{:S(2)}) collective-permute-start(bf16[256,512]{1,0:T(8,128)(2,1)S(1)} %collective-permute-done.13), channel_id=1, source_target_pairs={{0,1},{1,0},{2,3},{3,2},{4,5},{5,4},{6,7},{7,6},{8,9},{9,8},{10,11... | collective-permute-start | bytes 786440 | tf_op jit(solution)/shard_map/ppermute | solution.py:21
  69.1 5.8 %collective-permute-start.19 = (bf16[256,512]{1,0:T(8,128)(2,1)}, bf16[256,512]{1,0:T(8,128)(2,1)S(1)}, u32[]{:S(2)}, u32[]{:S(2)}) collective-permute-start(bf16[256,512]{1,0:T(8,128)(2,1)} %collective-permute-done.17), channel_id=1, source_target_pairs={{0,1},{1,0},{2,3},{3,2},{4,5},{5,4},{6,7},{7,6},{8,9},{9,8},{10,11... | collective-permute-start | bytes 786440 | tf_op jit(solution)/shard_map/ppermute | solution.py:21
  70.4 5.0 %collective-permute-start.18 = (bf16[256,512]{1,0:T(8,128)(2,1)}, bf16[256,512]{1,0:T(8,128)(2,1)S(1)}, u32[]{:S(2)}, u32[]{:S(2)}) collective-permute-start(bf16[256,512]{1,0:T(8,128)(2,1)} %collective-permute-done.16), channel_id=1, source_target_pairs={{0,1},{1,0},{2,3},{3,2},{4,5},{5,4},{6,7},{7,6},{8,9},{9,8},{10,11... | collective-permute-start | bytes 786440 | tf_op jit(solution)/shard_map/ppermute | solution.py:21
  72.2 3.4 %copy-start.1 = (bf16[128,5120]{1,0:T(8,128)(2,1)S(1)}, bf16[128,5120]{1,0:T(8,128)(2,1)}, u32[]{:S(2)}) copy-start(bf16[128,5120]{1,0:T(8,128)(2,1)} %param.7) | copy-start | bytes 3932164

commit v2 on v1

v2 whole, which is shorter than its diff:
```python
import functools

import jax
import jax.numpy as jnp
from jax import lax
from jax.experimental import pallas as pl
from jax.experimental.pallas import tpu as pltpu
from jax.sharding import PartitionSpec as P

TAG = 128
VMEM = pl.BlockSpec(memory_space=pltpu.VMEM)
SMEM = pl.BlockSpec(memory_space=pltpu.SMEM)


def call(kernel, out, operands, scalars=0, flops=0, scratch=()):
    moved = sum(o.size * o.dtype.itemsize for o in operands)
    moved += sum(o.size * o.dtype.itemsize for o in jax.tree.leaves(out))
    return pl.pallas_call(
        kernel,
        out_shape=out,
        in_specs=[SMEM] * scalars + [VMEM] * (len(operands) - scalars),
        out_specs=jax.tree.map(lambda _: VMEM, out),
        scratch_shapes=scratch,
        cost_estimate=pl.CostEstimate(flops=flops, bytes_accessed=moved, transcendentals=0),
        compiler_params=pltpu.CompilerParams(vmem_limit_bytes=48 << 20),
    )(*operands)


def slice_factors(place, down, up, own, swapped):
    quarter, qhalf = swapped.shape[1], own.shape[1] - swapped.shape[1]
    x, column = place[0], place[2]
    mine, theirs = x * 2 + column, x * 2 + 1 - column
    own[:, :quarter] = down[0, :, pl.ds(pl.multiple_of(mine * quarter, 128), quarter)]
    own[:, quarter:] = up[0, :, pl.ds(pl.multiple_of(x * qhalf, 128), qhalf)]
    swapped[...] = down[0, :, pl.ds(pl.multiple_of(theirs * quarter, 128), quarter)]


def slice_rows(place, hidden, slot, *outs):
    quarter = outs[0].shape[1] - TAG
    x, column = place[0], place[2]
    tag = jnp.broadcast_to(slot[...], (slot.shape[0], TAG)).astype(jnp.float32).astype(jnp.bfloat16)
    parts = (x * 2 + column, (1 - x) * 2 + column, x * 2 + 1 - column, (1 - x) * 2 + 1 - column)
    for part, out in zip(parts, outs):
        out[:, :quarter] = hidden[:, pl.ds(pl.multiple_of(part * quarter, 128), quarter)]
        out[:, quarter:] = tag


def ids_of(plane, column, core, first, count, rank):
    lane = lax.broadcasted_iota(jnp.int32, (1, count * rank), 1)
    return ((plane ^ (first + lane // rank)) * 4) + column * 2 + core


def sum_z(flipped, units, merged, place, *refs):
    plane, column, core = place[1], place[2], place[3]
    column = 1 - column if flipped else column
    blocks, refs = refs[:8], refs[8:]
    held, refs = refs[: units + merged], refs[units + merged :]
    *before, out, hid = refs
    rows, quarter = blocks[0].shape[0], blocks[0].shape[1] - TAG
    rank = held[0].shape[0]
    for i, block in enumerate(blocks):
        hid[i * rows : (i + 1) * rows, :] = block[:, :quarter]
    tags = [b[:, quarter : quarter + 1].astype(jnp.float32).astype(jnp.int32) for b in blocks]
    some = min(units, 4)
    for first in range(0, units, some):
        parts = [h[:, :quarter] for h in held[first : first + some]]
        if merged:
            parts[-1] = parts[-1] + held[units][:, :quarter]
        z = lax.dot_general(
            hid[...],
            jnp.concatenate(parts, axis=0),
            (((1,), (1,)), ((), ())),
            preferred_element_type=jnp.float32,
        )
        ids = ids_of(plane, column, core, first, some, rank)
        for i in range(8):
            kept = jnp.where(tags[i] == ids, z[i * rows : (i + 1) * rows, :], 0.0)
            kept = sum(kept[:, j : j + 128] for j in range(0, some * rank, 128))
            if first:
                out[i] += kept
            elif before:
                out[i] = before[0][i] + kept
            else:
                out[i] = kept


def add_up(planes, place, base, mine, total, swapped, *refs):
    *held, out = refs
    x, plane, column, core = place[0], place[1], place[2], place[3]
    rows, quarter = mine.shape[0], mine.shape[1] - TAG
    rank = total.shape[1] // 2
    qhalf = held[0].shape[1]
    tag = mine[:, quarter : quarter + 1].astype(jnp.float32).astype(jnp.int32)
    both = total[...] + swapped[...]
    z = (both[:, :rank] + both[:, rank:]).astype(jnp.bfloat16).astype(jnp.float32)
    some = min(planes, 4)
    spread = jnp.concatenate([z] * some, axis=1)
    near = jnp.zeros((rows, qhalf), jnp.float32)
    far = jnp.zeros((rows, qhalf), jnp.float32)
    for first in range(0, planes, some):
        span = slice(first * rank, (first + some) * rank)
        for c in range(2):
            for y in range(2):
                ids = ids_of(
                    plane, 1 - column if y else column, 1 - core if c else core, first, some, rank
                )
                picked = jnp.where(tag == ids, spread, 0.0).astype(jnp.bfloat16)
                near += jnp.dot(
                    picked, held[c * 4 + y * 2][span, :], preferred_element_type=jnp.float32
                )
                far += jnp.dot(
                    picked, held[c * 4 + y * 2 + 1][span, :], preferred_element_type=jnp.float32
                )
    at_near = pl.multiple_of(x * qhalf, 128)
    at_far = pl.multiple_of((1 - x) * qhalf, 128)
    out[:, pl.ds(at_near, qhalf)] = (base[:, pl.ds(at_near, qhalf)] + near).astype(out.dtype)
    out[:, pl.ds(at_far, qhalf)] = (base[:, pl.ds(at_far, qhalf)] + far).astype(out.dtype)


def body(hidden, base_weight, factor_down, factor_up, group_variants, row_choice, slot_of):
    owners = lax.axis_size("owner")
    assert lax.axis_size("replica") == 2 and owners % 4 == 0 and owners <= 256
    planes = owners // 4
    rows, width = hidden.shape
    rank = factor_down.shape[1]
    qwidth = factor_up.shape[2]
    quarter, qhalf = width // 4, qwidth // 2
    here = lax.axis_index("owner")
    place = jnp.stack([lax.axis_index("replica"), here // 4, (here // 2) % 2, here % 2])

    def by_owner(value, flip):
        return lax.ppermute(value, "owner", [(i, i ^ flip) for i in range(owners)])

    def between(value, pairs):
        return lax.ppermute(
            value, "owner", [(a * 4 + i, b * 4 + i) for a, b in pairs for i in range(4)]
        )

    def across(value, flip):
        pairs = [
            (r * owners + i, (1 - r) * owners + (i ^ flip)) for r in range(2) for i in range(owners)
        ]
        return lax.ppermute(value, ("replica", "owner"), pairs)

    def to_x(value):
        return across(value, 0)

    def to_y(value):
        return by_owner(value, 2)

    def to_d(value):
        return across(value, 2)

    def to_core(value):
        return by_owner(value, 1)

    def along(unit):
        if planes != 4:
            return [unit] + [by_owner(unit, 4 * s) for s in range(1, planes)]
        second = by_owner(unit, 8)
        first = by_owner(unit, 4)
        middle = between(unit, [(1, 2), (2, 1)])
        ends = between(second, [(1, 0), (2, 3)])
        return [unit, first, second, middle, ends]

    merged = 1 if planes == 4 else 0
    bf16, f32 = jnp.bfloat16, jnp.float32

    own, swapped = call(
        slice_factors,
        (
            jax.ShapeDtypeStruct((rank, quarter + qhalf), bf16),
            jax.ShapeDtypeStruct((rank, quarter), bf16),
        ),
        (place, factor_down, factor_up),
        scalars=1,
    )
    partner = to_y(swapped)
    a_units = along(own)
    b_units = along(partner)

    variants = jnp.arange(slot_of.shape[0], dtype=jnp.int32)
    listed = jnp.sum(
        jnp.where(group_variants[0][:, None] == variants[None, :], slot_of[None, :], 0), axis=1
    )
    places = jnp.arange(listed.shape[0], dtype=jnp.int32)
    slot = jnp.sum(jnp.where(row_choice[:, None] == places[None, :], listed[None, :], 0), axis=1)
    mine, for_x, for_y, for_d = call(
        slice_rows,
        (jax.ShapeDtypeStruct((rows, quarter + TAG), bf16),) * 4,
        (place, hidden, slot[:, None]),
        scalars=1,
    )
    blocks = [mine, to_x(for_x), to_y(for_y), to_d(for_d)]
    blocks = blocks + [to_core(b) for b in blocks]

    base = jnp.dot(hidden, base_weight, preferred_element_type=f32)

    ups = [u[:, quarter:] for u in a_units]
    if merged:
        ups = ups[:3] + [ups[3] + ups[4]]
    ups = jnp.concatenate(ups, axis=0)
    ups = [ups, to_x(ups), to_y(ups), to_d(ups)]
    ups = ups + [to_core(u) for u in ups]

    part_shape = jax.ShapeDtypeStruct((8, rows, 2 * rank), f32)
    scratch = [pltpu.VMEM((8 * rows, quarter), bf16)]
    flops = 2 * 8 * rows * quarter * planes * rank
    part = call(
        functools.partial(sum_z, False, planes, merged),
        part_shape,
        (place, *blocks, *a_units),
        scalars=1,
        flops=flops,
        scratch=scratch,
    )
    part = call(
        functools.partial(sum_z, True, planes, merged),
        part_shape,
        (place, *blocks, *b_units, part),
        scalars=1,
        flops=flops,
        scratch=scratch,
    )
    part = part.reshape(2, 4, rows, 2 * rank)
    total = part[:, 0] + to_x(part[:, 1]) + to_y(part[:, 2]) + to_d(part[:, 3])
    return call(
        functools.partial(add_up, planes),
        jax.ShapeDtypeStruct((rows, qwidth), bf16),
        (place, base, mine, total[0], to_core(total[1]), *ups),
        scalars=1,
        flops=2 * rows * owners * rank * qwidth,
    )


def solution(mesh):
    return jax.shard_map(
        body,
        mesh=mesh,
        in_specs=(
            P(("replica", "owner"), None),
            P(),
            P("owner", None, None),
            P("owner", None, None),
            P(("replica", "owner"), None),
            P(("replica", "owner")),
            P(),
        ),
        out_specs=P(("replica", "owner"), None),
        check_vma=False,
    )
```

time: 82.5 us -> 74 us (0.90)
  the two profiles are of different devices: /device:TPU:16 before, /device:TPU:0 now
where the time goes in v2:
time: 74 us; the launch traced here: 73.7 us
  waiting for transfers between devices  31.1 us (42%)
  starting transfers between devices  25.6 us (35%)
  Pallas kernels  5.89 us (8%)
  matrix products  5.62 us (8%)
  local copies, waits for them, and re-layouts  3.48 us (5%)
  other arithmetic  1.73 us (2%)
    ppermute x17, waiting for transfers between devices, by_owner(): return lax.ppermute(value, 'owner', [(i, i ^ flip) for i in range(owners)])  24.1 us
    ppermute x17, starting transfers between devices, by_owner(): return lax.ppermute(value, 'owner', [(i, i ^ flip) for i in range(owners)])  12.4 us
    ppermute x6, starting transfers between devices, across(): return lax.ppermute(value, ('replica', 'owner'), pairs)  9.32 us
    pallas_call x5, Pallas kernels, call(): pl.pallas_call(kernel, out_shape=out, in_specs=[SMEM] * scalars + [VMEM]...  5.89 us
    dot_general x1, matrix products, body(): base = jnp.dot(hidden, base_weight, preferred_element_type=f32)  5.62 us
    ppermute x6, waiting for transfers between devices, across(): return lax.ppermute(value, ('replica', 'owner'), pairs)  5.11 us
    ppermute x4, starting transfers between devices, between(): lax.ppermute(value, 'owner', [(a * 4 + i, b * 4 + i) for a, b in pairs fo...  3.88 us
    unnamed x8, local copies, waits for them, and re-layouts  3.31 us
  transfers between devices with their start and end apart: 27, of which 10 were waited for; matrix products, arithmetic and copies ran while one was open for 10% of the time, Pallas kernels for 5%

profile of v2, /device:TPU:0, one launch (start us, length us, event | category | flops | bytes accessed | tf_op | source)
XLA Modules:
  0.0 73.7 jit_solution(14333280893435507725)
XLA Ops:
  0.0 0.1 pad_add_fusion.place
  0.1 1.1 %copy-done.2 = bf16[1,64,5120]{2,1,0:T(8,128)(2,1)S(1)} copy-done((bf16[1,64,5120]{2,1,0:T(8,128)(2,1)S(1)}, bf16[1,64,5120]{2,1,0:T(8,128)(2,1)}, u32[]{:S(2)}) %copy-start.2) | copy-done | bytes 655384
  1.2 0.9 %copy-done.3 = bf16[1,64,1024]{2,1,0:T(8,128)(2,1)S(1)} copy-done((bf16[1,64,1024]{2,1,0:T(8,128)(2,1)S(1)}, bf16[1,64,1024]{2,1,0:T(8,128)(2,1)}, u32[]{:S(2)}) %copy-start.3) | copy-done | bytes 131096
  2.1 0.6 shard_map.74
  2.7 4.1 %collective-permute-start.13 = (bf16[64,1792]{1,0:T(8,128)(2,1)S(1)}, bf16[64,1792]{1,0:T(8,128)(2,1)S(1)}, u32[]{:S(2)}, u32[]{:S(2)}) collective-permute-start(bf16[64,1792]{1,0:T(8,128)(2,1)S(1)} %get-tuple-element.16.refs_8_), channel_id=1, source_target_pairs={{0,8},{1,9},{2,10},{3,11},{4,12},{5,13},{6,14},{7,15},{8,0},{9,1},... | collective-permute-start | bytes 688136 | tf_op jit(solution)/shard_map/ppermute | solution.py:132
  6.8 1.5 %collective-permute-start.7 = (bf16[64,1280]{1,0:T(8,128)(2,1)S(1)}, bf16[64,1280]{1,0:T(8,128)(2,1)S(1)}, u32[]{:S(2)}, u32[]{:S(2)}) collective-permute-start(bf16[64,1280]{1,0:T(8,128)(2,1)S(1)} %get-tuple-element.15), channel_id=1, source_target_pairs={{0,2},{1,3},{2,0},{3,1},{4,6},{5,7},{6,4},{7,5},{8,10},{9,11},{10,... | collective-permute-start | bytes 491528 | tf_op jit(solution)/shard_map/ppermute | solution.py:132
  8.3 0.9 %select_reduce_fusion.1 = s32[4]{0:T(128)S(1)} fusion(s32[16]{0:T(128)} %param.13, s32[4]{0:T(128)} %bitcast.38), kind=kLoop, calls=%fused_computation.12 | loop fusion | flops 188 | bytes 96 | tf_op jit(solution)/shard_map/reduce_sum | solution.py:183
  9.1 0.7 %select_reduce_fusion = s32[128]{0:T(128)S(1)} fusion(s32[4]{0:T(128)S(1)} %select_reduce_fusion.1, s32[128]{0:T(128)} %param.12), kind=kLoop, calls=%fused_computation.11 | loop fusion | flops 1408 | bytes 1040 | tf_op jit(solution)/shard_map/reduce_sum | solution.py:187
  9.9 0.1 copy.14.slot
  10.0 1.3 %copy-done = bf16[128,5120]{1,0:T(8,128)(2,1)S(1)} copy-done((bf16[128,5120]{1,0:T(8,128)(2,1)S(1)}, bf16[128,5120]{1,0:T(8,128)(2,1)}, u32[]{:S(2)}) %copy-start) | copy-done | bytes 1310744
  11.3 0.6 shard_map.73
  12.0 1.6 %collective-permute-start = (bf16[128,1408]{1,0:T(8,128)(2,1)S(1)}, bf16[128,1408]{1,0:T(8,128)(2,1)S(1)}, u32[]{:S(2)}, u32[]{:S(2)}) collective-permute-start(bf16[128,1408]{1,0:T(8,128)(2,1)S(1)} %get-tuple-element.12), channel_id=1, source_target_pairs={{0,16},{1,17},{2,18},{3,19},{4,20},{5,21},{6,22},{7,23},{8,24},{9,... | collective-permute-start | bytes 1081352 | tf_op jit(solution)/shard_map/ppermute | solution.py:143
  13.5 1.6 %collective-permute-start.12 = (bf16[64,1792]{1,0:T(8,128)(2,1)S(1)}, bf16[64,1792]{1,0:T(8,128)(2,1)S(1)}, u32[]{:S(2)}, u32[]{:S(2)}) collective-permute-start(bf16[64,1792]{1,0:T(8,128)(2,1)S(1)} %get-tuple-element.16.refs_8_), channel_id=1, source_target_pairs={{0,4},{1,5},{2,6},{3,7},{4,0},{5,1},{6,2},{7,3},{8,12},{9,13},{10,... | collective-permute-start | bytes 688136 | tf_op jit(solution)/shard_map/ppermute | solution.py:132
  15.1 0.5 collective-permute-start.1
  15.6 0.0 collective-permute-done.7.refs_8_
  15.6 1.5 %collective-permute-start.2 = (bf16[128,1408]{1,0:T(8,128)(2,1)S(1)}, bf16[128,1408]{1,0:T(8,128)(2,1)S(1)}, u32[]{:S(2)}, u32[]{:S(2)}) collective-permute-start(bf16[128,1408]{1,0:T(8,128)(2,1)S(1)} %get-tuple-element.14), channel_id=1, source_target_pairs={{0,18},{1,19},{2,16},{3,17},{4,22},{5,23},{6,20},{7,21},{8,26},{9,... | collective-permute-start | bytes 1081352 | tf_op jit(solution)/shard_map/ppermute | solution.py:143
  17.1 0.3 collective-permute-done.13.refs_10_
  17.4 0.7 collective-permute-start.14
  18.0 4.1 %collective-permute-done.12.refs_9_ = bf16[64,1792]{1,0:T(8,128)(2,1)S(1)} collective-permute-done((bf16[64,1792]{1,0:T(8,128)(2,1)S(1)}, bf16[64,1792]{1,0:T(8,128)(2,1)S(1)}, u32[]{:S(2)}, u32[]{:S(2)}) %collective-permute-start.12) | collective-permute-done | bytes 229408 | tf_op jit(solution)/shard_map/ppermute | solution.py:132
  22.2 1.3 %collective-permute-start.15 = (bf16[64,1792]{1,0:T(8,128)(2,1)S(1)}, bf16[64,1792]{1,0:T(8,128)(2,1)S(1)}, u32[]{:S(2)}, u32[]{:S(2)}) collective-permute-start(bf16[64,1792]{1,0:T(8,128)(2,1)S(1)} %collective-permute-done.13.refs_10_), channel_id=1, source_target_pairs={{4,0},{5,1},{6,2},{7,3},{8,12},{9,13},{10,14},{11,15},{20,16},{21,... | collective-permute-start | bytes 688136 | tf_op jit(solution)/shard_map/ppermute | solution.py:135
  23.5 0.0 collective-permute-done.14.refs_11_
  23.5 0.1 collective-permute-start.3
  23.6 0.0 collective-permute-done.refs_1_
  23.6 0.5 collective-permute-start.4
  24.1 7.8 %collective-permute-done.1.refs_2_ = bf16[128,1408]{1,0:T(8,128)(2,1)S(1)} collective-permute-done((bf16[128,1408]{1,0:T(8,128)(2,1)S(1)}, bf16[128,1408]{1,0:T(8,128)(2,1)S(1)}, u32[]{:S(2)}, u32[]{:S(2)}) %collective-permute-start.1) | collective-permute-done | bytes 360480 | tf_op jit(solution)/shard_map/ppermute | solution.py:132
  31.8 0.0 collective-permute-start.5
  31.9 0.0 collective-permute-done.2.refs_3_
  31.9 0.5 collective-permute-start.6
  32.4 0.0 collective-permute-done.15.refs_12_
  32.4 0.8 %collective-permute-start.9 = (bf16[64,1280]{1,0:T(8,128)(2,1)S(1)}, bf16[64,1280]{1,0:T(8,128)(2,1)S(1)}, u32[]{:S(2)}, u32[]{:S(2)}) collective-permute-start(bf16[64,1280]{1,0:T(8,128)(2,1)S(1)} %collective-permute-done.7.refs_8_), channel_id=1, source_target_pairs={{0,8},{1,9},{2,10},{3,11},{4,12},{5,13},{6,14},{7,15},{8,0},{9,1},... | collective-permute-start | bytes 491528 | tf_op jit(solution)/shard_map/ppermute | solution.py:132
  33.2 9.7 %collective-permute-done.9.refs_10_ = bf16[64,1280]{1,0:T(8,128)(2,1)S(1)} collective-permute-done((bf16[64,1280]{1,0:T(8,128)(2,1)S(1)}, bf16[64,1280]{1,0:T(8,128)(2,1)S(1)}, u32[]{:S(2)}, u32[]{:S(2)}) %collective-permute-start.9) | collective-permute-done | bytes 163872 | tf_op jit(solution)/shard_map/ppermute | solution.py:132
  42.9 0.7 collective-permute-start.10
  43.5 0.0 collective-permute-done.3.refs_4_
  43.6 1.4 %collective-permute-start.8 = (bf16[64,1280]{1,0:T(8,128)(2,1)S(1)}, bf16[64,1280]{1,0:T(8,128)(2,1)S(1)}, u32[]{:S(2)}, u32[]{:S(2)}) collective-permute-start(bf16[64,1280]{1,0:T(8,128)(2,1)S(1)} %collective-permute-done.7.refs_8_), channel_id=1, source_target_pairs={{0,4},{1,5},{2,6},{3,7},{4,0},{5,1},{6,2},{7,3},{8,12},{9,13},{10,... | collective-permute-start | bytes 491528 | tf_op jit(solution)/shard_map/ppermute | solution.py:132
  45.0 0.0 collective-permute-done.4.refs_5_
  45.0 1.3 %collective-permute-start.11 = (bf16[64,1280]{1,0:T(8,128)(2,1)S(1)}, bf16[64,1280]{1,0:T(8,128)(2,1)S(1)}, u32[]{:S(2)}, u32[]{:S(2)}) collective-permute-start(bf16[64,1280]{1,0:T(8,128)(2,1)S(1)} %collective-permute-done.9.refs_10_), channel_id=1, source_target_pairs={{4,0},{5,1},{6,2},{7,3},{8,12},{9,13},{10,14},{11,15},{20,16},{21,... | collective-permute-start | bytes 491528 | tf_op jit(solution)/shard_map/ppermute | solution.py:135
  46.3 0.0 collective-permute-done.5.refs_6_
  46.3 0.6 collective-permute-start.20
  46.9 0.0 collective-permute-done.6.refs_7_
  46.9 0.6 collective-permute-start.21
  47.5 1.4 %shard_map.75.refs_13_ = f32[8,128,128]{2,1,0:T(8,128)S(1)} custom-call(s32[4]{0:T(128)S(1)} %pad_add_fusion.place, bf16[128,1408]{1,0:T(8,128)(2,1)S(1)} %get-tuple-element.11.refs_0_.mine, bf16[128,1408]{1,0:T(8,128)(2,1)S(1)} %collective-permute-done.refs_1_, bf16[128,1408]{1,0:T(8,128)(2,1)S(1)} %collective-permute-done.1.refs_2_, ...), custom_call_target="tpu_custom_call" | custom-call | flops 671088640 | bytes 4554768 | tf_op jit(solution)/shard_map/pallas_call | solution.py:18
  49.0 0.0 collective-permute-done.10.refs_11_
  49.0 2.4 %collective-permute-start.22 = (bf16[256,512]{1,0:T(8,128)(2,1)S(1)}, bf16[256,512]{1,0:T(8,128)(2,1)S(1)}, u32[]{:S(2)}, u32[]{:S(2)}) collective-permute-start(bf16[256,512]{1,0:T(8,128)(2,1)S(1)} %pad_maximum_fusion.refs_0_), channel_id=1, source_target_pairs={{0,18},{1,19},{2,16},{3,17},{4,22},{5,23},{6,20},{7,21},{8,26},{9,... | collective-permute-start | bytes 786440 | tf_op jit(solution)/shard_map/ppermute | solution.py:143
  51.4 0.0 collective-permute-done.8.refs_9_
  51.4 1.9 %collective-permute-done.11.refs_12_ = bf16[64,1280]{1,0:T(8,128)(2,1)S(1)} collective-permute-done((bf16[64,1280]{1,0:T(8,128)(2,1)S(1)}, bf16[64,1280]{1,0:T(8,128)(2,1)S(1)}, u32[]{:S(2)}, u32[]{:S(2)}) %collective-permute-start.11) | collective-permute-done | bytes 163872 | tf_op jit(solution)/shard_map/ppermute | solution.py:135
  53.3 1.4 %shard_map.76 = f32[8,128,128]{2,1,0:T(8,128)S(1)} custom-call(s32[4]{0:T(128)S(1)} %pad_add_fusion.place, bf16[128,1408]{1,0:T(8,128)(2,1)S(1)} %get-tuple-element.11.refs_0_.mine, bf16[128,1408]{1,0:T(8,128)(2,1)S(1)} %collective-permute-done.refs_1_, bf16[128,1408]{1,0:T(8,128)(2,1)S(1)} %collective-permute-done.1.refs_2_, ...), custom_call_target="tpu_custom_call" | custom-call | flops 671088640 | bytes 4751376 | tf_op jit(solution)/shard_map/pallas_call | solution.py:18
  54.7 0.6 collective-permute-start.16
  55.3 0.2 collective-permute-start.17
  55.5 0.1 collective-permute-done.20.refs_1_
  55.6 2.7 %collective-permute-start.18 = (f32[2,128,128]{2,1,0:T(8,128)S(1)}, f32[2,128,128]{2,1,0:T(8,128)S(1)}, u32[]{:S(2)}, u32[]{:S(2)}) collective-permute-start(f32[2,128,128]{2,1,0:T(8,128)S(1)} %get-tuple-element.19), channel_id=1, source_target_pairs={{0,18},{1,19},{2,16},{3,17},{4,22},{5,23},{6,20},{7,21},{8,26},{9,... | collective-permute-start | bytes 393224 | tf_op jit(solution)/shard_map/ppermute | solution.py:143
  58.3 0.6 collective-permute-done.21.refs_2_
  58.9 0.0 collective-permute-start.23
  58.9 2.4 %collective-permute-done.22.refs_3_ = bf16[256,512]{1,0:T(8,128)(2,1)S(1)} collective-permute-done((bf16[256,512]{1,0:T(8,128)(2,1)S(1)}, bf16[256,512]{1,0:T(8,128)(2,1)S(1)}, u32[]{:S(2)}, u32[]{:S(2)}) %collective-permute-start.22) | collective-permute-done | bytes 262176 | tf_op jit(solution)/shard_map/ppermute | solution.py:143
  61.2 0.0 collective-permute-start.24
  61.3 2.7 %collective-permute-done.16 = f32[2,128,128]{2,1,0:T(8,128)S(1)} collective-permute-done((f32[2,128,128]{2,1,0:T(8,128)S(1)}, f32[2,128,128]{2,1,0:T(8,128)S(1)}, u32[]{:S(2)}, u32[]{:S(2)}) %collective-permute-start.16) | collective-permute-done | bytes 131104 | tf_op jit(solution)/shard_map/ppermute | solution.py:143
  63.9 0.0 collective-permute-start.25
  63.9 1.6 %collective-permute-done.17 = f32[2,128,128]{2,1,0:T(8,128)S(1)} collective-permute-done((f32[2,128,128]{2,1,0:T(8,128)S(1)}, f32[2,128,128]{2,1,0:T(8,128)S(1)}, u32[]{:S(2)}, u32[]{:S(2)}) %collective-permute-start.17) | collective-permute-done | bytes 131104 | tf_op jit(solution)/shard_map/ppermute | solution.py:132
  65.5 0.0 collective-permute-start.26
  65.5 0.0 collective-permute-done.18
  65.6 0.6 collective-permute-start.19
  66.2 5.6 %fusion.3.base = f32[128,1024]{1,0:T(8,128)S(1)} fusion(bf16[128,5120]{1,0:T(8,128)(2,1)S(1)} %copy-done.1, bf16[5120,1024]{1,0:T(8,128)(2,1)} %param.8), kind=kOutput, calls=%fused_computation.16 | convolution fusion | flops 1342177280 | bytes 12320768 | tf_op jit(solution)/shard_map/dot_general | solution.py:197
  71.8 0.0 collective-permute-done.19.swapped
  71.8 0.0 collective-permute-done.26.refs_7_
  71.8 1.8 %shard_map.77 = bf16[128,1024]{1,0:T(8,128)(2,1)} custom-call(s32[4]{0:T(128)S(1)} %pad_add_fusion.place, f32[128,1024]{1,0:T(8,128)S(1)} %fusion.3.base, bf16[128,1408]{1,0:T(8,128)(2,1)S(1)} %get-tuple-element.11.refs_0_.mine, f32[128,128]{1,0:T(8,128)S(1)} %get-tuple-element.21.total, f32[128,128]{1,0:T(8,128)S(1)} %collective-permute-done.19.swapped, ...), custom_call_target="tpu_custom_call" | custom-call | flops 268435456 | bytes 3375120 | tf_op jit(solution)/shard_map/pallas_call | solution.py:18
  (16 shorter events, 0.1 us)
Async XLA Ops:
  0.1 1.1 %copy-start.2 = (bf16[1,64,5120]{2,1,0:T(8,128)(2,1)S(1)}, bf16[1,64,5120]{2,1,0:T(8,128)(2,1)}, u32[]{:S(2)}) copy-start(bf16[1,64,5120]{2,1,0:T(8,128)(2,1)} %down.1) | copy-start | bytes 1966084
  1.2 0.9 %copy-start.3 = (bf16[1,64,1024]{2,1,0:T(8,128)(2,1)S(1)}, bf16[1,64,1024]{2,1,0:T(8,128)(2,1)}, u32[]{:S(2)}) copy-start(bf16[1,64,1024]{2,1,0:T(8,128)(2,1)} %up.1) | copy-start | bytes 393220
  2.7 14.7 %collective-permute-start.13 = (bf16[64,1792]{1,0:T(8,128)(2,1)S(1)}, bf16[64,1792]{1,0:T(8,128)(2,1)S(1)}, u32[]{:S(2)}, u32[]{:S(2)}) collective-permute-start(bf16[64,1792]{1,0:T(8,128)(2,1)S(1)} %get-tuple-element.16.refs_8_), channel_id=1, source_target_pairs={{0,8},{1,9},{2,10},{3,11},{4,12},{5,13},{6,14},{7,15},{8,0},{9,1},... | collective-permute-start | bytes 688136 | tf_op jit(solution)/shard_map/ppermute | solution.py:132
  6.8 8.8 %collective-permute-start.7 = (bf16[64,1280]{1,0:T(8,128)(2,1)S(1)}, bf16[64,1280]{1,0:T(8,128)(2,1)S(1)}, u32[]{:S(2)}, u32[]{:S(2)}) collective-permute-start(bf16[64,1280]{1,0:T(8,128)(2,1)S(1)} %get-tuple-element.15), channel_id=1, source_target_pairs={{0,2},{1,3},{2,0},{3,1},{4,6},{5,7},{6,4},{7,5},{8,10},{9,11},{10,... | collective-permute-start | bytes 491528 | tf_op jit(solution)/shard_map/ppermute | solution.py:132
  10.0 1.3 %copy-start = (bf16[128,5120]{1,0:T(8,128)(2,1)S(1)}, bf16[128,5120]{1,0:T(8,128)(2,1)}, u32[]{:S(2)}) copy-start(bf16[128,5120]{1,0:T(8,128)(2,1)} %hidden.1) | copy-start | bytes 3932164
  11.3 54.9 %copy-start.1 = (bf16[128,5120]{1,0:T(8,128)(2,1)S(1)}, bf16[128,5120]{1,0:T(8,128)(2,1)}, u32[]{:S(2)}) copy-start(bf16[128,5120]{1,0:T(8,128)(2,1)} %hidden.1) | copy-start | bytes 3932164
  12.0 11.6 %collective-permute-start = (bf16[128,1408]{1,0:T(8,128)(2,1)S(1)}, bf16[128,1408]{1,0:T(8,128)(2,1)S(1)}, u32[]{:S(2)}, u32[]{:S(2)}) collective-permute-start(bf16[128,1408]{1,0:T(8,128)(2,1)S(1)} %get-tuple-element.12), channel_id=1, source_target_pairs={{0,16},{1,17},{2,18},{3,19},{4,20},{5,21},{6,22},{7,23},{8,24},{9,... | collective-permute-start | bytes 1081352 | tf_op jit(solution)/shard_map/ppermute | solution.py:143
  13.5 8.7 %collective-permute-start.12 = (bf16[64,1792]{1,0:T(8,128)(2,1)S(1)}, bf16[64,1792]{1,0:T(8,128)(2,1)S(1)}, u32[]{:S(2)}, u32[]{:S(2)}) collective-permute-start(bf16[64,1792]{1,0:T(8,128)(2,1)S(1)} %get-tuple-element.16.refs_8_), channel_id=1, source_target_pairs={{0,4},{1,5},{2,6},{3,7},{4,0},{5,1},{6,2},{7,3},{8,12},{9,13},{10,... | collective-permute-start | bytes 688136 | tf_op jit(solution)/shard_map/ppermute | solution.py:132
  15.1 16.8 %collective-permute-start.1 = (bf16[128,1408]{1,0:T(8,128)(2,1)S(1)}, bf16[128,1408]{1,0:T(8,128)(2,1)S(1)}, u32[]{:S(2)}, u32[]{:S(2)}) collective-permute-start(bf16[128,1408]{1,0:T(8,128)(2,1)S(1)} %get-tuple-element.13), channel_id=1, source_target_pairs={{0,2},{1,3},{2,0},{3,1},{4,6},{5,7},{6,4},{7,5},{8,10},{9,11},{10,... | collective-permute-start | bytes 1081352 | tf_op jit(solution)/shard_map/ppermute | solution.py:132
  15.6 16.3 %collective-permute-start.2 = (bf16[128,1408]{1,0:T(8,128)(2,1)S(1)}, bf16[128,1408]{1,0:T(8,128)(2,1)S(1)}, u32[]{:S(2)}, u32[]{:S(2)}) collective-permute-start(bf16[128,1408]{1,0:T(8,128)(2,1)S(1)} %get-tuple-element.14), channel_id=1, source_target_pairs={{0,18},{1,19},{2,16},{3,17},{4,22},{5,23},{6,20},{7,21},{8,26},{9,... | collective-permute-start | bytes 1081352 | tf_op jit(solution)/shard_map/ppermute | solution.py:143
  17.4 6.1 %collective-permute-start.14 = (bf16[64,1792]{1,0:T(8,128)(2,1)S(1)}, bf16[64,1792]{1,0:T(8,128)(2,1)S(1)}, u32[]{:S(2)}, u32[]{:S(2)}) collective-permute-start(bf16[64,1792]{1,0:T(8,128)(2,1)S(1)} %get-tuple-element.16.refs_8_), channel_id=1, source_target_pairs={{4,8},{5,9},{6,10},{7,11},{8,4},{9,5},{10,6},{11,7},{20,24},{21,25... | collective-permute-start | bytes 688136 | tf_op jit(solution)/shard_map/ppermute | solution.py:135
  22.2 10.2 %collective-permute-start.15 = (bf16[64,1792]{1,0:T(8,128)(2,1)S(1)}, bf16[64,1792]{1,0:T(8,128)(2,1)S(1)}, u32[]{:S(2)}, u32[]{:S(2)}) collective-permute-start(bf16[64,1792]{1,0:T(8,128)(2,1)S(1)} %collective-permute-done.13.refs_10_), channel_id=1, source_target_pairs={{4,0},{5,1},{6,2},{7,3},{8,12},{9,13},{10,14},{11,15},{20,16},{21,... | collective-permute-start | bytes 688136 | tf_op jit(solution)/shard_map/ppermute | solution.py:135
  23.5 20.1 %collective-permute-start.3 = (bf16[128,1408]{1,0:T(8,128)(2,1)S(1)}, bf16[128,1408]{1,0:T(8,128)(2,1)S(1)}, u32[]{:S(2)}, u32[]{:S(2)}) collective-permute-start(bf16[128,1408]{1,0:T(8,128)(2,1)S(1)} %get-tuple-element.11.refs_0_.mine), channel_id=1, source_target_pairs={{0,1},{1,0},{2,3},{3,2},{4,5},{5,4},{6,7},{7,6},{8,9},{9,8},{10,11... | collective-permute-start | bytes 1081352 | tf_op jit(solution)/shard_map/ppermute | solution.py:132
  23.6 21.4 %collective-permute-start.4 = (bf16[128,1408]{1,0:T(8,128)(2,1)S(1)}, bf16[128,1408]{1,0:T(8,128)(2,1)S(1)}, u32[]{:S(2)}, u32[]{:S(2)}) collective-permute-start(bf16[128,1408]{1,0:T(8,128)(2,1)S(1)} %collective-permute-done.refs_1_), channel_id=1, source_target_pairs={{0,1},{1,0},{2,3},{3,2},{4,5},{5,4},{6,7},{7,6},{8,9},{9,8},{10,11... | collective-permute-start | bytes 1081352 | tf_op jit(solution)/shard_map/ppermute | solution.py:132
  31.8 14.4 %collective-permute-start.5 = (bf16[128,1408]{1,0:T(8,128)(2,1)S(1)}, bf16[128,1408]{1,0:T(8,128)(2,1)S(1)}, u32[]{:S(2)}, u32[]{:S(2)}) collective-permute-start(bf16[128,1408]{1,0:T(8,128)(2,1)S(1)} %collective-permute-done.1.refs_2_), channel_id=1, source_target_pairs={{0,1},{1,0},{2,3},{3,2},{4,5},{5,4},{6,7},{7,6},{8,9},{9,8},{10,11... | collective-permute-start | bytes 1081352 | tf_op jit(solution)/shard_map/ppermute | solution.py:132
  31.9 15.0 %collective-permute-start.6 = (bf16[128,1408]{1,0:T(8,128)(2,1)S(1)}, bf16[128,1408]{1,0:T(8,128)(2,1)S(1)}, u32[]{:S(2)}, u32[]{:S(2)}) collective-permute-start(bf16[128,1408]{1,0:T(8,128)(2,1)S(1)} %collective-permute-done.2.refs_3_), channel_id=1, source_target_pairs={{0,1},{1,0},{2,3},{3,2},{4,5},{5,4},{6,7},{7,6},{8,9},{9,8},{10,11... | collective-permute-start | bytes 1081352 | tf_op jit(solution)/shard_map/ppermute | solution.py:132
  32.4 10.5 %collective-permute-start.9 = (bf16[64,1280]{1,0:T(8,128)(2,1)S(1)}, bf16[64,1280]{1,0:T(8,128)(2,1)S(1)}, u32[]{:S(2)}, u32[]{:S(2)}) collective-permute-start(bf16[64,1280]{1,0:T(8,128)(2,1)S(1)} %collective-permute-done.7.refs_8_), channel_id=1, source_target_pairs={{0,8},{1,9},{2,10},{3,11},{4,12},{5,13},{6,14},{7,15},{8,0},{9,1},... | collective-permute-start | bytes 491528 | tf_op jit(solution)/shard_map/ppermute | solution.py:132
  42.9 6.1 %collective-permute-start.10 = (bf16[64,1280]{1,0:T(8,128)(2,1)S(1)}, bf16[64,1280]{1,0:T(8,128)(2,1)S(1)}, u32[]{:S(2)}, u32[]{:S(2)}) collective-permute-start(bf16[64,1280]{1,0:T(8,128)(2,1)S(1)} %collective-permute-done.7.refs_8_), channel_id=1, source_target_pairs={{4,8},{5,9},{6,10},{7,11},{8,4},{9,5},{10,6},{11,7},{20,24},{21,25... | collective-permute-start | bytes 491528 | tf_op jit(solution)/shard_map/ppermute | solution.py:135
  43.6 7.8 %collective-permute-start.8 = (bf16[64,1280]{1,0:T(8,128)(2,1)S(1)}, bf16[64,1280]{1,0:T(8,128)(2,1)S(1)}, u32[]{:S(2)}, u32[]{:S(2)}) collective-permute-start(bf16[64,1280]{1,0:T(8,128)(2,1)S(1)} %collective-permute-done.7.refs_8_), channel_id=1, source_target_pairs={{0,4},{1,5},{2,6},{3,7},{4,0},{5,1},{6,2},{7,3},{8,12},{9,13},{10,... | collective-permute-start | bytes 491528 | tf_op jit(solution)/shard_map/ppermute | solution.py:132
  45.0 8.3 %collective-permute-start.11 = (bf16[64,1280]{1,0:T(8,128)(2,1)S(1)}, bf16[64,1280]{1,0:T(8,128)(2,1)S(1)}, u32[]{:S(2)}, u32[]{:S(2)}) collective-permute-start(bf16[64,1280]{1,0:T(8,128)(2,1)S(1)} %collective-permute-done.9.refs_10_), channel_id=1, source_target_pairs={{4,0},{5,1},{6,2},{7,3},{8,12},{9,13},{10,14},{11,15},{20,16},{21,... | collective-permute-start | bytes 491528 | tf_op jit(solution)/shard_map/ppermute | solution.py:135
  46.3 9.3 %collective-permute-start.20 = (bf16[256,512]{1,0:T(8,128)(2,1)S(1)}, bf16[256,512]{1,0:T(8,128)(2,1)S(1)}, u32[]{:S(2)}, u32[]{:S(2)}) collective-permute-start(bf16[256,512]{1,0:T(8,128)(2,1)S(1)} %pad_maximum_fusion.refs_0_), channel_id=1, source_target_pairs={{0,16},{1,17},{2,18},{3,19},{4,20},{5,21},{6,22},{7,23},{8,24},{9,... | collective-permute-start | bytes 786440 | tf_op jit(solution)/shard_map/ppermute | solution.py:143
  46.9 12.0 %collective-permute-start.21 = (bf16[256,512]{1,0:T(8,128)(2,1)S(1)}, bf16[256,512]{1,0:T(8,128)(2,1)S(1)}, u32[]{:S(2)}, u32[]{:S(2)}) collective-permute-start(bf16[256,512]{1,0:T(8,128)(2,1)S(1)} %pad_maximum_fusion.refs_0_), channel_id=1, source_target_pairs={{0,2},{1,3},{2,0},{3,1},{4,6},{5,7},{6,4},{7,5},{8,10},{9,11},{10,... | collective-permute-start | bytes 786440 | tf_op jit(solution)/shard_map/ppermute | solution.py:132
  49.0 12.3 %collective-permute-start.22 = (bf16[256,512]{1,0:T(8,128)(2,1)S(1)}, bf16[256,512]{1,0:T(8,128)(2,1)S(1)}, u32[]{:S(2)}, u32[]{:S(2)}) collective-permute-start(bf16[256,512]{1,0:T(8,128)(2,1)S(1)} %pad_maximum_fusion.refs_0_), channel_id=1, source_target_pairs={{0,18},{1,19},{2,16},{3,17},{4,22},{5,23},{6,20},{7,21},{8,26},{9,... | collective-permute-start | bytes 786440 | tf_op jit(solution)/shard_map/ppermute | solution.py:143
  54.7 9.2 %collective-permute-start.16 = (f32[2,128,128]{2,1,0:T(8,128)S(1)}, f32[2,128,128]{2,1,0:T(8,128)S(1)}, u32[]{:S(2)}, u32[]{:S(2)}) collective-permute-start(f32[2,128,128]{2,1,0:T(8,128)S(1)} %get-tuple-element.17), channel_id=1, source_target_pairs={{0,16},{1,17},{2,18},{3,19},{4,20},{5,21},{6,22},{7,23},{8,24},{9,... | collective-permute-start | bytes 393224 | tf_op jit(solution)/shard_map/ppermute | solution.py:143
  55.3 10.2 %collective-permute-start.17 = (f32[2,128,128]{2,1,0:T(8,128)S(1)}, f32[2,128,128]{2,1,0:T(8,128)S(1)}, u32[]{:S(2)}, u32[]{:S(2)}) collective-permute-start(f32[2,128,128]{2,1,0:T(8,128)S(1)} %get-tuple-element.18), channel_id=1, source_target_pairs={{0,2},{1,3},{2,0},{3,1},{4,6},{5,7},{6,4},{7,5},{8,10},{9,11},{10,... | collective-permute-start | bytes 393224 | tf_op jit(solution)/shard_map/ppermute | solution.py:132
  55.6 9.9 %collective-permute-start.18 = (f32[2,128,128]{2,1,0:T(8,128)S(1)}, f32[2,128,128]{2,1,0:T(8,128)S(1)}, u32[]{:S(2)}, u32[]{:S(2)}) collective-permute-start(f32[2,128,128]{2,1,0:T(8,128)S(1)} %get-tuple-element.19), channel_id=1, source_target_pairs={{0,18},{1,19},{2,16},{3,17},{4,22},{5,23},{6,20},{7,21},{8,26},{9,... | collective-permute-start | bytes 393224 | tf_op jit(solution)/shard_map/ppermute | solution.py:143
  58.9 12.9 %collective-permute-start.23 = (bf16[256,512]{1,0:T(8,128)(2,1)S(1)}, bf16[256,512]{1,0:T(8,128)(2,1)S(1)}, u32[]{:S(2)}, u32[]{:S(2)}) collective-permute-start(bf16[256,512]{1,0:T(8,128)(2,1)S(1)} %pad_maximum_fusion.refs_0_), channel_id=1, source_target_pairs={{0,1},{1,0},{2,3},{3,2},{4,5},{5,4},{6,7},{7,6},{8,9},{9,8},{10,11... | collective-permute-start | bytes 786440 | tf_op jit(solution)/shard_map/ppermute | solution.py:132
  61.2 10.6 %collective-permute-start.24 = (bf16[256,512]{1,0:T(8,128)(2,1)S(1)}, bf16[256,512]{1,0:T(8,128)(2,1)S(1)}, u32[]{:S(2)}, u32[]{:S(2)}) collective-permute-start(bf16[256,512]{1,0:T(8,128)(2,1)S(1)} %collective-permute-done.20.refs_1_), channel_id=1, source_target_pairs={{0,1},{1,0},{2,3},{3,2},{4,5},{5,4},{6,7},{7,6},{8,9},{9,8},{10,11... | collective-permute-start | bytes 786440 | tf_op jit(solution)/shard_map/ppermute | solution.py:132
  63.9 7.9 %collective-permute-start.25 = (bf16[256,512]{1,0:T(8,128)(2,1)S(1)}, bf16[256,512]{1,0:T(8,128)(2,1)S(1)}, u32[]{:S(2)}, u32[]{:S(2)}) collective-permute-start(bf16[256,512]{1,0:T(8,128)(2,1)S(1)} %collective-permute-done.21.refs_2_), channel_id=1, source_target_pairs={{0,1},{1,0},{2,3},{3,2},{4,5},{5,4},{6,7},{7,6},{8,9},{9,8},{10,11... | collective-permute-start | bytes 786440 | tf_op jit(solution)/shard_map/ppermute | solution.py:132
  65.5 6.3 %collective-permute-start.26 = (bf16[256,512]{1,0:T(8,128)(2,1)S(1)}, bf16[256,512]{1,0:T(8,128)(2,1)S(1)}, u32[]{:S(2)}, u32[]{:S(2)}) collective-permute-start(bf16[256,512]{1,0:T(8,128)(2,1)S(1)} %collective-permute-done.22.refs_3_), channel_id=1, source_target_pairs={{0,1},{1,0},{2,3},{3,2},{4,5},{5,4},{6,7},{7,6},{8,9},{9,8},{10,11... | collective-permute-start | bytes 786440 | tf_op jit(solution)/shard_map/ppermute | solution.py:132
  65.6 6.2 %collective-permute-start.19 = (f32[128,128]{1,0:T(8,128)S(1)}, f32[128,128]{1,0:T(8,128)S(1)}, u32[]{:S(2)}, u32[]{:S(2)}) collective-permute-start(f32[128,128]{1,0:T(8,128)S(1)} %get-tuple-element.20), channel_id=1, source_target_pairs={{0,1},{1,0},{2,3},{3,2},{4,5},{5,4},{6,7},{7,6},{8,9},{9,8},{10,11... | collective-permute-start | bytes 196616 | tf_op jit(solution)/shard_map/ppermute | solution.py:132

commit v3 on v2

v3 whole, which is shorter than its diff:
```python
import functools

import jax
import jax.numpy as jnp
from jax import lax
from jax.experimental import pallas as pl
from jax.experimental.pallas import tpu as pltpu
from jax.sharding import PartitionSpec as P

TAG = 128
ORDER = {
    "Y": ("P", "A1"),
    "A3": ("A1", "P"),
    "D": ("X", "A2"),
    "B1": ("A3", "Y"),
    "B3": ("A3",),
    "base": ("P",),
    "A4": ("base",),
    "B4": ("A4",),
    "C1": ("A4", "B1", "B2"),
    "C2": ("A4", "B1", "B2"),
}
VMEM = pl.BlockSpec(memory_space=pltpu.VMEM)
SMEM = pl.BlockSpec(memory_space=pltpu.SMEM)
HBM = pl.BlockSpec(memory_space=pltpu.HBM)


def call(kernel, out, operands, scalars=0, whole=0, flops=0, scratch=()):
    operands = list(operands)
    if whole:
        operands[-whole:] = [
            pltpu.with_memory_space_constraint(o, pltpu.HBM) for o in operands[-whole:]
        ]
    moved = sum(o.size * o.dtype.itemsize for o in operands)
    return pl.pallas_call(
        kernel,
        out_shape=out,
        in_specs=[SMEM] * scalars + [VMEM] * (len(operands) - scalars - whole) + [HBM] * whole,
        out_specs=jax.tree.map(lambda _: VMEM, out),
        scratch_shapes=scratch,
        cost_estimate=pl.CostEstimate(flops=flops, bytes_accessed=moved, transcendentals=0),
        compiler_params=pltpu.CompilerParams(vmem_limit_bytes=(16 if whole else 48) << 20),
    )(*operands)


def slices(place, down, up, hbm_variants, hbm_slots, hbm_choice, hidden, *refs):
    swapped, own, *outs, variants, slot_of, choice, sems = refs
    quarter, qhalf = swapped.shape[1], own.shape[1] - swapped.shape[1]
    rows = outs[0].shape[0]
    x, column = place[0], place[2]

    def columns(part, width):
        return pl.ds(pl.multiple_of(part * width, 128), width)

    parts = (x * 2 + column, (1 - x) * 2 + column, x * 2 + 1 - column, (1 - x) * 2 + 1 - column)
    pairs = [
        (hbm_variants, variants),
        (hbm_slots, slot_of),
        (hbm_choice, choice),
        (down.at[0, :, columns(parts[2], quarter)], swapped),
        (down.at[0, :, columns(parts[0], quarter)], own.at[:, :quarter]),
        (up.at[0, :, columns(x, qhalf)], own.at[:, quarter:]),
    ]
    pairs += [
        (hidden.at[:, columns(part, quarter)], out.at[:, :quarter])
        for part, out in zip(parts, outs)
    ]
    copies = [pltpu.make_async_copy(a, b, sems.at[i]) for i, (a, b) in enumerate(pairs)]
    for copy in copies:
        copy.start()
    for copy in copies[:3]:
        copy.wait()
    slot = jnp.zeros((1, rows), jnp.int32)
    for k in range(variants.shape[1]):
        slot = jnp.where(choice[...] == k, slot_of[variants[0, k]], slot)
    diagonal = lax.broadcasted_iota(jnp.int32, (rows, rows), 0) == lax.broadcasted_iota(
        jnp.int32, (rows, rows), 1
    )
    column = jnp.sum(jnp.where(diagonal, slot.astype(jnp.float32), 0.0), axis=1, keepdims=True)
    tag = jnp.broadcast_to(column, (rows, TAG)).astype(jnp.bfloat16)
    for out in outs:
        out[:, quarter:] = tag
    for copy in copies[3:]:
        copy.wait()


def ids_of(plane, column, core, first, count, rank):
    lane = lax.broadcasted_iota(jnp.int32, (1, count * rank), 1)
    return ((plane ^ (first + lane // rank)) * 4) + column * 2 + core


def sum_z(flipped, units, merged, place, *refs):
    plane, column, core = place[1], place[2], place[3]
    column = 1 - column if flipped else column
    blocks, refs = refs[:6], refs[6:]
    held, refs = refs[: units + merged], refs[units + merged :]
    *refs, hid = refs
    before, outs = (refs[:1], refs[1:]) if flipped else ((), refs)
    rows, quarter = blocks[0].shape[0], blocks[0].shape[1] - TAG
    rank = held[0].shape[0]
    tags = []
    for block in blocks:
        for first in range(0, block.shape[0], rows):
            span = slice(first, first + rows)
            hid[len(tags) * rows : (len(tags) + 1) * rows, :] = block[span, :quarter]
            tag = block[span, quarter : quarter + 1]
            tags.append(tag.astype(jnp.float32).astype(jnp.int32))
    some = min(units, 4)
    sums = [before[0][i] if before else None for i in range(8)]
    for first in range(0, units, some):
        parts = [h[:, :quarter] for h in held[first : first + some]]
        if merged:
            parts[-1] = parts[-1] + held[units][:, :quarter]
        z = lax.dot_general(
            hid[...],
            jnp.concatenate(parts, axis=0),
            (((1,), (1,)), ((), ())),
            preferred_element_type=jnp.float32,
        )
        ids = ids_of(plane, column, core, first, some, rank)
        for i in range(8):
            kept = jnp.where(tags[i] == ids, z[i * rows : (i + 1) * rows, :], 0.0)
            kept = sum(kept[:, j : j + 128] for j in range(0, some * rank, 128))
            sums[i] = kept if sums[i] is None else sums[i] + kept
    for i in range(8):
        if flipped:
            outs[i % 4][i // 4] = sums[i]
        else:
            outs[0][i] = sums[i]


def add_up(planes, place, base, mine, theirs, z_here, z_x, z_y, z_d, *refs):
    *held, out, away = refs
    x, plane, column, core = place[0], place[1], place[2], place[3]
    rows, quarter = mine.shape[0], mine.shape[1] - TAG
    rank = z_here.shape[2] // 2
    qhalf = held[0].shape[1]
    tag = jnp.concatenate(
        [mine[:, quarter : quarter + 1], theirs[:rows, quarter : quarter + 1]], axis=0
    )
    tag = tag.astype(jnp.float32).astype(jnp.int32)
    both = [z_here[i] + z_x[i] + z_y[i] + z_d[i] for i in range(2)]
    z = jnp.concatenate([b[:, :rank] + b[:, rank:] for b in both], axis=0)
    z = z.astype(jnp.bfloat16).astype(jnp.float32)
    some = min(planes, 4)
    spread = jnp.concatenate([z] * some, axis=1)
    near = jnp.zeros((2 * rows, qhalf), jnp.float32)
    far = jnp.zeros((2 * rows, qhalf), jnp.float32)
    for first in range(0, planes, some):
        span = slice(first * rank, (first + some) * rank)
        for y in range(2):
            ids = ids_of(plane, 1 - column if y else column, core, first, some, rank)
            picked = jnp.where(tag == ids, spread, 0.0).astype(jnp.bfloat16)
            near += jnp.dot(picked, held[y * 2][span, :], preferred_element_type=jnp.float32)
            far += jnp.dot(picked, held[y * 2 + 1][span, :], preferred_element_type=jnp.float32)
    for half, value in ((x, near), (1 - x, far)):
        columns = pl.ds(pl.multiple_of(half * qhalf, 128), qhalf)
        out[:, columns] = base[:, columns] + value[:rows]
        away[:, columns] = value[rows:]


def add(here, came, out):
    out[...] = (here[...] + came[...]).astype(out.dtype)


def body(hidden, base_weight, factor_down, factor_up, group_variants, row_choice, slot_of):
    owners = lax.axis_size("owner")
    assert lax.axis_size("replica") == 2 and owners % 4 == 0 and owners <= 256
    planes = owners // 4
    rows, width = hidden.shape
    rank = factor_down.shape[1]
    qwidth = factor_up.shape[2]
    quarter, qhalf = width // 4, qwidth // 2
    here = lax.axis_index("owner")
    place = jnp.stack([lax.axis_index("replica"), here // 4, (here // 2) % 2, here % 2])

    def by_owner(value, flip):
        return lax.ppermute(value, "owner", [(i, i ^ flip) for i in range(owners)])

    def between(value, pairs):
        return lax.ppermute(
            value, "owner", [(a * 4 + i, b * 4 + i) for a, b in pairs for i in range(4)]
        )

    def across(value, flip):
        pairs = [
            (r * owners + i, (1 - r) * owners + (i ^ flip)) for r in range(2) for i in range(owners)
        ]
        return lax.ppermute(value, ("replica", "owner"), pairs)

    def to_x(value):
        return across(value, 0)

    def to_y(value):
        return by_owner(value, 2)

    def to_d(value):
        return across(value, 2)

    def to_core(value):
        return by_owner(value, 1)

    def along(unit):
        return [unit] + [by_owner(unit, 4 * s) for s in range(1, planes)]

    def middle(unit):
        return between(unit, [(1, 2), (2, 1)])

    def ends(unit):
        return between(unit, [(1, 0), (2, 3)])

    merged = 1 if planes == 4 else 0
    bf16, f32 = jnp.bfloat16, jnp.float32

    swapped, own, mine, for_x, for_y, for_d = call(
        slices,
        (pltpu.VMEM((rank, quarter), bf16), pltpu.VMEM((rank, quarter + qhalf), bf16))
        + (pltpu.VMEM((rows, quarter + TAG), bf16),) * 4,
        (
            place,
            factor_down,
            factor_up,
            group_variants,
            slot_of,
            row_choice[None, :],
            hidden,
        ),
        scalars=1,
        whole=6,
        scratch=[
            pltpu.SMEM(group_variants.shape, jnp.int32),
            pltpu.SMEM(slot_of.shape, jnp.int32),
            pltpu.VMEM((1, rows), jnp.int32),
            pltpu.SemaphoreType.DMA((10,)),
        ],
    )
    done = {}

    def step(name):
        if name not in done:
            done[name] = None
            waits = [step(w) for w in (ORDER.get(name, ()) if planes == 4 else ())]
            done[name] = steps[name](lambda *v: lax.optimization_barrier((*v, *waits))[: len(v)])
        return done[name]

    def held_up():
        parts = [own, step("A1"), step("A2"), step("A3") + step("A4")]
        return jnp.concatenate([u[:, quarter:] for u in parts], axis=0)

    steps = {
        "P": lambda late: to_y(*late(swapped)),
        "X": lambda late: to_x(*late(for_x)),
        "Y": lambda late: to_y(*late(for_y)),
        "D": lambda late: to_d(*late(for_d)),
        "A1": lambda late: by_owner(*late(own), 4),
        "A2": lambda late: by_owner(*late(own), 8),
        "A3": lambda late: middle(*late(own)),
        "A4": lambda late: ends(*late(step("A2"))),
        "B1": lambda late: by_owner(*late(step("P")), 4),
        "B2": lambda late: by_owner(*late(step("P")), 8),
        "B3": lambda late: middle(*late(step("P"))),
        "B4": lambda late: ends(*late(step("B2"))),
        "base": lambda late: jnp.dot(*late(hidden), base_weight, preferred_element_type=f32),
        "C1": lambda late: to_core(jnp.concatenate(late(mine, step("X")), axis=0)),
        "C2": lambda late: to_core(jnp.concatenate(late(step("Y"), step("D")), axis=0)),
        "U": lambda late: late(held_up())[0],
        "UX": lambda late: to_x(*late(step("U"))),
        "UY": lambda late: to_y(*late(step("U"))),
        "UD": lambda late: to_d(*late(step("U"))),
        "K": lambda late: late(place)[0],
    }
    if merged:
        a_units = [own] + [step(f"A{i}") for i in range(1, 5)]
        b_units = [step("P")] + [step(f"B{i}") for i in range(1, 5)]
        ups = [step("U"), step("UX"), step("UY"), step("UD")]
    else:
        a_units, b_units = along(own), along(step("P"))
        ups = jnp.concatenate([u[:, quarter:] for u in a_units], axis=0)
        ups = [ups, to_x(ups), to_y(ups), to_d(ups)]
    blocks = [mine] + [step(n) for n in ("X", "Y", "D", "C1", "C2")]
    pair, base = step("C1"), step("base")
    first_place = step("K")

    scratch = [pltpu.VMEM((8 * rows, quarter), bf16)]
    flops = 2 * 8 * rows * quarter * planes * rank
    part = call(
        functools.partial(sum_z, False, planes, merged),
        jax.ShapeDtypeStruct((8, rows, 2 * rank), f32),
        (first_place, *blocks, *a_units),
        scalars=1,
        flops=flops,
        scratch=scratch,
    )
    z_here, z_x, z_y, z_d = call(
        functools.partial(sum_z, True, planes, merged),
        (jax.ShapeDtypeStruct((2, rows, 2 * rank), f32),) * 4,
        (place, *blocks, *b_units, part),
        scalars=1,
        flops=flops,
        scratch=scratch,
    )
    here_sum, away = call(
        functools.partial(add_up, planes),
        (jax.ShapeDtypeStruct((rows, qwidth), f32),) * 2,
        (place, base, mine, pair, z_here, to_x(z_x), to_y(z_y), to_d(z_d), *ups),
        scalars=1,
        flops=2 * rows * owners * rank * qwidth,
    )
    return call(
        add, jax.ShapeDtypeStruct((rows, qwidth), bf16), (here_sum, to_core(away)), flops=rows * qwidth
    )


def solution(mesh):
    return jax.shard_map(
        body,
        mesh=mesh,
        in_specs=(
            P(("replica", "owner"), None),
            P(),
            P("owner", None, None),
            P("owner", None, None),
            P(("replica", "owner"), None),
            P(("replica", "owner")),
            P(),
        ),
        out_specs=P(("replica", "owner"), None),
        check_vma=False,
    )
```

time: 74 us -> 66.3 us (0.90)
  waiting for transfers between devices: 31.1 us -> 24.6 us
  local copies, waits for them, and re-layouts: 3.48 us -> 0.02 us
  starting transfers between devices: 25.6 us -> 28.6 us
  other arithmetic: 1.73 us -> 0.22 us
  Pallas kernels: 5.89 us -> 6.84 us
    ppermute x6, waiting for transfers between devices: 5.11 us -> 0.02 us  [across(): return lax.ppermute(value, ('replica', 'owner'), pairs)]
    ppermute x17 -> x11, waiting for transfers between devices: 24.1 us -> 20.2 us  [by_owner(): return lax.ppermute(value, 'owner', [(i, i ^ flip) for i in range(owners)])]
    unnamed x8 -> x2, local copies, waits for them, and re-layouts: 3.31 us -> 0.01 us
    ppermute x17 -> x11, starting transfers between devices: 12.4 us -> 15 us  [by_owner(): return lax.ppermute(value, 'owner', [(i, i ^ flip) for i in range(owners)])]
    ppermute x4, waiting for transfers between devices: 1.9 us -> 4.36 us  [between(): lax.ppermute(value, 'owner', [(a * 4 + i, b * 4 + i) for a, b in pairs fo...]
    reduce_sum x2 -> x0, other arithmetic: 1.59 us -> none  [the longest x1 0.85 us: body(): jnp.sum(jnp.where(group_variants[0][:, None] == variants[None, :], slot_o...]
    pallas_call x5, Pallas kernels: 5.89 us -> 6.84 us  [call(): pl.pallas_call(kernel, out_shape=out, in_specs=[SMEM] * scalars + [VMEM]...]
  transfers between devices with their start and end apart: 27 -> 21, of which waited for: 10 -> 9; matrix products, arithmetic and copies ran while one was open for 10% -> 9% of each run, Pallas kernels for 5% -> 4%
where the time goes in v3:
time: 66.3 us; the launch traced here: 66 us
  starting transfers between devices  28.6 us (43%)
  waiting for transfers between devices  24.6 us (37%)
  Pallas kernels  6.84 us (10%)
  matrix products  5.52 us (8%)
    ppermute x11, waiting for transfers between devices, by_owner(): return lax.ppermute(value, 'owner', [(i, i ^ flip) for i in range(owners)])  20.2 us
    ppermute x11, starting transfers between devices, by_owner(): return lax.ppermute(value, 'owner', [(i, i ^ flip) for i in range(owners)])  15 us
    ppermute x6, starting transfers between devices, across(): return lax.ppermute(value, ('replica', 'owner'), pairs)  9.69 us
    pallas_call x5, Pallas kernels, call(): pl.pallas_call(kernel, out_shape=out, in_specs=[SMEM] * scalars + [VMEM]...  6.84 us
    dot_general x1, matrix products, body(): jnp.dot(*late(hidden), base_weight, preferred_element_type=f32)  5.52 us
    ppermute x4, waiting for transfers between devices, between(): lax.ppermute(value, 'owner', [(a * 4 + i, b * 4 + i) for a, b in pairs fo...  4.36 us
    ppermute x4, starting transfers between devices, between(): lax.ppermute(value, 'owner', [(a * 4 + i, b * 4 + i) for a, b in pairs fo...  3.91 us
  transfers between devices with their start and end apart: 21, of which 9 were waited for; matrix products, arithmetic and copies ran while one was open for 9% of the time, Pallas kernels for 4%

profile of v3, /device:TPU:0, one launch (start us, length us, event | category | flops | bytes accessed | tf_op | source)
XLA Modules:
  0.0 66.0 jit_solution(5440319508209394251)
XLA Ops:
  0.0 0.0 copy-start
  0.0 0.1 pad_add_fusion.place
  0.1 2.1 %shard_map.73 = (bf16[64,1280]{1,0:T(8,128)(2,1)S(1)}, bf16[64,1792]{1,0:T(8,128)(2,1)S(1)}, bf16[128,1408]{1,0:T(8,128)(2,1)S(1)}, bf16[128,1408]{1,0:T(8,128)(...) custom-call(s32[4]{0:T(128)S(1)} %pad_add_fusion.place, bf16[1,64,5120]{2,1,0:T(8,128)(2,1)} %down.1, ...), custom_call_target="tpu_custom_call" | custom-call | bytes 2097760 | tf_op jit(solution)/shard_map/pallas_call | solution.py:35
  2.2 3.1 %collective-permute-start.4 = (bf16[64,1792]{1,0:T(8,128)(2,1)S(1)}, bf16[64,1792]{1,0:T(8,128)(2,1)S(1)}, u32[]{:S(2)}, u32[]{:S(2)}) collective-permute-start(bf16[64,1792]{1,0:T(8,128)(2,1)S(1)} %get-tuple-element.35.refs_6_), channel_id=1, source_target_pairs={{0,4},{1,5},{2,6},{3,7},{4,0},{5,1},{6,2},{7,3},{8,12},{9,13},{10,... | collective-permute-start | bytes 688136 | tf_op jit(solution)/shard_map/ppermute | solution.py:178
  5.3 1.5 %collective-permute-start = (bf16[64,1280]{1,0:T(8,128)(2,1)S(1)}, bf16[64,1280]{1,0:T(8,128)(2,1)S(1)}, u32[]{:S(2)}, u32[]{:S(2)}) collective-permute-start(bf16[64,1280]{1,0:T(8,128)(2,1)S(1)} %get-tuple-element.29), channel_id=1, source_target_pairs={{0,2},{1,3},{2,0},{3,1},{4,6},{5,7},{6,4},{7,5},{8,10},{9,11},{10,... | collective-permute-start | bytes 491528 | tf_op jit(solution)/shard_map/ppermute | solution.py:178
  6.8 2.6 %collective-permute-start.2 = (bf16[64,1792]{1,0:T(8,128)(2,1)S(1)}, bf16[64,1792]{1,0:T(8,128)(2,1)S(1)}, u32[]{:S(2)}, u32[]{:S(2)}) collective-permute-start(bf16[64,1792]{1,0:T(8,128)(2,1)S(1)} %get-tuple-element.35.refs_6_), channel_id=1, source_target_pairs={{0,8},{1,9},{2,10},{3,11},{4,12},{5,13},{6,14},{7,15},{8,0},{9,1},... | collective-permute-start | bytes 688136 | tf_op jit(solution)/shard_map/ppermute | solution.py:178
  9.4 1.5 %collective-permute-start.1 = (bf16[128,1408]{1,0:T(8,128)(2,1)S(1)}, bf16[128,1408]{1,0:T(8,128)(2,1)S(1)}, u32[]{:S(2)}, u32[]{:S(2)}) collective-permute-start(bf16[128,1408]{1,0:T(8,128)(2,1)S(1)} %get-tuple-element.32), channel_id=1, source_target_pairs={{0,16},{1,17},{2,18},{3,19},{4,20},{5,21},{6,22},{7,23},{8,24},{9,... | collective-permute-start | bytes 1081352 | tf_op jit(solution)/shard_map/ppermute | solution.py:189
  10.9 0.1 collective-permute-done.refs_6_
  11.0 3.5 %collective-permute-done.4.refs_7_ = bf16[64,1792]{1,0:T(8,128)(2,1)S(1)} collective-permute-done((bf16[64,1792]{1,0:T(8,128)(2,1)S(1)}, bf16[64,1792]{1,0:T(8,128)(2,1)S(1)}, u32[]{:S(2)}, u32[]{:S(2)}) %collective-permute-start.4) | collective-permute-done | bytes 229408 | tf_op jit(solution)/shard_map/ppermute | solution.py:178
  14.5 0.7 %collective-permute-start.5 = (bf16[64,1792]{1,0:T(8,128)(2,1)S(1)}, bf16[64,1792]{1,0:T(8,128)(2,1)S(1)}, u32[]{:S(2)}, u32[]{:S(2)}) collective-permute-start(bf16[64,1792]{1,0:T(8,128)(2,1)S(1)} %get-tuple-element.35.refs_6_), channel_id=1, source_target_pairs={{4,8},{5,9},{6,10},{7,11},{8,4},{9,5},{10,6},{11,7},{20,24},{21,25... | collective-permute-start | bytes 688136 | tf_op jit(solution)/shard_map/ppermute | solution.py:181
  15.1 2.8 %collective-permute-start.6 = (bf16[128,1408]{1,0:T(8,128)(2,1)S(1)}, bf16[128,1408]{1,0:T(8,128)(2,1)S(1)}, u32[]{:S(2)}, u32[]{:S(2)}) collective-permute-start(bf16[128,1408]{1,0:T(8,128)(2,1)S(1)} %get-tuple-element.37), channel_id=1, source_target_pairs={{0,2},{1,3},{2,0},{3,1},{4,6},{5,7},{6,4},{7,5},{8,10},{9,11},{10,... | collective-permute-start | bytes 1081352 | tf_op jit(solution)/shard_map/ppermute | solution.py:178
  17.9 0.0 copy-done
  17.9 5.5 %fusion.base = f32[128,1024]{1,0:T(8,128)S(1)} fusion(bf16[128,5120]{1,0:T(8,128)(2,1)S(1)} %copy-done, bf16[5120,1024]{1,0:T(8,128)(2,1)} %param.8), kind=kOutput, calls=%fused_computation.5 | convolution fusion | flops 1342177280 | bytes 12320768 | tf_op jit(solution)/shard_map/dot_general | solution.py:263
  23.4 0.0 collective-permute-done.2.refs_8_
  23.4 1.3 %collective-permute-start.3 = (bf16[64,1792]{1,0:T(8,128)(2,1)S(1)}, bf16[64,1792]{1,0:T(8,128)(2,1)S(1)}, u32[]{:S(2)}, u32[]{:S(2)}) collective-permute-start(bf16[64,1792]{1,0:T(8,128)(2,1)S(1)} %collective-permute-done.2.refs_8_), channel_id=1, source_target_pairs={{4,0},{5,1},{6,2},{7,3},{8,12},{9,13},{10,14},{11,15},{20,16},{21,... | collective-permute-start | bytes 688136 | tf_op jit(solution)/shard_map/ppermute | solution.py:181
  24.7 3.7 %collective-permute-start.8 = (bf16[64,1280]{1,0:T(8,128)(2,1)S(1)}, bf16[64,1280]{1,0:T(8,128)(2,1)S(1)}, u32[]{:S(2)}, u32[]{:S(2)}) collective-permute-start(bf16[64,1280]{1,0:T(8,128)(2,1)S(1)} %collective-permute-done.refs_6_), channel_id=1, source_target_pairs={{0,8},{1,9},{2,10},{3,11},{4,12},{5,13},{6,14},{7,15},{8,0},{9,1},... | collective-permute-start | bytes 491528 | tf_op jit(solution)/shard_map/ppermute | solution.py:178
  28.5 0.0 collective-permute-done.5.refs_9_
  28.5 0.0 collective-permute-done.6.refs_2_
  28.5 0.0 collective-permute-start.7
  28.5 0.0 collective-permute-done.1.refs_1_
  28.5 1.7 %collective-permute-start.10 = (bf16[128,1408]{1,0:T(8,128)(2,1)S(1)}, bf16[128,1408]{1,0:T(8,128)(2,1)S(1)}, u32[]{:S(2)}, u32[]{:S(2)}) collective-permute-start(bf16[128,1408]{1,0:T(8,128)(2,1)S(1)} %get-tuple-element.42), channel_id=1, source_target_pairs={{0,18},{1,19},{2,16},{3,17},{4,22},{5,23},{6,20},{7,21},{8,26},{9,... | collective-permute-start | bytes 1081352 | tf_op jit(solution)/shard_map/ppermute | solution.py:189
  30.2 4.7 %collective-permute-done.8.refs_8_ = bf16[64,1280]{1,0:T(8,128)(2,1)S(1)} collective-permute-done((bf16[64,1280]{1,0:T(8,128)(2,1)S(1)}, bf16[64,1280]{1,0:T(8,128)(2,1)S(1)}, u32[]{:S(2)}, u32[]{:S(2)}) %collective-permute-start.8) | collective-permute-done | bytes 163872 | tf_op jit(solution)/shard_map/ppermute | solution.py:178
  34.9 1.4 %collective-permute-done.3.refs_10_ = bf16[64,1792]{1,0:T(8,128)(2,1)S(1)} collective-permute-done((bf16[64,1792]{1,0:T(8,128)(2,1)S(1)}, bf16[64,1792]{1,0:T(8,128)(2,1)S(1)}, u32[]{:S(2)}, u32[]{:S(2)}) %collective-permute-start.3) | collective-permute-done | bytes 229408 | tf_op jit(solution)/shard_map/ppermute | solution.py:181
  36.3 2.2 %collective-permute-done.7.refs_7_ = bf16[64,1280]{1,0:T(8,128)(2,1)S(1)} collective-permute-done((bf16[64,1280]{1,0:T(8,128)(2,1)S(1)}, bf16[64,1280]{1,0:T(8,128)(2,1)S(1)}, u32[]{:S(2)}, u32[]{:S(2)}) %collective-permute-start.7) | collective-permute-done | bytes 163872 | tf_op jit(solution)/shard_map/ppermute | solution.py:178
  38.5 0.1 pad_maximum_fusion
  38.6 0.1 collective-permute-start.9
  38.7 0.0 collective-permute-done.10.refs_3_
  38.7 0.1 pad_maximum_fusion.1
  38.7 0.5 collective-permute-start.11
  39.4 1.6 %collective-permute-start.17 = (bf16[256,512]{1,0:T(8,128)(2,1)S(1)}, bf16[256,512]{1,0:T(8,128)(2,1)S(1)}, u32[]{:S(2)}, u32[]{:S(2)}) collective-permute-start(bf16[256,512]{1,0:T(8,128)(2,1)S(1)} %pad_maximum_fusion.2.refs_0_), channel_id=1, source_target_pairs={{0,16},{1,17},{2,18},{3,19},{4,20},{5,21},{6,22},{7,23},{8,24},{9,... | collective-permute-start | bytes 786440 | tf_op jit(solution)/shard_map/ppermute | solution.py:189
  40.9 0.7 collective-permute-start.12
  41.6 1.3 %collective-permute-start.13 = (bf16[64,1280]{1,0:T(8,128)(2,1)S(1)}, bf16[64,1280]{1,0:T(8,128)(2,1)S(1)}, u32[]{:S(2)}, u32[]{:S(2)}) collective-permute-start(bf16[64,1280]{1,0:T(8,128)(2,1)S(1)} %collective-permute-done.8.refs_8_), channel_id=1, source_target_pairs={{4,0},{5,1},{6,2},{7,3},{8,12},{9,13},{10,14},{11,15},{20,16},{21,... | collective-permute-start | bytes 491528 | tf_op jit(solution)/shard_map/ppermute | solution.py:181
  42.9 0.0 collective-permute-done.9.refs_4_.theirs
  42.9 0.4 collective-permute-start.18
  43.3 0.0 collective-permute-done.11.refs_5_
  43.3 1.7 %collective-permute-start.19 = (bf16[256,512]{1,0:T(8,128)(2,1)S(1)}, bf16[256,512]{1,0:T(8,128)(2,1)S(1)}, u32[]{:S(2)}, u32[]{:S(2)}) collective-permute-start(bf16[256,512]{1,0:T(8,128)(2,1)S(1)} %pad_maximum_fusion.2.refs_0_), channel_id=1, source_target_pairs={{0,18},{1,19},{2,16},{3,17},{4,22},{5,23},{6,20},{7,21},{8,26},{9,... | collective-permute-start | bytes 786440 | tf_op jit(solution)/shard_map/ppermute | solution.py:189
  45.0 1.4 %shard_map.74.refs_11_ = f32[8,128,128]{2,1,0:T(8,128)S(1)} custom-call(s32[4]{0:T(128)S(1)} %pad_add_fusion.place, bf16[128,1408]{1,0:T(8,128)(2,1)S(1)} %get-tuple-element.39.refs_0_.mine, bf16[128,1408]{1,0:T(8,128)(2,1)S(1)} %collective-permute-done.1.refs_1_, bf16[128,1408]{1,0:T(8,128)(2,1)S(1)} %collective-permute-done.6.refs_2_, ...), custom_call_target="tpu_custom_call" | custom-call | flops 671088640 | bytes 4030480 | tf_op jit(solution)/shard_map/pallas_call | solution.py:35
  46.4 0.0 collective-permute-done.12.refs_9_
  46.4 2.9 %collective-permute-done.13.refs_10_ = bf16[64,1280]{1,0:T(8,128)(2,1)S(1)} collective-permute-done((bf16[64,1280]{1,0:T(8,128)(2,1)S(1)}, bf16[64,1280]{1,0:T(8,128)(2,1)S(1)}, u32[]{:S(2)}, u32[]{:S(2)}) %collective-permute-start.13) | collective-permute-done | bytes 163872 | tf_op jit(solution)/shard_map/ppermute | solution.py:181
  49.3 1.4 %shard_map.75 = (f32[2,128,128]{2,1,0:T(8,128)S(1)}, f32[2,128,128]{2,1,0:T(8,128)S(1)}, f32[2,128,128]{2,1,0:T(8,128)S(1)}, f32[2,128,128]{2,1,0:T(8,128)S(1)}) custom-call(s32[4]{0:T(128)S(1)} %pad_add_fusion.place, bf16[128,1408]{1,0:T(8,128)(2,1)S(1)} %get-tuple-element.39.refs_0_.mine, bf16[128,1408]{1,0:T(8,128)(2,1)S(1)} %collective-permute-done.1.refs_1_, ...), custom_call_target="tpu_custom_call" | custom-call | flops 671088640 | bytes 4227088 | tf_op jit(solution)/shard_map/pallas_call | solution.py:35
  50.8 0.6 collective-permute-start.14
  51.4 0.3 collective-permute-start.15
  51.7 0.0 collective-permute-done.17.refs_1_
  51.7 2.7 %collective-permute-start.16 = (f32[2,128,128]{2,1,0:T(8,128)S(1)}, f32[2,128,128]{2,1,0:T(8,128)S(1)}, u32[]{:S(2)}, u32[]{:S(2)}) collective-permute-start(f32[2,128,128]{2,1,0:T(8,128)S(1)} %get-tuple-element.50), channel_id=1, source_target_pairs={{0,18},{1,19},{2,16},{3,17},{4,22},{5,23},{6,20},{7,21},{8,26},{9,... | collective-permute-start | bytes 393224 | tf_op jit(solution)/shard_map/ppermute | solution.py:189
  54.3 6.2 %collective-permute-done.18.refs_2_ = bf16[256,512]{1,0:T(8,128)(2,1)S(1)} collective-permute-done((bf16[256,512]{1,0:T(8,128)(2,1)S(1)}, bf16[256,512]{1,0:T(8,128)(2,1)S(1)}, u32[]{:S(2)}, u32[]{:S(2)}) %collective-permute-start.18) | collective-permute-done | bytes 262176 | tf_op jit(solution)/shard_map/ppermute | solution.py:178
  60.6 0.0 collective-permute-done.19.refs_3_
  60.6 0.0 collective-permute-done.14.z_x
  60.6 1.6 %collective-permute-done.15.z_y = f32[2,128,128]{2,1,0:T(8,128)S(1)} collective-permute-done((f32[2,128,128]{2,1,0:T(8,128)S(1)}, f32[2,128,128]{2,1,0:T(8,128)S(1)}, u32[]{:S(2)}, u32[]{:S(2)}) %collective-permute-start.15) | collective-permute-done | bytes 131104 | tf_op jit(solution)/shard_map/ppermute | solution.py:178
  62.2 0.0 collective-permute-done.16.z_d
  62.2 1.1 %shard_map.76 = (f32[128,1024]{1,0:T(8,128)S(1)}, f32[128,1024]{1,0:T(8,128)S(1)}) custom-call(s32[4]{0:T(128)S(1)} %pad_add_fusion.place, f32[128,1024]{1,0:T(8,128)S(1)} %fusion.base, bf16[128,1408]{1,0:T(8,128)(2,1)S(1)} %get-tuple-element.39.refs_0_.mine, bf16[256,1408]{1,0:T(8,128)(2,1)S(1)} %collective-permute-done.9.refs_4_.theirs, ...), custom_call_target="tpu_custom_call" | custom-call | flops 268435456 | bytes 3178512 | tf_op jit(solution)/shard_map/pallas_call | solution.py:35
  63.3 0.1 collective-permute-start.20
  63.4 1.9 %collective-permute-done.20.came = f32[128,1024]{1,0:T(8,128)S(1)} collective-permute-done((f32[128,1024]{1,0:T(8,128)S(1)}, f32[128,1024]{1,0:T(8,128)S(1)}, u32[]{:S(2)}, u32[]{:S(2)}) %collective-permute-start.20) | collective-permute-done | bytes 524320 | tf_op jit(solution)/shard_map/ppermute | solution.py:178
  65.3 0.8 %shard_map.77 = bf16[128,1024]{1,0:T(8,128)(2,1)} custom-call(f32[128,1024]{1,0:T(8,128)S(1)} %get-tuple-element.51.here, f32[128,1024]{1,0:T(8,128)S(1)} %collective-permute-done.20.came), custom_call_target="tpu_custom_call" | custom-call | flops 131072 | bytes 1048576 | tf_op jit(solution)/shard_map/pallas_call | solution.py:35
  (5 shorter events, 0.0 us)
Async XLA Ops:
  0.0 17.9 %copy-start = (bf16[128,5120]{1,0:T(8,128)(2,1)S(1)}, bf16[128,5120]{1,0:T(8,128)(2,1)}, u32[]{:S(2)}) copy-start(bf16[128,5120]{1,0:T(8,128)(2,1)} %hidden.1) | copy-start | bytes 3932164
  2.2 12.3 %collective-permute-start.4 = (bf16[64,1792]{1,0:T(8,128)(2,1)S(1)}, bf16[64,1792]{1,0:T(8,128)(2,1)S(1)}, u32[]{:S(2)}, u32[]{:S(2)}) collective-permute-start(bf16[64,1792]{1,0:T(8,128)(2,1)S(1)} %get-tuple-element.35.refs_6_), channel_id=1, source_target_pairs={{0,4},{1,5},{2,6},{3,7},{4,0},{5,1},{6,2},{7,3},{8,12},{9,13},{10,... | collective-permute-start | bytes 688136 | tf_op jit(solution)/shard_map/ppermute | solution.py:178
  5.3 5.7 %collective-permute-start = (bf16[64,1280]{1,0:T(8,128)(2,1)S(1)}, bf16[64,1280]{1,0:T(8,128)(2,1)S(1)}, u32[]{:S(2)}, u32[]{:S(2)}) collective-permute-start(bf16[64,1280]{1,0:T(8,128)(2,1)S(1)} %get-tuple-element.29), channel_id=1, source_target_pairs={{0,2},{1,3},{2,0},{3,1},{4,6},{5,7},{6,4},{7,5},{8,10},{9,11},{10,... | collective-permute-start | bytes 491528 | tf_op jit(solution)/shard_map/ppermute | solution.py:178
  6.8 16.6 %collective-permute-start.2 = (bf16[64,1792]{1,0:T(8,128)(2,1)S(1)}, bf16[64,1792]{1,0:T(8,128)(2,1)S(1)}, u32[]{:S(2)}, u32[]{:S(2)}) collective-permute-start(bf16[64,1792]{1,0:T(8,128)(2,1)S(1)} %get-tuple-element.35.refs_6_), channel_id=1, source_target_pairs={{0,8},{1,9},{2,10},{3,11},{4,12},{5,13},{6,14},{7,15},{8,0},{9,1},... | collective-permute-start | bytes 688136 | tf_op jit(solution)/shard_map/ppermute | solution.py:178
  9.4 19.1 %collective-permute-start.1 = (bf16[128,1408]{1,0:T(8,128)(2,1)S(1)}, bf16[128,1408]{1,0:T(8,128)(2,1)S(1)}, u32[]{:S(2)}, u32[]{:S(2)}) collective-permute-start(bf16[128,1408]{1,0:T(8,128)(2,1)S(1)} %get-tuple-element.32), channel_id=1, source_target_pairs={{0,16},{1,17},{2,18},{3,19},{4,20},{5,21},{6,22},{7,23},{8,24},{9,... | collective-permute-start | bytes 1081352 | tf_op jit(solution)/shard_map/ppermute | solution.py:189
  14.5 14.0 %collective-permute-start.5 = (bf16[64,1792]{1,0:T(8,128)(2,1)S(1)}, bf16[64,1792]{1,0:T(8,128)(2,1)S(1)}, u32[]{:S(2)}, u32[]{:S(2)}) collective-permute-start(bf16[64,1792]{1,0:T(8,128)(2,1)S(1)} %get-tuple-element.35.refs_6_), channel_id=1, source_target_pairs={{4,8},{5,9},{6,10},{7,11},{8,4},{9,5},{10,6},{11,7},{20,24},{21,25... | collective-permute-start | bytes 688136 | tf_op jit(solution)/shard_map/ppermute | solution.py:181
  15.1 13.3 %collective-permute-start.6 = (bf16[128,1408]{1,0:T(8,128)(2,1)S(1)}, bf16[128,1408]{1,0:T(8,128)(2,1)S(1)}, u32[]{:S(2)}, u32[]{:S(2)}) collective-permute-start(bf16[128,1408]{1,0:T(8,128)(2,1)S(1)} %get-tuple-element.37), channel_id=1, source_target_pairs={{0,2},{1,3},{2,0},{3,1},{4,6},{5,7},{6,4},{7,5},{8,10},{9,11},{10,... | collective-permute-start | bytes 1081352 | tf_op jit(solution)/shard_map/ppermute | solution.py:178
  23.4 12.9 %collective-permute-start.3 = (bf16[64,1792]{1,0:T(8,128)(2,1)S(1)}, bf16[64,1792]{1,0:T(8,128)(2,1)S(1)}, u32[]{:S(2)}, u32[]{:S(2)}) collective-permute-start(bf16[64,1792]{1,0:T(8,128)(2,1)S(1)} %collective-permute-done.2.refs_8_), channel_id=1, source_target_pairs={{4,0},{5,1},{6,2},{7,3},{8,12},{9,13},{10,14},{11,15},{20,16},{21,... | collective-permute-start | bytes 688136 | tf_op jit(solution)/shard_map/ppermute | solution.py:181
  24.7 10.2 %collective-permute-start.8 = (bf16[64,1280]{1,0:T(8,128)(2,1)S(1)}, bf16[64,1280]{1,0:T(8,128)(2,1)S(1)}, u32[]{:S(2)}, u32[]{:S(2)}) collective-permute-start(bf16[64,1280]{1,0:T(8,128)(2,1)S(1)} %collective-permute-done.refs_6_), channel_id=1, source_target_pairs={{0,8},{1,9},{2,10},{3,11},{4,12},{5,13},{6,14},{7,15},{8,0},{9,1},... | collective-permute-start | bytes 491528 | tf_op jit(solution)/shard_map/ppermute | solution.py:178
  28.5 10.1 %collective-permute-start.7 = (bf16[64,1280]{1,0:T(8,128)(2,1)S(1)}, bf16[64,1280]{1,0:T(8,128)(2,1)S(1)}, u32[]{:S(2)}, u32[]{:S(2)}) collective-permute-start(bf16[64,1280]{1,0:T(8,128)(2,1)S(1)} %collective-permute-done.refs_6_), channel_id=1, source_target_pairs={{0,4},{1,5},{2,6},{3,7},{4,0},{5,1},{6,2},{7,3},{8,12},{9,13},{10,... | collective-permute-start | bytes 491528 | tf_op jit(solution)/shard_map/ppermute | solution.py:178
  28.5 10.2 %collective-permute-start.10 = (bf16[128,1408]{1,0:T(8,128)(2,1)S(1)}, bf16[128,1408]{1,0:T(8,128)(2,1)S(1)}, u32[]{:S(2)}, u32[]{:S(2)}) collective-permute-start(bf16[128,1408]{1,0:T(8,128)(2,1)S(1)} %get-tuple-element.42), channel_id=1, source_target_pairs={{0,18},{1,19},{2,16},{3,17},{4,22},{5,23},{6,20},{7,21},{8,26},{9,... | collective-permute-start | bytes 1081352 | tf_op jit(solution)/shard_map/ppermute | solution.py:189
  38.6 4.3 %collective-permute-start.9 = (bf16[256,1408]{1,0:T(8,128)(2,1)S(1)}, bf16[256,1408]{1,0:T(8,128)(2,1)S(1)}, u32[]{:S(2)}, u32[]{:S(2)}) collective-permute-start(bf16[256,1408]{1,0:T(8,128)(2,1)S(1)} %pad_maximum_fusion), channel_id=1, source_target_pairs={{0,1},{1,0},{2,3},{3,2},{4,5},{5,4},{6,7},{7,6},{8,9},{9,8},{10,11... | collective-permute-start | bytes 2162696 | tf_op jit(solution)/shard_map/ppermute | solution.py:178
  38.7 4.5 %collective-permute-start.11 = (bf16[256,1408]{1,0:T(8,128)(2,1)S(1)}, bf16[256,1408]{1,0:T(8,128)(2,1)S(1)}, u32[]{:S(2)}, u32[]{:S(2)}) collective-permute-start(bf16[256,1408]{1,0:T(8,128)(2,1)S(1)} %pad_maximum_fusion.1), channel_id=1, source_target_pairs={{0,1},{1,0},{2,3},{3,2},{4,5},{5,4},{6,7},{7,6},{8,9},{9,8},{10,11... | collective-permute-start | bytes 2162696 | tf_op jit(solution)/shard_map/ppermute | solution.py:178
  39.4 12.3 %collective-permute-start.17 = (bf16[256,512]{1,0:T(8,128)(2,1)S(1)}, bf16[256,512]{1,0:T(8,128)(2,1)S(1)}, u32[]{:S(2)}, u32[]{:S(2)}) collective-permute-start(bf16[256,512]{1,0:T(8,128)(2,1)S(1)} %pad_maximum_fusion.2.refs_0_), channel_id=1, source_target_pairs={{0,16},{1,17},{2,18},{3,19},{4,20},{5,21},{6,22},{7,23},{8,24},{9,... | collective-permute-start | bytes 786440 | tf_op jit(solution)/shard_map/ppermute | solution.py:189
  40.9 5.5 %collective-permute-start.12 = (bf16[64,1280]{1,0:T(8,128)(2,1)S(1)}, bf16[64,1280]{1,0:T(8,128)(2,1)S(1)}, u32[]{:S(2)}, u32[]{:S(2)}) collective-permute-start(bf16[64,1280]{1,0:T(8,128)(2,1)S(1)} %collective-permute-done.refs_6_), channel_id=1, source_target_pairs={{4,8},{5,9},{6,10},{7,11},{8,4},{9,5},{10,6},{11,7},{20,24},{21,25... | collective-permute-start | bytes 491528 | tf_op jit(solution)/shard_map/ppermute | solution.py:181
  41.6 7.7 %collective-permute-start.13 = (bf16[64,1280]{1,0:T(8,128)(2,1)S(1)}, bf16[64,1280]{1,0:T(8,128)(2,1)S(1)}, u32[]{:S(2)}, u32[]{:S(2)}) collective-permute-start(bf16[64,1280]{1,0:T(8,128)(2,1)S(1)} %collective-permute-done.8.refs_8_), channel_id=1, source_target_pairs={{4,0},{5,1},{6,2},{7,3},{8,12},{9,13},{10,14},{11,15},{20,16},{21,... | collective-permute-start | bytes 491528 | tf_op jit(solution)/shard_map/ppermute | solution.py:181
  42.9 17.7 %collective-permute-start.18 = (bf16[256,512]{1,0:T(8,128)(2,1)S(1)}, bf16[256,512]{1,0:T(8,128)(2,1)S(1)}, u32[]{:S(2)}, u32[]{:S(2)}) collective-permute-start(bf16[256,512]{1,0:T(8,128)(2,1)S(1)} %pad_maximum_fusion.2.refs_0_), channel_id=1, source_target_pairs={{0,2},{1,3},{2,0},{3,1},{4,6},{5,7},{6,4},{7,5},{8,10},{9,11},{10,... | collective-permute-start | bytes 786440 | tf_op jit(solution)/shard_map/ppermute | solution.py:178
  43.3 17.3 %collective-permute-start.19 = (bf16[256,512]{1,0:T(8,128)(2,1)S(1)}, bf16[256,512]{1,0:T(8,128)(2,1)S(1)}, u32[]{:S(2)}, u32[]{:S(2)}) collective-permute-start(bf16[256,512]{1,0:T(8,128)(2,1)S(1)} %pad_maximum_fusion.2.refs_0_), channel_id=1, source_target_pairs={{0,18},{1,19},{2,16},{3,17},{4,22},{5,23},{6,20},{7,21},{8,26},{9,... | collective-permute-start | bytes 786440 | tf_op jit(solution)/shard_map/ppermute | solution.py:189
  50.8 9.8 %collective-permute-start.14 = (f32[2,128,128]{2,1,0:T(8,128)S(1)}, f32[2,128,128]{2,1,0:T(8,128)S(1)}, u32[]{:S(2)}, u32[]{:S(2)}) collective-permute-start(f32[2,128,128]{2,1,0:T(8,128)S(1)} %get-tuple-element.48), channel_id=1, source_target_pairs={{0,16},{1,17},{2,18},{3,19},{4,20},{5,21},{6,22},{7,23},{8,24},{9,... | collective-permute-start | bytes 393224 | tf_op jit(solution)/shard_map/ppermute | solution.py:189
  51.4 10.8 %collective-permute-start.15 = (f32[2,128,128]{2,1,0:T(8,128)S(1)}, f32[2,128,128]{2,1,0:T(8,128)S(1)}, u32[]{:S(2)}, u32[]{:S(2)}) collective-permute-start(f32[2,128,128]{2,1,0:T(8,128)S(1)} %get-tuple-element.49), channel_id=1, source_target_pairs={{0,2},{1,3},{2,0},{3,1},{4,6},{5,7},{6,4},{7,5},{8,10},{9,11},{10,... | collective-permute-start | bytes 393224 | tf_op jit(solution)/shard_map/ppermute | solution.py:178
  51.7 10.5 %collective-permute-start.16 = (f32[2,128,128]{2,1,0:T(8,128)S(1)}, f32[2,128,128]{2,1,0:T(8,128)S(1)}, u32[]{:S(2)}, u32[]{:S(2)}) collective-permute-start(f32[2,128,128]{2,1,0:T(8,128)S(1)} %get-tuple-element.50), channel_id=1, source_target_pairs={{0,18},{1,19},{2,16},{3,17},{4,22},{5,23},{6,20},{7,21},{8,26},{9,... | collective-permute-start | bytes 393224 | tf_op jit(solution)/shard_map/ppermute | solution.py:189
  63.3 2.0 %collective-permute-start.20 = (f32[128,1024]{1,0:T(8,128)S(1)}, f32[128,1024]{1,0:T(8,128)S(1)}, u32[]{:S(2)}, u32[]{:S(2)}) collective-permute-start(f32[128,1024]{1,0:T(8,128)S(1)} %get-tuple-element.52), channel_id=1, source_target_pairs={{0,1},{1,0},{2,3},{3,2},{4,5},{5,4},{6,7},{7,6},{8,9},{9,8},{10,11... | collective-permute-start | bytes 1572872 | tf_op jit(solution)/shard_map/ppermute | solution.py:178

commit v4 on v3

--- a/solution.py
+++ b/solution.py
@@ -8,18 +8,11 @@
 from jax.sharding import PartitionSpec as P
 
 TAG = 128
-ORDER = {
-    "Y": ("P", "A1"),
-    "A3": ("A1", "P"),
-    "D": ("X", "A2"),
-    "B1": ("A3", "Y"),
-    "B3": ("A3",),
-    "base": ("P",),
-    "A4": ("base",),
-    "B4": ("A4",),
-    "C1": ("A4", "B1", "B2"),
-    "C2": ("A4", "B1", "B2"),
-}
+FIRST = ("P", "X", "A2", "A1", "Y")
+SECOND = ("A4", "A3", "D")
+ORDER = {"D": ("P",)}
+ORDER |= dict.fromkeys(("A3", "A4", "B1", "B2", "B3"), FIRST)
+ORDER |= dict.fromkeys(("U", "C1", "C2"), SECOND)
 VMEM = pl.BlockSpec(memory_space=pltpu.VMEM)
 SMEM = pl.BlockSpec(memory_space=pltpu.SMEM)
 HBM = pl.BlockSpec(memory_space=pltpu.HBM)
@@ -258,8 +251,7 @@
         "A4": lambda late: ends(*late(step("A2"))),
         "B1": lambda late: by_owner(*late(step("P")), 4),
         "B2": lambda late: by_owner(*late(step("P")), 8),
-        "B3": lambda late: middle(*late(step("P"))),
-        "B4": lambda late: ends(*late(step("B2"))),
+        "B3": lambda late: by_owner(*late(step("P")), 12),
         "base": lambda late: jnp.dot(*late(hidden), base_weight, preferred_element_type=f32),
         "C1": lambda late: to_core(jnp.concatenate(late(mine, step("X")), axis=0)),
         "C2": lambda late: to_core(jnp.concatenate(late(step("Y"), step("D")), axis=0)),
@@ -271,7 +263,7 @@
     }
     if merged:
         a_units = [own] + [step(f"A{i}") for i in range(1, 5)]
-        b_units = [step("P")] + [step(f"B{i}") for i in range(1, 5)]
+        b_units = [step("P")] + [step(f"B{i}") for i in range(1, 4)]
         ups = [step("U"), step("UX"), step("UY"), step("UD")]
     else:
         a_units, b_units = along(own), along(step("P"))
@@ -292,7 +284,7 @@
         scratch=scratch,
     )
     z_here, z_x, z_y, z_d = call(
-        functools.partial(sum_z, True, planes, merged),
+        functools.partial(sum_z, True, planes, 0),
         (jax.ShapeDtypeStruct((2, rows, 2 * rank), f32),) * 4,
         (place, *blocks, *b_units, part),
         scalars=1,

time: 66.3 us -> 62.1 us (0.937)
  starting transfers between devices: 28.6 us -> 24 us
  waiting for transfers between devices: 24.6 us -> 27.4 us
  matrix products: 5.52 us -> 2.9 us
    ppermute x6, waiting for transfers between devices: 0.02 us -> 8.18 us  [across(): return lax.ppermute(value, ('replica', 'owner'), pairs)]
    ppermute x11 -> x12, waiting for transfers between devices: 20.2 us -> 17.2 us  [by_owner(): return lax.ppermute(value, 'owner', [(i, i ^ flip) for i in range(owners)])]
    dot_general x1, matrix products: 5.52 us -> 2.9 us  [body(): jnp.dot(*late(hidden), base_weight, preferred_element_type=f32)]
    ppermute x4 -> x2, waiting for transfers between devices: 4.36 us -> 1.99 us  [between(): lax.ppermute(value, 'owner', [(a * 4 + i, b * 4 + i) for a, b in pairs fo...]
    ppermute x4 -> x2, starting transfers between devices: 3.91 us -> 1.97 us  [between(): lax.ppermute(value, 'owner', [(a * 4 + i, b * 4 + i) for a, b in pairs fo...]
    ppermute x11 -> x12, starting transfers between devices: 15 us -> 13.3 us  [by_owner(): return lax.ppermute(value, 'owner', [(i, i ^ flip) for i in range(owners)])]
    ppermute x6, starting transfers between devices: 9.69 us -> 8.73 us  [across(): return lax.ppermute(value, ('replica', 'owner'), pairs)]
  transfers between devices with their start and end apart: 21 -> 20, of which waited for: 9 -> 7; matrix products, arithmetic and copies ran while one was open for 9% -> 5% of each run, Pallas kernels for 4% -> 5%
where the time goes in v4:
time: 62.1 us; the launch traced here: 61.5 us
  waiting for transfers between devices  27.4 us (44%)
  starting transfers between devices  24 us (39%)
  Pallas kernels  6.85 us (11%)
  matrix products  2.9 us (5%)
    ppermute x12, waiting for transfers between devices, by_owner(): return lax.ppermute(value, 'owner', [(i, i ^ flip) for i in range(owners)])  17.2 us
    ppermute x12, starting transfers between devices, by_owner(): return lax.ppermute(value, 'owner', [(i, i ^ flip) for i in range(owners)])  13.3 us
    ppermute x6, starting transfers between devices, across(): return lax.ppermute(value, ('replica', 'owner'), pairs)  8.73 us
    ppermute x6, waiting for transfers between devices, across(): return lax.ppermute(value, ('replica', 'owner'), pairs)  8.18 us
    pallas_call x5, Pallas kernels, call(): pl.pallas_call(kernel, out_shape=out, in_specs=[SMEM] * scalars + [VMEM]...  6.85 us
    dot_general x1, matrix products, body(): jnp.dot(*late(hidden), base_weight, preferred_element_type=f32)  2.9 us
    ppermute x2, waiting for transfers between devices, between(): lax.ppermute(value, 'owner', [(a * 4 + i, b * 4 + i) for a, b in pairs fo...  1.99 us
    ppermute x2, starting transfers between devices, between(): lax.ppermute(value, 'owner', [(a * 4 + i, b * 4 + i) for a, b in pairs fo...  1.97 us
  transfers between devices with their start and end apart: 20, of which 7 were waited for; matrix products, arithmetic and copies ran while one was open for 5% of the time, Pallas kernels for 5%

profile of v4, /device:TPU:0, one launch (start us, length us, event | category | flops | bytes accessed | tf_op | source)
XLA Modules:
  0.0 61.5 jit_solution(18030046810141822495)
XLA Ops:
  0.0 0.1 pad_add_fusion.place
  0.1 2.1 %shard_map.73 = (bf16[64,1280]{1,0:T(8,128)(2,1)S(1)}, bf16[64,1792]{1,0:T(8,128)(2,1)S(1)}, bf16[128,1408]{1,0:T(8,128)(2,1)S(1)}, bf16[128,1408]{1,0:T(8,128)(...) custom-call(s32[4]{0:T(128)S(1)} %pad_add_fusion.place, bf16[1,64,5120]{2,1,0:T(8,128)(2,1)} %down.1, ...), custom_call_target="tpu_custom_call" | custom-call | bytes 2097760 | tf_op jit(solution)/shard_map/pallas_call | solution.py:28
  2.2 3.0 %collective-permute-start = (bf16[128,1408]{1,0:T(8,128)(2,1)S(1)}, bf16[128,1408]{1,0:T(8,128)(2,1)S(1)}, u32[]{:S(2)}, u32[]{:S(2)}) collective-permute-start(bf16[128,1408]{1,0:T(8,128)(2,1)S(1)} %get-tuple-element.27), channel_id=1, source_target_pairs={{0,16},{1,17},{2,18},{3,19},{4,20},{5,21},{6,22},{7,23},{8,24},{9,... | collective-permute-start | bytes 1081352 | tf_op jit(solution)/shard_map/ppermute | solution.py:182
  5.2 1.5 %collective-permute-start.4 = (bf16[128,1408]{1,0:T(8,128)(2,1)S(1)}, bf16[128,1408]{1,0:T(8,128)(2,1)S(1)}, u32[]{:S(2)}, u32[]{:S(2)}) collective-permute-start(bf16[128,1408]{1,0:T(8,128)(2,1)S(1)} %get-tuple-element.30), channel_id=1, source_target_pairs={{0,2},{1,3},{2,0},{3,1},{4,6},{5,7},{6,4},{7,5},{8,10},{9,11},{10,... | collective-permute-start | bytes 1081352 | tf_op jit(solution)/shard_map/ppermute | solution.py:171
  6.7 0.5 collective-permute-start.2
  7.2 2.6 %collective-permute-start.1 = (bf16[64,1792]{1,0:T(8,128)(2,1)S(1)}, bf16[64,1792]{1,0:T(8,128)(2,1)S(1)}, u32[]{:S(2)}, u32[]{:S(2)}) collective-permute-start(bf16[64,1792]{1,0:T(8,128)(2,1)S(1)} %get-tuple-element.32.refs_6_), channel_id=1, source_target_pairs={{0,8},{1,9},{2,10},{3,11},{4,12},{5,13},{6,14},{7,15},{8,0},{9,1},... | collective-permute-start | bytes 688136 | tf_op jit(solution)/shard_map/ppermute | solution.py:171
  9.8 1.6 %collective-permute-start.3 = (bf16[64,1792]{1,0:T(8,128)(2,1)S(1)}, bf16[64,1792]{1,0:T(8,128)(2,1)S(1)}, u32[]{:S(2)}, u32[]{:S(2)}) collective-permute-start(bf16[64,1792]{1,0:T(8,128)(2,1)S(1)} %get-tuple-element.32.refs_6_), channel_id=1, source_target_pairs={{0,4},{1,5},{2,6},{3,7},{4,0},{5,1},{6,2},{7,3},{8,12},{9,13},{10,... | collective-permute-start | bytes 688136 | tf_op jit(solution)/shard_map/ppermute | solution.py:171
  11.4 7.2 %collective-permute-done.2.refs_6_ = bf16[64,1280]{1,0:T(8,128)(2,1)S(1)} collective-permute-done((bf16[64,1280]{1,0:T(8,128)(2,1)S(1)}, bf16[64,1280]{1,0:T(8,128)(2,1)S(1)}, u32[]{:S(2)}, u32[]{:S(2)}) %collective-permute-start.2) | collective-permute-done | bytes 163872 | tf_op jit(solution)/shard_map/ppermute | solution.py:171
  18.6 1.5 %collective-permute-start.7 = (bf16[128,1408]{1,0:T(8,128)(2,1)S(1)}, bf16[128,1408]{1,0:T(8,128)(2,1)S(1)}, u32[]{:S(2)}, u32[]{:S(2)}) collective-permute-start(bf16[128,1408]{1,0:T(8,128)(2,1)S(1)} %get-tuple-element.34), channel_id=1, source_target_pairs={{0,18},{1,19},{2,16},{3,17},{4,22},{5,23},{6,20},{7,21},{8,26},{9,... | collective-permute-start | bytes 1081352 | tf_op jit(solution)/shard_map/ppermute | solution.py:182
  20.1 0.0 collective-permute-done.1.refs_8_
  20.1 0.0 collective-permute-done.3.refs_7_
  20.1 0.0 collective-permute-done.refs_1_
  20.1 0.0 collective-permute-done.4.refs_2_
  20.1 0.7 %collective-permute-start.6 = (bf16[64,1792]{1,0:T(8,128)(2,1)S(1)}, bf16[64,1792]{1,0:T(8,128)(2,1)S(1)}, u32[]{:S(2)}, u32[]{:S(2)}) collective-permute-start(bf16[64,1792]{1,0:T(8,128)(2,1)S(1)} %get-tuple-element.32.refs_6_), channel_id=1, source_target_pairs={{4,8},{5,9},{6,10},{7,11},{8,4},{9,5},{10,6},{11,7},{20,24},{21,25... | collective-permute-start | bytes 688136 | tf_op jit(solution)/shard_map/ppermute | solution.py:174
  20.8 1.3 %collective-permute-start.5 = (bf16[64,1792]{1,0:T(8,128)(2,1)S(1)}, bf16[64,1792]{1,0:T(8,128)(2,1)S(1)}, u32[]{:S(2)}, u32[]{:S(2)}) collective-permute-start(bf16[64,1792]{1,0:T(8,128)(2,1)S(1)} %collective-permute-done.1.refs_8_), channel_id=1, source_target_pairs={{4,0},{5,1},{6,2},{7,3},{8,12},{9,13},{10,14},{11,15},{20,16},{21,... | collective-permute-start | bytes 688136 | tf_op jit(solution)/shard_map/ppermute | solution.py:174
  22.1 6.4 %collective-permute-done.7.refs_3_ = bf16[128,1408]{1,0:T(8,128)(2,1)S(1)} collective-permute-done((bf16[128,1408]{1,0:T(8,128)(2,1)S(1)}, bf16[128,1408]{1,0:T(8,128)(2,1)S(1)}, u32[]{:S(2)}, u32[]{:S(2)}) %collective-permute-start.7) | collective-permute-done | bytes 360480 | tf_op jit(solution)/shard_map/ppermute | solution.py:182
  28.5 0.0 collective-permute-done.6.refs_9_
  28.5 2.0 %collective-permute-done.5.refs_10_ = bf16[64,1792]{1,0:T(8,128)(2,1)S(1)} collective-permute-done((bf16[64,1792]{1,0:T(8,128)(2,1)S(1)}, bf16[64,1792]{1,0:T(8,128)(2,1)S(1)}, u32[]{:S(2)}, u32[]{:S(2)}) %collective-permute-start.5) | collective-permute-done | bytes 229408 | tf_op jit(solution)/shard_map/ppermute | solution.py:174
  30.4 0.1 pad_maximum_fusion.1
  30.5 0.1 collective-permute-start.9
  30.6 0.0 copy-start
  30.6 0.1 pad_maximum_fusion
  30.7 0.5 collective-permute-start.8
  31.3 1.6 %collective-permute-start.16 = (bf16[256,512]{1,0:T(8,128)(2,1)S(1)}, bf16[256,512]{1,0:T(8,128)(2,1)S(1)}, u32[]{:S(2)}, u32[]{:S(2)}) collective-permute-start(bf16[256,512]{1,0:T(8,128)(2,1)S(1)} %pad_maximum_fusion.2.refs_0_), channel_id=1, source_target_pairs={{0,16},{1,17},{2,18},{3,19},{4,20},{5,21},{6,22},{7,23},{8,24},{9,... | collective-permute-start | bytes 786440 | tf_op jit(solution)/shard_map/ppermute | solution.py:182
  32.8 0.0 collective-permute-start.10
  32.8 2.4 %collective-permute-start.11 = (bf16[64,1280]{1,0:T(8,128)(2,1)S(1)}, bf16[64,1280]{1,0:T(8,128)(2,1)S(1)}, u32[]{:S(2)}, u32[]{:S(2)}) collective-permute-start(bf16[64,1280]{1,0:T(8,128)(2,1)S(1)} %collective-permute-done.2.refs_6_), channel_id=1, source_target_pairs={{0,8},{1,9},{2,10},{3,11},{4,12},{5,13},{6,14},{7,15},{8,0},{9,1},... | collective-permute-start | bytes 491528 | tf_op jit(solution)/shard_map/ppermute | solution.py:171
  35.3 0.0 collective-permute-done.9.refs_5_
  35.3 2.0 %collective-permute-start.12 = (bf16[64,1280]{1,0:T(8,128)(2,1)S(1)}, bf16[64,1280]{1,0:T(8,128)(2,1)S(1)}, u32[]{:S(2)}, u32[]{:S(2)}) collective-permute-start(bf16[64,1280]{1,0:T(8,128)(2,1)S(1)} %collective-permute-done.2.refs_6_), channel_id=1, source_target_pairs={{0,12},{1,13},{2,14},{3,15},{4,8},{5,9},{6,10},{7,11},{8,4},{9,5},... | collective-permute-start | bytes 491528 | tf_op jit(solution)/shard_map/ppermute | solution.py:171
  37.2 0.0 collective-permute-done.8.refs_4_.theirs
  37.2 0.5 collective-permute-start.17
  37.7 1.4 %shard_map.74.refs_10_ = f32[8,128,128]{2,1,0:T(8,128)S(1)} custom-call(s32[4]{0:T(128)S(1)} %pad_add_fusion.place, bf16[128,1408]{1,0:T(8,128)(2,1)S(1)} %get-tuple-element.35.refs_0_.mine, bf16[128,1408]{1,0:T(8,128)(2,1)S(1)} %collective-permute-done.refs_1_, bf16[128,1408]{1,0:T(8,128)(2,1)S(1)} %collective-permute-done.4.refs_2_, ...), custom_call_target="tpu_custom_call" | custom-call | flops 671088640 | bytes 4030480 | tf_op jit(solution)/shard_map/pallas_call | solution.py:28
  39.2 2.1 %collective-permute-done.10.refs_7_ = bf16[64,1280]{1,0:T(8,128)(2,1)S(1)} collective-permute-done((bf16[64,1280]{1,0:T(8,128)(2,1)S(1)}, bf16[64,1280]{1,0:T(8,128)(2,1)S(1)}, u32[]{:S(2)}, u32[]{:S(2)}) %collective-permute-start.10) | collective-permute-done | bytes 163872 | tf_op jit(solution)/shard_map/ppermute | solution.py:171
  41.2 0.6 %collective-permute-start.18 = (bf16[256,512]{1,0:T(8,128)(2,1)S(1)}, bf16[256,512]{1,0:T(8,128)(2,1)S(1)}, u32[]{:S(2)}, u32[]{:S(2)}) collective-permute-start(bf16[256,512]{1,0:T(8,128)(2,1)S(1)} %pad_maximum_fusion.2.refs_0_), channel_id=1, source_target_pairs={{0,18},{1,19},{2,16},{3,17},{4,22},{5,23},{6,20},{7,21},{8,26},{9,... | collective-permute-start | bytes 786440 | tf_op jit(solution)/shard_map/ppermute | solution.py:182
  41.9 6.0 %collective-permute-done.11.refs_8_ = bf16[64,1280]{1,0:T(8,128)(2,1)S(1)} collective-permute-done((bf16[64,1280]{1,0:T(8,128)(2,1)S(1)}, bf16[64,1280]{1,0:T(8,128)(2,1)S(1)}, u32[]{:S(2)}, u32[]{:S(2)}) %collective-permute-start.11) | collective-permute-done | bytes 163872 | tf_op jit(solution)/shard_map/ppermute | solution.py:171
  47.9 0.0 collective-permute-done.12.refs_9_
  47.9 1.4 %shard_map.75 = (f32[2,128,128]{2,1,0:T(8,128)S(1)}, f32[2,128,128]{2,1,0:T(8,128)S(1)}, f32[2,128,128]{2,1,0:T(8,128)S(1)}, f32[2,128,128]{2,1,0:T(8,128)S(1)}) custom-call(s32[4]{0:T(128)S(1)} %pad_add_fusion.place, bf16[128,1408]{1,0:T(8,128)(2,1)S(1)} %get-tuple-element.35.refs_0_.mine, bf16[128,1408]{1,0:T(8,128)(2,1)S(1)} %collective-permute-done.refs_1_, ...), custom_call_target="tpu_custom_call" | custom-call | flops 671088640 | bytes 4063248 | tf_op jit(solution)/shard_map/pallas_call | solution.py:28
  49.3 0.9 %collective-permute-start.13 = (f32[2,128,128]{2,1,0:T(8,128)S(1)}, f32[2,128,128]{2,1,0:T(8,128)S(1)}, u32[]{:S(2)}, u32[]{:S(2)}) collective-permute-start(f32[2,128,128]{2,1,0:T(8,128)S(1)} %get-tuple-element.41), channel_id=1, source_target_pairs={{0,16},{1,17},{2,18},{3,19},{4,20},{5,21},{6,22},{7,23},{8,24},{9,... | collective-permute-start | bytes 393224 | tf_op jit(solution)/shard_map/ppermute | solution.py:182
  50.3 1.5 %collective-permute-start.14 = (f32[2,128,128]{2,1,0:T(8,128)S(1)}, f32[2,128,128]{2,1,0:T(8,128)S(1)}, u32[]{:S(2)}, u32[]{:S(2)}) collective-permute-start(f32[2,128,128]{2,1,0:T(8,128)S(1)} %get-tuple-element.42), channel_id=1, source_target_pairs={{0,2},{1,3},{2,0},{3,1},{4,6},{5,7},{6,4},{7,5},{8,10},{9,11},{10,... | collective-permute-start | bytes 393224 | tf_op jit(solution)/shard_map/ppermute | solution.py:171
  51.8 0.0 collective-permute-done.16.refs_1_
  51.8 1.1 %collective-permute-start.15 = (f32[2,128,128]{2,1,0:T(8,128)S(1)}, f32[2,128,128]{2,1,0:T(8,128)S(1)}, u32[]{:S(2)}, u32[]{:S(2)}) collective-permute-start(f32[2,128,128]{2,1,0:T(8,128)S(1)} %get-tuple-element.43), channel_id=1, source_target_pairs={{0,18},{1,19},{2,16},{3,17},{4,22},{5,23},{6,20},{7,21},{8,26},{9,... | collective-permute-start | bytes 393224 | tf_op jit(solution)/shard_map/ppermute | solution.py:182
  52.9 0.0 copy-done
  52.9 2.9 %fusion.base = f32[128,1024]{1,0:T(8,128)S(1)} fusion(bf16[128,5120]{1,0:T(8,128)(2,1)} %hidden.1, bf16[5120,1024]{1,0:T(8,128)(2,1)S(1)} %copy-done), kind=kOutput, calls=%fused_computation.5 | convolution fusion | flops 1342177280 | bytes 12320768 | tf_op jit(solution)/shard_map/dot_general | solution.py:255
  55.8 0.0 collective-permute-done.17.refs_2_
  55.8 0.0 collective-permute-done.18.refs_3_
  55.8 0.0 collective-permute-done.13.z_x
  55.8 0.0 collective-permute-done.14.z_y
  55.8 1.8 %collective-permute-done.15.z_d = f32[2,128,128]{2,1,0:T(8,128)S(1)} collective-permute-done((f32[2,128,128]{2,1,0:T(8,128)S(1)}, f32[2,128,128]{2,1,0:T(8,128)S(1)}, u32[]{:S(2)}, u32[]{:S(2)}) %collective-permute-start.15) | collective-permute-done | bytes 131104 | tf_op jit(solution)/shard_map/ppermute | solution.py:182
  57.6 1.1 %shard_map.76 = (f32[128,1024]{1,0:T(8,128)S(1)}, f32[128,1024]{1,0:T(8,128)S(1)}) custom-call(s32[4]{0:T(128)S(1)} %pad_add_fusion.place, f32[128,1024]{1,0:T(8,128)S(1)} %fusion.base, bf16[128,1408]{1,0:T(8,128)(2,1)S(1)} %get-tuple-element.35.refs_0_.mine, bf16[256,1408]{1,0:T(8,128)(2,1)S(1)} %collective-permute-done.8.refs_4_.theirs, ...), custom_call_target="tpu_custom_call" | custom-call | flops 268435456 | bytes 3178512 | tf_op jit(solution)/shard_map/pallas_call | solution.py:28
  58.8 0.1 collective-permute-start.19
  58.8 1.9 %collective-permute-done.19.came = f32[128,1024]{1,0:T(8,128)S(1)} collective-permute-done((f32[128,1024]{1,0:T(8,128)S(1)}, f32[128,1024]{1,0:T(8,128)S(1)}, u32[]{:S(2)}, u32[]{:S(2)}) %collective-permute-start.19) | collective-permute-done | bytes 524320 | tf_op jit(solution)/shard_map/ppermute | solution.py:171
  60.7 0.8 %shard_map.77 = bf16[128,1024]{1,0:T(8,128)(2,1)} custom-call(f32[128,1024]{1,0:T(8,128)S(1)} %get-tuple-element.45.here, f32[128,1024]{1,0:T(8,128)S(1)} %collective-permute-done.19.came), custom_call_target="tpu_custom_call" | custom-call | flops 131072 | bytes 1048576 | tf_op jit(solution)/shard_map/pallas_call | solution.py:28
  (5 shorter events, 0.0 us)
Async XLA Ops:
  2.2 17.9 %collective-permute-start = (bf16[128,1408]{1,0:T(8,128)(2,1)S(1)}, bf16[128,1408]{1,0:T(8,128)(2,1)S(1)}, u32[]{:S(2)}, u32[]{:S(2)}) collective-permute-start(bf16[128,1408]{1,0:T(8,128)(2,1)S(1)} %get-tuple-element.27), channel_id=1, source_target_pairs={{0,16},{1,17},{2,18},{3,19},{4,20},{5,21},{6,22},{7,23},{8,24},{9,... | collective-permute-start | bytes 1081352 | tf_op jit(solution)/shard_map/ppermute | solution.py:182
  5.2 14.9 %collective-permute-start.4 = (bf16[128,1408]{1,0:T(8,128)(2,1)S(1)}, bf16[128,1408]{1,0:T(8,128)(2,1)S(1)}, u32[]{:S(2)}, u32[]{:S(2)}) collective-permute-start(bf16[128,1408]{1,0:T(8,128)(2,1)S(1)} %get-tuple-element.30), channel_id=1, source_target_pairs={{0,2},{1,3},{2,0},{3,1},{4,6},{5,7},{6,4},{7,5},{8,10},{9,11},{10,... | collective-permute-start | bytes 1081352 | tf_op jit(solution)/shard_map/ppermute | solution.py:171
  6.7 11.9 %collective-permute-start.2 = (bf16[64,1280]{1,0:T(8,128)(2,1)S(1)}, bf16[64,1280]{1,0:T(8,128)(2,1)S(1)}, u32[]{:S(2)}, u32[]{:S(2)}) collective-permute-start(bf16[64,1280]{1,0:T(8,128)(2,1)S(1)} %get-tuple-element.29), channel_id=1, source_target_pairs={{0,2},{1,3},{2,0},{3,1},{4,6},{5,7},{6,4},{7,5},{8,10},{9,11},{10,... | collective-permute-start | bytes 491528 | tf_op jit(solution)/shard_map/ppermute | solution.py:171
  7.2 12.9 %collective-permute-start.1 = (bf16[64,1792]{1,0:T(8,128)(2,1)S(1)}, bf16[64,1792]{1,0:T(8,128)(2,1)S(1)}, u32[]{:S(2)}, u32[]{:S(2)}) collective-permute-start(bf16[64,1792]{1,0:T(8,128)(2,1)S(1)} %get-tuple-element.32.refs_6_), channel_id=1, source_target_pairs={{0,8},{1,9},{2,10},{3,11},{4,12},{5,13},{6,14},{7,15},{8,0},{9,1},... | collective-permute-start | bytes 688136 | tf_op jit(solution)/shard_map/ppermute | solution.py:171
  9.8 10.3 %collective-permute-start.3 = (bf16[64,1792]{1,0:T(8,128)(2,1)S(1)}, bf16[64,1792]{1,0:T(8,128)(2,1)S(1)}, u32[]{:S(2)}, u32[]{:S(2)}) collective-permute-start(bf16[64,1792]{1,0:T(8,128)(2,1)S(1)} %get-tuple-element.32.refs_6_), channel_id=1, source_target_pairs={{0,4},{1,5},{2,6},{3,7},{4,0},{5,1},{6,2},{7,3},{8,12},{9,13},{10,... | collective-permute-start | bytes 688136 | tf_op jit(solution)/shard_map/ppermute | solution.py:171
  18.6 9.9 %collective-permute-start.7 = (bf16[128,1408]{1,0:T(8,128)(2,1)S(1)}, bf16[128,1408]{1,0:T(8,128)(2,1)S(1)}, u32[]{:S(2)}, u32[]{:S(2)}) collective-permute-start(bf16[128,1408]{1,0:T(8,128)(2,1)S(1)} %get-tuple-element.34), channel_id=1, source_target_pairs={{0,18},{1,19},{2,16},{3,17},{4,22},{5,23},{6,20},{7,21},{8,26},{9,... | collective-permute-start | bytes 1081352 | tf_op jit(solution)/shard_map/ppermute | solution.py:182
  20.1 8.4 %collective-permute-start.6 = (bf16[64,1792]{1,0:T(8,128)(2,1)S(1)}, bf16[64,1792]{1,0:T(8,128)(2,1)S(1)}, u32[]{:S(2)}, u32[]{:S(2)}) collective-permute-start(bf16[64,1792]{1,0:T(8,128)(2,1)S(1)} %get-tuple-element.32.refs_6_), channel_id=1, source_target_pairs={{4,8},{5,9},{6,10},{7,11},{8,4},{9,5},{10,6},{11,7},{20,24},{21,25... | collective-permute-start | bytes 688136 | tf_op jit(solution)/shard_map/ppermute | solution.py:174
  20.8 9.7 %collective-permute-start.5 = (bf16[64,1792]{1,0:T(8,128)(2,1)S(1)}, bf16[64,1792]{1,0:T(8,128)(2,1)S(1)}, u32[]{:S(2)}, u32[]{:S(2)}) collective-permute-start(bf16[64,1792]{1,0:T(8,128)(2,1)S(1)} %collective-permute-done.1.refs_8_), channel_id=1, source_target_pairs={{4,0},{5,1},{6,2},{7,3},{8,12},{9,13},{10,14},{11,15},{20,16},{21,... | collective-permute-start | bytes 688136 | tf_op jit(solution)/shard_map/ppermute | solution.py:174
  30.5 4.8 %collective-permute-start.9 = (bf16[256,1408]{1,0:T(8,128)(2,1)S(1)}, bf16[256,1408]{1,0:T(8,128)(2,1)S(1)}, u32[]{:S(2)}, u32[]{:S(2)}) collective-permute-start(bf16[256,1408]{1,0:T(8,128)(2,1)S(1)} %pad_maximum_fusion.1), channel_id=1, source_target_pairs={{0,1},{1,0},{2,3},{3,2},{4,5},{5,4},{6,7},{7,6},{8,9},{9,8},{10,11... | collective-permute-start | bytes 2162696 | tf_op jit(solution)/shard_map/ppermute | solution.py:171
  30.6 22.3 %copy-start = (bf16[5120,1024]{1,0:T(8,128)(2,1)S(1)}, bf16[5120,1024]{1,0:T(8,128)(2,1)}, u32[]{:S(2)}) copy-start(bf16[5120,1024]{1,0:T(8,128)(2,1)} %param.8) | copy-start | bytes 31457284
  30.7 6.6 %collective-permute-start.8 = (bf16[256,1408]{1,0:T(8,128)(2,1)S(1)}, bf16[256,1408]{1,0:T(8,128)(2,1)S(1)}, u32[]{:S(2)}, u32[]{:S(2)}) collective-permute-start(bf16[256,1408]{1,0:T(8,128)(2,1)S(1)} %pad_maximum_fusion), channel_id=1, source_target_pairs={{0,1},{1,0},{2,3},{3,2},{4,5},{5,4},{6,7},{7,6},{8,9},{9,8},{10,11... | collective-permute-start | bytes 2162696 | tf_op jit(solution)/shard_map/ppermute | solution.py:171
  31.3 20.5 %collective-permute-start.16 = (bf16[256,512]{1,0:T(8,128)(2,1)S(1)}, bf16[256,512]{1,0:T(8,128)(2,1)S(1)}, u32[]{:S(2)}, u32[]{:S(2)}) collective-permute-start(bf16[256,512]{1,0:T(8,128)(2,1)S(1)} %pad_maximum_fusion.2.refs_0_), channel_id=1, source_target_pairs={{0,16},{1,17},{2,18},{3,19},{4,20},{5,21},{6,22},{7,23},{8,24},{9,... | collective-permute-start | bytes 786440 | tf_op jit(solution)/shard_map/ppermute | solution.py:182
  32.8 8.4 %collective-permute-start.10 = (bf16[64,1280]{1,0:T(8,128)(2,1)S(1)}, bf16[64,1280]{1,0:T(8,128)(2,1)S(1)}, u32[]{:S(2)}, u32[]{:S(2)}) collective-permute-start(bf16[64,1280]{1,0:T(8,128)(2,1)S(1)} %collective-permute-done.2.refs_6_), channel_id=1, source_target_pairs={{0,4},{1,5},{2,6},{3,7},{4,0},{5,1},{6,2},{7,3},{8,12},{9,13},{10,... | collective-permute-start | bytes 491528 | tf_op jit(solution)/shard_map/ppermute | solution.py:171
  32.8 15.0 %collective-permute-start.11 = (bf16[64,1280]{1,0:T(8,128)(2,1)S(1)}, bf16[64,1280]{1,0:T(8,128)(2,1)S(1)}, u32[]{:S(2)}, u32[]{:S(2)}) collective-permute-start(bf16[64,1280]{1,0:T(8,128)(2,1)S(1)} %collective-permute-done.2.refs_6_), channel_id=1, source_target_pairs={{0,8},{1,9},{2,10},{3,11},{4,12},{5,13},{6,14},{7,15},{8,0},{9,1},... | collective-permute-start | bytes 491528 | tf_op jit(solution)/shard_map/ppermute | solution.py:171
  35.3 12.6 %collective-permute-start.12 = (bf16[64,1280]{1,0:T(8,128)(2,1)S(1)}, bf16[64,1280]{1,0:T(8,128)(2,1)S(1)}, u32[]{:S(2)}, u32[]{:S(2)}) collective-permute-start(bf16[64,1280]{1,0:T(8,128)(2,1)S(1)} %collective-permute-done.2.refs_6_), channel_id=1, source_target_pairs={{0,12},{1,13},{2,14},{3,15},{4,8},{5,9},{6,10},{7,11},{8,4},{9,5},... | collective-permute-start | bytes 491528 | tf_op jit(solution)/shard_map/ppermute | solution.py:171
  37.2 18.5 %collective-permute-start.17 = (bf16[256,512]{1,0:T(8,128)(2,1)S(1)}, bf16[256,512]{1,0:T(8,128)(2,1)S(1)}, u32[]{:S(2)}, u32[]{:S(2)}) collective-permute-start(bf16[256,512]{1,0:T(8,128)(2,1)S(1)} %pad_maximum_fusion.2.refs_0_), channel_id=1, source_target_pairs={{0,2},{1,3},{2,0},{3,1},{4,6},{5,7},{6,4},{7,5},{8,10},{9,11},{10,... | collective-permute-start | bytes 786440 | tf_op jit(solution)/shard_map/ppermute | solution.py:171
  41.2 14.6 %collective-permute-start.18 = (bf16[256,512]{1,0:T(8,128)(2,1)S(1)}, bf16[256,512]{1,0:T(8,128)(2,1)S(1)}, u32[]{:S(2)}, u32[]{:S(2)}) collective-permute-start(bf16[256,512]{1,0:T(8,128)(2,1)S(1)} %pad_maximum_fusion.2.refs_0_), channel_id=1, source_target_pairs={{0,18},{1,19},{2,16},{3,17},{4,22},{5,23},{6,20},{7,21},{8,26},{9,... | collective-permute-start | bytes 786440 | tf_op jit(solution)/shard_map/ppermute | solution.py:182
  49.3 6.5 %collective-permute-start.13 = (f32[2,128,128]{2,1,0:T(8,128)S(1)}, f32[2,128,128]{2,1,0:T(8,128)S(1)}, u32[]{:S(2)}, u32[]{:S(2)}) collective-permute-start(f32[2,128,128]{2,1,0:T(8,128)S(1)} %get-tuple-element.41), channel_id=1, source_target_pairs={{0,16},{1,17},{2,18},{3,19},{4,20},{5,21},{6,22},{7,23},{8,24},{9,... | collective-permute-start | bytes 393224 | tf_op jit(solution)/shard_map/ppermute | solution.py:182
  50.3 5.6 %collective-permute-start.14 = (f32[2,128,128]{2,1,0:T(8,128)S(1)}, f32[2,128,128]{2,1,0:T(8,128)S(1)}, u32[]{:S(2)}, u32[]{:S(2)}) collective-permute-start(f32[2,128,128]{2,1,0:T(8,128)S(1)} %get-tuple-element.42), channel_id=1, source_target_pairs={{0,2},{1,3},{2,0},{3,1},{4,6},{5,7},{6,4},{7,5},{8,10},{9,11},{10,... | collective-permute-start | bytes 393224 | tf_op jit(solution)/shard_map/ppermute | solution.py:171
  51.8 5.9 %collective-permute-start.15 = (f32[2,128,128]{2,1,0:T(8,128)S(1)}, f32[2,128,128]{2,1,0:T(8,128)S(1)}, u32[]{:S(2)}, u32[]{:S(2)}) collective-permute-start(f32[2,128,128]{2,1,0:T(8,128)S(1)} %get-tuple-element.43), channel_id=1, source_target_pairs={{0,18},{1,19},{2,16},{3,17},{4,22},{5,23},{6,20},{7,21},{8,26},{9,... | collective-permute-start | bytes 393224 | tf_op jit(solution)/shard_map/ppermute | solution.py:182
  58.8 2.0 %collective-permute-start.19 = (f32[128,1024]{1,0:T(8,128)S(1)}, f32[128,1024]{1,0:T(8,128)S(1)}, u32[]{:S(2)}, u32[]{:S(2)}) collective-permute-start(f32[128,1024]{1,0:T(8,128)S(1)} %get-tuple-element.46), channel_id=1, source_target_pairs={{0,1},{1,0},{2,3},{3,2},{4,5},{5,4},{6,7},{7,6},{8,9},{9,8},{10,11... | collective-permute-start | bytes 1572872 | tf_op jit(solution)/shard_map/ppermute | solution.py:171

commit v5 on v4

--- a/solution.py
+++ b/solution.py
@@ -8,11 +8,16 @@
 from jax.sharding import PartitionSpec as P
 
 TAG = 128
-FIRST = ("P", "X", "A2", "A1", "Y")
-SECOND = ("A4", "A3", "D")
-ORDER = {"D": ("P",)}
-ORDER |= dict.fromkeys(("A3", "A4", "B1", "B2", "B3"), FIRST)
-ORDER |= dict.fromkeys(("U", "C1", "C2"), SECOND)
+ORDER = {
+    "Y": ("A1",),
+    "A3": ("A1", "P"),
+    "D": ("X", "P"),
+    "B1": ("A3",),
+    "B3": ("A3",),
+    "U": ("A3", "D"),
+    "C1": ("A3", "A4", "B2", "D"),
+    "C2": ("A3", "A4", "B2", "D"),
+}
 VMEM = pl.BlockSpec(memory_space=pltpu.VMEM)
 SMEM = pl.BlockSpec(memory_space=pltpu.SMEM)
 HBM = pl.BlockSpec(memory_space=pltpu.HBM)

time: 62.1 us -> 60.2 us (0.969)
  waiting for transfers between devices: 27.4 us -> 19.2 us
  starting transfers between devices: 24 us -> 28 us
  matrix products: 2.9 us -> 5.61 us
    ppermute x6, waiting for transfers between devices: 8.18 us -> 0.02 us  [across(): return lax.ppermute(value, ('replica', 'owner'), pairs)]
    ppermute x12, starting transfers between devices: 13.3 us -> 18.8 us  [by_owner(): return lax.ppermute(value, 'owner', [(i, i ^ flip) for i in range(owners)])]
    dot_general x1, matrix products: 2.9 us -> 5.61 us  [body(): jnp.dot(*late(hidden), base_weight, preferred_element_type=f32)]
    ppermute x12, waiting for transfers between devices: 17.2 us -> 19.2 us  [by_owner(): return lax.ppermute(value, 'owner', [(i, i ^ flip) for i in range(owners)])]
    ppermute x2, waiting for transfers between devices: 1.99 us -> 0.01 us  [between(): lax.ppermute(value, 'owner', [(a * 4 + i, b * 4 + i) for a, b in pairs fo...]
    ppermute x6, starting transfers between devices: 8.73 us -> 7.25 us  [across(): return lax.ppermute(value, ('replica', 'owner'), pairs)]
  transfers between devices with their start and end apart: 20 -> 20, of which waited for: 7 -> 7; matrix products, arithmetic and copies ran while one was open for 5% -> 10% of each run, Pallas kernels for 5% -> 5%
where the time goes in v5:
time: 60.2 us; the launch traced here: 60 us
  starting transfers between devices  28 us (47%)
  waiting for transfers between devices  19.2 us (32%)
  Pallas kernels  6.85 us (11%)
  matrix products  5.61 us (9%)
    ppermute x12, waiting for transfers between devices, by_owner(): return lax.ppermute(value, 'owner', [(i, i ^ flip) for i in range(owners)])  19.2 us
    ppermute x12, starting transfers between devices, by_owner(): return lax.ppermute(value, 'owner', [(i, i ^ flip) for i in range(owners)])  18.8 us
    ppermute x6, starting transfers between devices, across(): return lax.ppermute(value, ('replica', 'owner'), pairs)  7.25 us
    pallas_call x5, Pallas kernels, call(): pl.pallas_call(kernel, out_shape=out, in_specs=[SMEM] * scalars + [VMEM]...  6.85 us
    dot_general x1, matrix products, body(): jnp.dot(*late(hidden), base_weight, preferred_element_type=f32)  5.61 us
    ppermute x2, starting transfers between devices, between(): lax.ppermute(value, 'owner', [(a * 4 + i, b * 4 + i) for a, b in pairs fo...  1.94 us
  transfers between devices with their start and end apart: 20, of which 7 were waited for; matrix products, arithmetic and copies ran while one was open for 10% of the time, Pallas kernels for 5%

profile of v5, /device:TPU:0, one launch (start us, length us, event | category | flops | bytes accessed | tf_op | source)
XLA Modules:
  0.0 60.0 jit_solution(14701963546835707424)
XLA Ops:
  0.0 0.1 pad_add_fusion.place
  0.1 2.1 %shard_map.73 = (bf16[64,1280]{1,0:T(8,128)(2,1)S(1)}, bf16[64,1792]{1,0:T(8,128)(2,1)S(1)}, bf16[128,1408]{1,0:T(8,128)(2,1)S(1)}, bf16[128,1408]{1,0:T(8,128)(...) custom-call(s32[4]{0:T(128)S(1)} %pad_add_fusion.place, bf16[1,64,5120]{2,1,0:T(8,128)(2,1)} %down.1, ...), custom_call_target="tpu_custom_call" | custom-call | bytes 2097760 | tf_op jit(solution)/shard_map/pallas_call | solution.py:33
  2.2 3.0 %collective-permute-start = (bf16[128,1408]{1,0:T(8,128)(2,1)S(1)}, bf16[128,1408]{1,0:T(8,128)(2,1)S(1)}, u32[]{:S(2)}, u32[]{:S(2)}) collective-permute-start(bf16[128,1408]{1,0:T(8,128)(2,1)S(1)} %get-tuple-element.27), channel_id=1, source_target_pairs={{0,16},{1,17},{2,18},{3,19},{4,20},{5,21},{6,22},{7,23},{8,24},{9,... | collective-permute-start | bytes 1081352 | tf_op jit(solution)/shard_map/ppermute | solution.py:187
  5.2 1.6 %collective-permute-start.1 = (bf16[64,1792]{1,0:T(8,128)(2,1)S(1)}, bf16[64,1792]{1,0:T(8,128)(2,1)S(1)}, u32[]{:S(2)}, u32[]{:S(2)}) collective-permute-start(bf16[64,1792]{1,0:T(8,128)(2,1)S(1)} %get-tuple-element.30.refs_6_), channel_id=1, source_target_pairs={{0,4},{1,5},{2,6},{3,7},{4,0},{5,1},{6,2},{7,3},{8,12},{9,13},{10,... | collective-permute-start | bytes 688136 | tf_op jit(solution)/shard_map/ppermute | solution.py:176
  6.8 1.5 %collective-permute-start.2 = (bf16[64,1280]{1,0:T(8,128)(2,1)S(1)}, bf16[64,1280]{1,0:T(8,128)(2,1)S(1)}, u32[]{:S(2)}, u32[]{:S(2)}) collective-permute-start(bf16[64,1280]{1,0:T(8,128)(2,1)S(1)} %get-tuple-element.29), channel_id=1, source_target_pairs={{0,2},{1,3},{2,0},{3,1},{4,6},{5,7},{6,4},{7,5},{8,10},{9,11},{10,... | collective-permute-start | bytes 491528 | tf_op jit(solution)/shard_map/ppermute | solution.py:176
  8.3 2.6 %collective-permute-start.4 = (bf16[64,1792]{1,0:T(8,128)(2,1)S(1)}, bf16[64,1792]{1,0:T(8,128)(2,1)S(1)}, u32[]{:S(2)}, u32[]{:S(2)}) collective-permute-start(bf16[64,1792]{1,0:T(8,128)(2,1)S(1)} %get-tuple-element.30.refs_6_), channel_id=1, source_target_pairs={{0,8},{1,9},{2,10},{3,11},{4,12},{5,13},{6,14},{7,15},{8,0},{9,1},... | collective-permute-start | bytes 688136 | tf_op jit(solution)/shard_map/ppermute | solution.py:176
  10.9 4.8 %collective-permute-done.1.refs_7_ = bf16[64,1792]{1,0:T(8,128)(2,1)S(1)} collective-permute-done((bf16[64,1792]{1,0:T(8,128)(2,1)S(1)}, bf16[64,1792]{1,0:T(8,128)(2,1)S(1)}, u32[]{:S(2)}, u32[]{:S(2)}) %collective-permute-start.1) | collective-permute-done | bytes 229408 | tf_op jit(solution)/shard_map/ppermute | solution.py:176
  15.7 2.7 %collective-permute-start.9 = (bf16[128,1408]{1,0:T(8,128)(2,1)S(1)}, bf16[128,1408]{1,0:T(8,128)(2,1)S(1)}, u32[]{:S(2)}, u32[]{:S(2)}) collective-permute-start(bf16[128,1408]{1,0:T(8,128)(2,1)S(1)} %get-tuple-element.36), channel_id=1, source_target_pairs={{0,2},{1,3},{2,0},{3,1},{4,6},{5,7},{6,4},{7,5},{8,10},{9,11},{10,... | collective-permute-start | bytes 1081352 | tf_op jit(solution)/shard_map/ppermute | solution.py:176
  18.4 0.0 collective-permute-done.2.refs_6_
  18.4 0.0 collective-permute-done.refs_1_
  18.4 0.0 collective-permute-start.7
  18.4 0.7 %collective-permute-start.3 = (bf16[64,1792]{1,0:T(8,128)(2,1)S(1)}, bf16[64,1792]{1,0:T(8,128)(2,1)S(1)}, u32[]{:S(2)}, u32[]{:S(2)}) collective-permute-start(bf16[64,1792]{1,0:T(8,128)(2,1)S(1)} %get-tuple-element.30.refs_6_), channel_id=1, source_target_pairs={{4,8},{5,9},{6,10},{7,11},{8,4},{9,5},{10,6},{11,7},{20,24},{21,25... | collective-permute-start | bytes 688136 | tf_op jit(solution)/shard_map/ppermute | solution.py:179
  19.1 1.7 %collective-permute-done.4.refs_8_ = bf16[64,1792]{1,0:T(8,128)(2,1)S(1)} collective-permute-done((bf16[64,1792]{1,0:T(8,128)(2,1)S(1)}, bf16[64,1792]{1,0:T(8,128)(2,1)S(1)}, u32[]{:S(2)}, u32[]{:S(2)}) %collective-permute-start.4) | collective-permute-done | bytes 229408 | tf_op jit(solution)/shard_map/ppermute | solution.py:176
  20.8 1.3 %collective-permute-start.5 = (bf16[64,1792]{1,0:T(8,128)(2,1)S(1)}, bf16[64,1792]{1,0:T(8,128)(2,1)S(1)}, u32[]{:S(2)}, u32[]{:S(2)}) collective-permute-start(bf16[64,1792]{1,0:T(8,128)(2,1)S(1)} %collective-permute-done.4.refs_8_), channel_id=1, source_target_pairs={{4,0},{5,1},{6,2},{7,3},{8,12},{9,13},{10,14},{11,15},{20,16},{21,... | collective-permute-start | bytes 688136 | tf_op jit(solution)/shard_map/ppermute | solution.py:179
  22.1 3.7 %collective-permute-start.6 = (bf16[64,1280]{1,0:T(8,128)(2,1)S(1)}, bf16[64,1280]{1,0:T(8,128)(2,1)S(1)}, u32[]{:S(2)}, u32[]{:S(2)}) collective-permute-start(bf16[64,1280]{1,0:T(8,128)(2,1)S(1)} %collective-permute-done.2.refs_6_), channel_id=1, source_target_pairs={{0,8},{1,9},{2,10},{3,11},{4,12},{5,13},{6,14},{7,15},{8,0},{9,1},... | collective-permute-start | bytes 491528 | tf_op jit(solution)/shard_map/ppermute | solution.py:176
  25.8 6.8 %collective-permute-done.6.refs_8_ = bf16[64,1280]{1,0:T(8,128)(2,1)S(1)} collective-permute-done((bf16[64,1280]{1,0:T(8,128)(2,1)S(1)}, bf16[64,1280]{1,0:T(8,128)(2,1)S(1)}, u32[]{:S(2)}, u32[]{:S(2)}) %collective-permute-start.6) | collective-permute-done | bytes 163872 | tf_op jit(solution)/shard_map/ppermute | solution.py:176
  32.6 0.0 collective-permute-done.3.refs_9_
  32.6 0.0 collective-permute-done.5.refs_10_
  32.6 0.1 collective-permute-done.9.refs_2_
  32.7 0.0 collective-permute-done.7.refs_3_
  32.7 0.1 pad_maximum_fusion.1
  32.8 0.1 collective-permute-start.10
  32.9 0.1 pad_maximum_fusion
  32.9 0.6 collective-permute-start.8
  33.6 1.2 %collective-permute-start.16 = (bf16[256,512]{1,0:T(8,128)(2,1)S(1)}, bf16[256,512]{1,0:T(8,128)(2,1)S(1)}, u32[]{:S(2)}, u32[]{:S(2)}) collective-permute-start(bf16[256,512]{1,0:T(8,128)(2,1)S(1)} %pad_maximum_fusion.2.refs_0_), channel_id=1, source_target_pairs={{0,16},{1,17},{2,18},{3,19},{4,20},{5,21},{6,22},{7,23},{8,24},{9,... | collective-permute-start | bytes 786440 | tf_op jit(solution)/shard_map/ppermute | solution.py:187
  34.7 0.0 collective-permute-start.11
  34.7 2.5 %collective-permute-start.12 = (bf16[64,1280]{1,0:T(8,128)(2,1)S(1)}, bf16[64,1280]{1,0:T(8,128)(2,1)S(1)}, u32[]{:S(2)}, u32[]{:S(2)}) collective-permute-start(bf16[64,1280]{1,0:T(8,128)(2,1)S(1)} %collective-permute-done.2.refs_6_), channel_id=1, source_target_pairs={{0,12},{1,13},{2,14},{3,15},{4,8},{5,9},{6,10},{7,11},{8,4},{9,5},... | collective-permute-start | bytes 491528 | tf_op jit(solution)/shard_map/ppermute | solution.py:176
  37.2 0.0 collective-permute-done.10.refs_5_
  37.2 1.7 %collective-permute-start.17 = (bf16[256,512]{1,0:T(8,128)(2,1)S(1)}, bf16[256,512]{1,0:T(8,128)(2,1)S(1)}, u32[]{:S(2)}, u32[]{:S(2)}) collective-permute-start(bf16[256,512]{1,0:T(8,128)(2,1)S(1)} %pad_maximum_fusion.2.refs_0_), channel_id=1, source_target_pairs={{0,2},{1,3},{2,0},{3,1},{4,6},{5,7},{6,4},{7,5},{8,10},{9,11},{10,... | collective-permute-start | bytes 786440 | tf_op jit(solution)/shard_map/ppermute | solution.py:176
  39.0 0.0 collective-permute-done.8.refs_4_.theirs
  39.0 1.2 %collective-permute-start.18 = (bf16[256,512]{1,0:T(8,128)(2,1)S(1)}, bf16[256,512]{1,0:T(8,128)(2,1)S(1)}, u32[]{:S(2)}, u32[]{:S(2)}) collective-permute-start(bf16[256,512]{1,0:T(8,128)(2,1)S(1)} %pad_maximum_fusion.2.refs_0_), channel_id=1, source_target_pairs={{0,18},{1,19},{2,16},{3,17},{4,22},{5,23},{6,20},{7,21},{8,26},{9,... | collective-permute-start | bytes 786440 | tf_op jit(solution)/shard_map/ppermute | solution.py:187
  40.2 1.4 %shard_map.74.refs_10_ = f32[8,128,128]{2,1,0:T(8,128)S(1)} custom-call(s32[4]{0:T(128)S(1)} %pad_add_fusion.place, bf16[128,1408]{1,0:T(8,128)(2,1)S(1)} %get-tuple-element.33.refs_0_.mine, bf16[128,1408]{1,0:T(8,128)(2,1)S(1)} %collective-permute-done.refs_1_, bf16[128,1408]{1,0:T(8,128)(2,1)S(1)} %collective-permute-done.9.refs_2_, ...), custom_call_target="tpu_custom_call" | custom-call | flops 671088640 | bytes 4030480 | tf_op jit(solution)/shard_map/pallas_call | solution.py:33
  41.6 0.0 copy-start
  41.6 0.0 collective-permute-done.11.refs_7_
  41.7 3.3 %collective-permute-done.12.refs_9_ = bf16[64,1280]{1,0:T(8,128)(2,1)S(1)} collective-permute-done((bf16[64,1280]{1,0:T(8,128)(2,1)S(1)}, bf16[64,1280]{1,0:T(8,128)(2,1)S(1)}, u32[]{:S(2)}, u32[]{:S(2)}) %collective-permute-start.12) | collective-permute-done | bytes 163872 | tf_op jit(solution)/shard_map/ppermute | solution.py:176
  45.0 1.4 %shard_map.75 = (f32[2,128,128]{2,1,0:T(8,128)S(1)}, f32[2,128,128]{2,1,0:T(8,128)S(1)}, f32[2,128,128]{2,1,0:T(8,128)S(1)}, f32[2,128,128]{2,1,0:T(8,128)S(1)}) custom-call(s32[4]{0:T(128)S(1)} %pad_add_fusion.place, bf16[128,1408]{1,0:T(8,128)(2,1)S(1)} %get-tuple-element.33.refs_0_.mine, bf16[128,1408]{1,0:T(8,128)(2,1)S(1)} %collective-permute-done.refs_1_, ...), custom_call_target="tpu_custom_call" | custom-call | flops 671088640 | bytes 4063248 | tf_op jit(solution)/shard_map/pallas_call | solution.py:33
  46.4 1.6 %collective-permute-start.13 = (f32[2,128,128]{2,1,0:T(8,128)S(1)}, f32[2,128,128]{2,1,0:T(8,128)S(1)}, u32[]{:S(2)}, u32[]{:S(2)}) collective-permute-start(f32[2,128,128]{2,1,0:T(8,128)S(1)} %get-tuple-element.41), channel_id=1, source_target_pairs={{0,16},{1,17},{2,18},{3,19},{4,20},{5,21},{6,22},{7,23},{8,24},{9,... | collective-permute-start | bytes 393224 | tf_op jit(solution)/shard_map/ppermute | solution.py:187
  48.0 1.7 %collective-permute-start.14 = (f32[2,128,128]{2,1,0:T(8,128)S(1)}, f32[2,128,128]{2,1,0:T(8,128)S(1)}, u32[]{:S(2)}, u32[]{:S(2)}) collective-permute-start(f32[2,128,128]{2,1,0:T(8,128)S(1)} %get-tuple-element.42), channel_id=1, source_target_pairs={{0,2},{1,3},{2,0},{3,1},{4,6},{5,7},{6,4},{7,5},{8,10},{9,11},{10,... | collective-permute-start | bytes 393224 | tf_op jit(solution)/shard_map/ppermute | solution.py:176
  49.7 0.0 collective-permute-done.16.refs_1_
  49.7 0.2 collective-permute-start.15
  50.0 0.0 copy-done
  50.0 5.6 %fusion.base = f32[128,1024]{1,0:T(8,128)S(1)} fusion(bf16[128,5120]{1,0:T(8,128)(2,1)S(1)} %copy-done, bf16[5120,1024]{1,0:T(8,128)(2,1)} %param.8), kind=kOutput, calls=%fused_computation.5 | convolution fusion | flops 1342177280 | bytes 12320768 | tf_op jit(solution)/shard_map/dot_general | solution.py:260
  55.6 0.0 collective-permute-done.17.refs_2_
  55.6 0.0 collective-permute-done.18.refs_3_
  55.6 0.0 collective-permute-done.13.z_x
  55.6 0.6 collective-permute-done.14.z_y
  56.2 0.0 collective-permute-done.15.z_d
  56.2 1.1 %shard_map.76 = (f32[128,1024]{1,0:T(8,128)S(1)}, f32[128,1024]{1,0:T(8,128)S(1)}) custom-call(s32[4]{0:T(128)S(1)} %pad_add_fusion.place, f32[128,1024]{1,0:T(8,128)S(1)} %fusion.base, bf16[128,1408]{1,0:T(8,128)(2,1)S(1)} %get-tuple-element.33.refs_0_.mine, bf16[256,1408]{1,0:T(8,128)(2,1)S(1)} %collective-permute-done.8.refs_4_.theirs, ...), custom_call_target="tpu_custom_call" | custom-call | flops 268435456 | bytes 3178512 | tf_op jit(solution)/shard_map/pallas_call | solution.py:33
  57.3 0.1 collective-permute-start.19
  57.4 1.9 %collective-permute-done.19.came = f32[128,1024]{1,0:T(8,128)S(1)} collective-permute-done((f32[128,1024]{1,0:T(8,128)S(1)}, f32[128,1024]{1,0:T(8,128)S(1)}, u32[]{:S(2)}, u32[]{:S(2)}) %collective-permute-start.19) | collective-permute-done | bytes 524320 | tf_op jit(solution)/shard_map/ppermute | solution.py:176
  59.3 0.8 %shard_map.77 = bf16[128,1024]{1,0:T(8,128)(2,1)} custom-call(f32[128,1024]{1,0:T(8,128)S(1)} %get-tuple-element.45.here, f32[128,1024]{1,0:T(8,128)S(1)} %collective-permute-done.19.came), custom_call_target="tpu_custom_call" | custom-call | flops 131072 | bytes 1048576 | tf_op jit(solution)/shard_map/pallas_call | solution.py:33
  (5 shorter events, 0.0 us)
Async XLA Ops:
  2.2 16.2 %collective-permute-start = (bf16[128,1408]{1,0:T(8,128)(2,1)S(1)}, bf16[128,1408]{1,0:T(8,128)(2,1)S(1)}, u32[]{:S(2)}, u32[]{:S(2)}) collective-permute-start(bf16[128,1408]{1,0:T(8,128)(2,1)S(1)} %get-tuple-element.27), channel_id=1, source_target_pairs={{0,16},{1,17},{2,18},{3,19},{4,20},{5,21},{6,22},{7,23},{8,24},{9,... | collective-permute-start | bytes 1081352 | tf_op jit(solution)/shard_map/ppermute | solution.py:187
  5.2 10.5 %collective-permute-start.1 = (bf16[64,1792]{1,0:T(8,128)(2,1)S(1)}, bf16[64,1792]{1,0:T(8,128)(2,1)S(1)}, u32[]{:S(2)}, u32[]{:S(2)}) collective-permute-start(bf16[64,1792]{1,0:T(8,128)(2,1)S(1)} %get-tuple-element.30.refs_6_), channel_id=1, source_target_pairs={{0,4},{1,5},{2,6},{3,7},{4,0},{5,1},{6,2},{7,3},{8,12},{9,13},{10,... | collective-permute-start | bytes 688136 | tf_op jit(solution)/shard_map/ppermute | solution.py:176
  6.8 11.6 %collective-permute-start.2 = (bf16[64,1280]{1,0:T(8,128)(2,1)S(1)}, bf16[64,1280]{1,0:T(8,128)(2,1)S(1)}, u32[]{:S(2)}, u32[]{:S(2)}) collective-permute-start(bf16[64,1280]{1,0:T(8,128)(2,1)S(1)} %get-tuple-element.29), channel_id=1, source_target_pairs={{0,2},{1,3},{2,0},{3,1},{4,6},{5,7},{6,4},{7,5},{8,10},{9,11},{10,... | collective-permute-start | bytes 491528 | tf_op jit(solution)/shard_map/ppermute | solution.py:176
  8.3 12.5 %collective-permute-start.4 = (bf16[64,1792]{1,0:T(8,128)(2,1)S(1)}, bf16[64,1792]{1,0:T(8,128)(2,1)S(1)}, u32[]{:S(2)}, u32[]{:S(2)}) collective-permute-start(bf16[64,1792]{1,0:T(8,128)(2,1)S(1)} %get-tuple-element.30.refs_6_), channel_id=1, source_target_pairs={{0,8},{1,9},{2,10},{3,11},{4,12},{5,13},{6,14},{7,15},{8,0},{9,1},... | collective-permute-start | bytes 688136 | tf_op jit(solution)/shard_map/ppermute | solution.py:176
  15.7 17.0 %collective-permute-start.9 = (bf16[128,1408]{1,0:T(8,128)(2,1)S(1)}, bf16[128,1408]{1,0:T(8,128)(2,1)S(1)}, u32[]{:S(2)}, u32[]{:S(2)}) collective-permute-start(bf16[128,1408]{1,0:T(8,128)(2,1)S(1)} %get-tuple-element.36), channel_id=1, source_target_pairs={{0,2},{1,3},{2,0},{3,1},{4,6},{5,7},{6,4},{7,5},{8,10},{9,11},{10,... | collective-permute-start | bytes 1081352 | tf_op jit(solution)/shard_map/ppermute | solution.py:176
  18.4 14.3 %collective-permute-start.7 = (bf16[128,1408]{1,0:T(8,128)(2,1)S(1)}, bf16[128,1408]{1,0:T(8,128)(2,1)S(1)}, u32[]{:S(2)}, u32[]{:S(2)}) collective-permute-start(bf16[128,1408]{1,0:T(8,128)(2,1)S(1)} %get-tuple-element.32), channel_id=1, source_target_pairs={{0,18},{1,19},{2,16},{3,17},{4,22},{5,23},{6,20},{7,21},{8,26},{9,... | collective-permute-start | bytes 1081352 | tf_op jit(solution)/shard_map/ppermute | solution.py:187
  18.4 14.2 %collective-permute-start.3 = (bf16[64,1792]{1,0:T(8,128)(2,1)S(1)}, bf16[64,1792]{1,0:T(8,128)(2,1)S(1)}, u32[]{:S(2)}, u32[]{:S(2)}) collective-permute-start(bf16[64,1792]{1,0:T(8,128)(2,1)S(1)} %get-tuple-element.30.refs_6_), channel_id=1, source_target_pairs={{4,8},{5,9},{6,10},{7,11},{8,4},{9,5},{10,6},{11,7},{20,24},{21,25... | collective-permute-start | bytes 688136 | tf_op jit(solution)/shard_map/ppermute | solution.py:179
  20.8 11.8 %collective-permute-start.5 = (bf16[64,1792]{1,0:T(8,128)(2,1)S(1)}, bf16[64,1792]{1,0:T(8,128)(2,1)S(1)}, u32[]{:S(2)}, u32[]{:S(2)}) collective-permute-start(bf16[64,1792]{1,0:T(8,128)(2,1)S(1)} %collective-permute-done.4.refs_8_), channel_id=1, source_target_pairs={{4,0},{5,1},{6,2},{7,3},{8,12},{9,13},{10,14},{11,15},{20,16},{21,... | collective-permute-start | bytes 688136 | tf_op jit(solution)/shard_map/ppermute | solution.py:179
  22.1 10.5 %collective-permute-start.6 = (bf16[64,1280]{1,0:T(8,128)(2,1)S(1)}, bf16[64,1280]{1,0:T(8,128)(2,1)S(1)}, u32[]{:S(2)}, u32[]{:S(2)}) collective-permute-start(bf16[64,1280]{1,0:T(8,128)(2,1)S(1)} %collective-permute-done.2.refs_6_), channel_id=1, source_target_pairs={{0,8},{1,9},{2,10},{3,11},{4,12},{5,13},{6,14},{7,15},{8,0},{9,1},... | collective-permute-start | bytes 491528 | tf_op jit(solution)/shard_map/ppermute | solution.py:176
  32.8 4.5 %collective-permute-start.10 = (bf16[256,1408]{1,0:T(8,128)(2,1)S(1)}, bf16[256,1408]{1,0:T(8,128)(2,1)S(1)}, u32[]{:S(2)}, u32[]{:S(2)}) collective-permute-start(bf16[256,1408]{1,0:T(8,128)(2,1)S(1)} %pad_maximum_fusion.1), channel_id=1, source_target_pairs={{0,1},{1,0},{2,3},{3,2},{4,5},{5,4},{6,7},{7,6},{8,9},{9,8},{10,11... | collective-permute-start | bytes 2162696 | tf_op jit(solution)/shard_map/ppermute | solution.py:176
  32.9 6.1 %collective-permute-start.8 = (bf16[256,1408]{1,0:T(8,128)(2,1)S(1)}, bf16[256,1408]{1,0:T(8,128)(2,1)S(1)}, u32[]{:S(2)}, u32[]{:S(2)}) collective-permute-start(bf16[256,1408]{1,0:T(8,128)(2,1)S(1)} %pad_maximum_fusion), channel_id=1, source_target_pairs={{0,1},{1,0},{2,3},{3,2},{4,5},{5,4},{6,7},{7,6},{8,9},{9,8},{10,11... | collective-permute-start | bytes 2162696 | tf_op jit(solution)/shard_map/ppermute | solution.py:176
  33.6 16.2 %collective-permute-start.16 = (bf16[256,512]{1,0:T(8,128)(2,1)S(1)}, bf16[256,512]{1,0:T(8,128)(2,1)S(1)}, u32[]{:S(2)}, u32[]{:S(2)}) collective-permute-start(bf16[256,512]{1,0:T(8,128)(2,1)S(1)} %pad_maximum_fusion.2.refs_0_), channel_id=1, source_target_pairs={{0,16},{1,17},{2,18},{3,19},{4,20},{5,21},{6,22},{7,23},{8,24},{9,... | collective-permute-start | bytes 786440 | tf_op jit(solution)/shard_map/ppermute | solution.py:187
  34.7 6.9 %collective-permute-start.11 = (bf16[64,1280]{1,0:T(8,128)(2,1)S(1)}, bf16[64,1280]{1,0:T(8,128)(2,1)S(1)}, u32[]{:S(2)}, u32[]{:S(2)}) collective-permute-start(bf16[64,1280]{1,0:T(8,128)(2,1)S(1)} %collective-permute-done.2.refs_6_), channel_id=1, source_target_pairs={{0,4},{1,5},{2,6},{3,7},{4,0},{5,1},{6,2},{7,3},{8,12},{9,13},{10,... | collective-permute-start | bytes 491528 | tf_op jit(solution)/shard_map/ppermute | solution.py:176
  34.7 10.2 %collective-permute-start.12 = (bf16[64,1280]{1,0:T(8,128)(2,1)S(1)}, bf16[64,1280]{1,0:T(8,128)(2,1)S(1)}, u32[]{:S(2)}, u32[]{:S(2)}) collective-permute-start(bf16[64,1280]{1,0:T(8,128)(2,1)S(1)} %collective-permute-done.2.refs_6_), channel_id=1, source_target_pairs={{0,12},{1,13},{2,14},{3,15},{4,8},{5,9},{6,10},{7,11},{8,4},{9,5},... | collective-permute-start | bytes 491528 | tf_op jit(solution)/shard_map/ppermute | solution.py:176
  37.2 18.3 %collective-permute-start.17 = (bf16[256,512]{1,0:T(8,128)(2,1)S(1)}, bf16[256,512]{1,0:T(8,128)(2,1)S(1)}, u32[]{:S(2)}, u32[]{:S(2)}) collective-permute-start(bf16[256,512]{1,0:T(8,128)(2,1)S(1)} %pad_maximum_fusion.2.refs_0_), channel_id=1, source_target_pairs={{0,2},{1,3},{2,0},{3,1},{4,6},{5,7},{6,4},{7,5},{8,10},{9,11},{10,... | collective-permute-start | bytes 786440 | tf_op jit(solution)/shard_map/ppermute | solution.py:176
  39.0 16.6 %collective-permute-start.18 = (bf16[256,512]{1,0:T(8,128)(2,1)S(1)}, bf16[256,512]{1,0:T(8,128)(2,1)S(1)}, u32[]{:S(2)}, u32[]{:S(2)}) collective-permute-start(bf16[256,512]{1,0:T(8,128)(2,1)S(1)} %pad_maximum_fusion.2.refs_0_), channel_id=1, source_target_pairs={{0,18},{1,19},{2,16},{3,17},{4,22},{5,23},{6,20},{7,21},{8,26},{9,... | collective-permute-start | bytes 786440 | tf_op jit(solution)/shard_map/ppermute | solution.py:187
  41.6 8.3 %copy-start = (bf16[128,5120]{1,0:T(8,128)(2,1)S(1)}, bf16[128,5120]{1,0:T(8,128)(2,1)}, u32[]{:S(2)}) copy-start(bf16[128,5120]{1,0:T(8,128)(2,1)} %hidden.1) | copy-start | bytes 3932164
  46.4 9.2 %collective-permute-start.13 = (f32[2,128,128]{2,1,0:T(8,128)S(1)}, f32[2,128,128]{2,1,0:T(8,128)S(1)}, u32[]{:S(2)}, u32[]{:S(2)}) collective-permute-start(f32[2,128,128]{2,1,0:T(8,128)S(1)} %get-tuple-element.41), channel_id=1, source_target_pairs={{0,16},{1,17},{2,18},{3,19},{4,20},{5,21},{6,22},{7,23},{8,24},{9,... | collective-permute-start | bytes 393224 | tf_op jit(solution)/shard_map/ppermute | solution.py:187
  48.0 8.2 %collective-permute-start.14 = (f32[2,128,128]{2,1,0:T(8,128)S(1)}, f32[2,128,128]{2,1,0:T(8,128)S(1)}, u32[]{:S(2)}, u32[]{:S(2)}) collective-permute-start(f32[2,128,128]{2,1,0:T(8,128)S(1)} %get-tuple-element.42), channel_id=1, source_target_pairs={{0,2},{1,3},{2,0},{3,1},{4,6},{5,7},{6,4},{7,5},{8,10},{9,11},{10,... | collective-permute-start | bytes 393224 | tf_op jit(solution)/shard_map/ppermute | solution.py:176
  49.7 6.5 %collective-permute-start.15 = (f32[2,128,128]{2,1,0:T(8,128)S(1)}, f32[2,128,128]{2,1,0:T(8,128)S(1)}, u32[]{:S(2)}, u32[]{:S(2)}) collective-permute-start(f32[2,128,128]{2,1,0:T(8,128)S(1)} %get-tuple-element.43), channel_id=1, source_target_pairs={{0,18},{1,19},{2,16},{3,17},{4,22},{5,23},{6,20},{7,21},{8,26},{9,... | collective-permute-start | bytes 393224 | tf_op jit(solution)/shard_map/ppermute | solution.py:187
  57.3 2.0 %collective-permute-start.19 = (f32[128,1024]{1,0:T(8,128)S(1)}, f32[128,1024]{1,0:T(8,128)S(1)}, u32[]{:S(2)}, u32[]{:S(2)}) collective-permute-start(f32[128,1024]{1,0:T(8,128)S(1)} %get-tuple-element.46), channel_id=1, source_target_pairs={{0,1},{1,0},{2,3},{3,2},{4,5},{5,4},{6,7},{7,6},{8,9},{9,8},{10,11... | collective-permute-start | bytes 1572872 | tf_op jit(solution)/shard_map/ppermute | solution.py:176

commit v6 on v5

--- a/solution.py
+++ b/solution.py
@@ -37,7 +37,7 @@
         out_specs=jax.tree.map(lambda _: VMEM, out),
         scratch_shapes=scratch,
         cost_estimate=pl.CostEstimate(flops=flops, bytes_accessed=moved, transcendentals=0),
-        compiler_params=pltpu.CompilerParams(vmem_limit_bytes=(16 if whole else 48) << 20),
+        compiler_params=pltpu.CompilerParams(vmem_limit_bytes=(16 if whole else 32) << 20),
     )(*operands)
 
 
@@ -120,25 +120,27 @@
             kept = jnp.where(tags[i] == ids, z[i * rows : (i + 1) * rows, :], 0.0)
             kept = sum(kept[:, j : j + 128] for j in range(0, some * rank, 128))
             sums[i] = kept if sums[i] is None else sums[i] + kept
-    for i in range(8):
-        if flipped:
-            outs[i % 4][i // 4] = sums[i]
-        else:
+    if not flipped:
+        for i in range(8):
             outs[0][i] = sums[i]
+        return
+    sums = [v[:, :rank] + v[:, rank:] for v in sums]
+    for i in range(4):
+        outs[i][...] = jnp.concatenate([sums[i], sums[i + 4]], axis=1)
 
 
 def add_up(planes, place, base, mine, theirs, z_here, z_x, z_y, z_d, *refs):
     *held, out, away = refs
     x, plane, column, core = place[0], place[1], place[2], place[3]
     rows, quarter = mine.shape[0], mine.shape[1] - TAG
-    rank = z_here.shape[2] // 2
+    rank = z_here.shape[1] // 2
     qhalf = held[0].shape[1]
     tag = jnp.concatenate(
         [mine[:, quarter : quarter + 1], theirs[:rows, quarter : quarter + 1]], axis=0
     )
     tag = tag.astype(jnp.float32).astype(jnp.int32)
-    both = [z_here[i] + z_x[i] + z_y[i] + z_d[i] for i in range(2)]
-    z = jnp.concatenate([b[:, :rank] + b[:, rank:] for b in both], axis=0)
+    both = z_here[...] + z_x[...] + z_y[...] + z_d[...]
+    z = jnp.concatenate([both[:, :rank], both[:, rank:]], axis=0)
     z = z.astype(jnp.bfloat16).astype(jnp.float32)
     some = min(planes, 4)
     spread = jnp.concatenate([z] * some, axis=1)
@@ -290,7 +292,7 @@
     )
     z_here, z_x, z_y, z_d = call(
         functools.partial(sum_z, True, planes, 0),
-        (jax.ShapeDtypeStruct((2, rows, 2 * rank), f32),) * 4,
+        (jax.ShapeDtypeStruct((rows, 2 * rank), f32),) * 4,
         (place, *blocks, *b_units, part),
         scalars=1,
         flops=flops,

time: 60.2 us -> 58.3 us (0.968)
  matrix products: 5.61 us -> 1.53 us
  waiting for transfers between devices: 19.2 us -> 21.8 us
    dot_general x1, matrix products: 5.61 us -> 1.53 us  [body(): jnp.dot(*late(hidden), base_weight, preferred_element_type=f32)]
    ppermute x6, waiting for transfers between devices: 0.02 us -> 3.89 us  [across(): return lax.ppermute(value, ('replica', 'owner'), pairs)]
    ppermute x12, starting transfers between devices: 18.8 us -> 16.8 us  [by_owner(): return lax.ppermute(value, 'owner', [(i, i ^ flip) for i in range(owners)])]
    ppermute x6, starting transfers between devices: 7.25 us -> 8.82 us  [across(): return lax.ppermute(value, ('replica', 'owner'), pairs)]
    ppermute x12, waiting for transfers between devices: 19.2 us -> 17.9 us  [by_owner(): return lax.ppermute(value, 'owner', [(i, i ^ flip) for i in range(owners)])]
  transfers between devices with their start and end apart: 20 -> 20, of which waited for: 7 -> 10; matrix products, arithmetic and copies ran while one was open for 10% -> 3% of each run, Pallas kernels for 5% -> 5%
where the time goes in v6:
time: 58.3 us; the launch traced here: 58.1 us
  starting transfers between devices  27.6 us (47%)
  waiting for transfers between devices  21.8 us (37%)
  Pallas kernels  6.9 us (12%)
  matrix products  1.53 us (3%)
    ppermute x12, waiting for transfers between devices, by_owner(): return lax.ppermute(value, 'owner', [(i, i ^ flip) for i in range(owners)])  17.9 us
    ppermute x12, starting transfers between devices, by_owner(): return lax.ppermute(value, 'owner', [(i, i ^ flip) for i in range(owners)])  16.8 us
    ppermute x6, starting transfers between devices, across(): return lax.ppermute(value, ('replica', 'owner'), pairs)  8.82 us
    pallas_call x5, Pallas kernels, call(): pl.pallas_call(kernel, out_shape=out, in_specs=[SMEM] * scalars + [VMEM]...  6.9 us
    ppermute x6, waiting for transfers between devices, across(): return lax.ppermute(value, ('replica', 'owner'), pairs)  3.89 us
    ppermute x2, starting transfers between devices, between(): lax.ppermute(value, 'owner', [(a * 4 + i, b * 4 + i) for a, b in pairs fo...  1.94 us
    dot_general x1, matrix products, body(): jnp.dot(*late(hidden), base_weight, preferred_element_type=f32)  1.53 us
  transfers between devices with their start and end apart: 20, of which 10 were waited for; matrix products, arithmetic and copies ran while one was open for 3% of the time, Pallas kernels for 5%

profile of v6, /device:TPU:0, one launch (start us, length us, event | category | flops | bytes accessed | tf_op | source)
XLA Modules:
  0.0 58.1 jit_solution(1298574102829153312)
XLA Ops:
  0.0 0.1 pad_add_fusion.place
  0.1 2.1 %shard_map.73 = (bf16[64,1280]{1,0:T(8,128)(2,1)S(1)}, bf16[64,1792]{1,0:T(8,128)(2,1)S(1)}, bf16[128,1408]{1,0:T(8,128)(2,1)S(1)}, bf16[128,1408]{1,0:T(8,128)(...) custom-call(s32[4]{0:T(128)S(1)} %pad_add_fusion.place, bf16[1,64,5120]{2,1,0:T(8,128)(2,1)} %down.1, ...), custom_call_target="tpu_custom_call" | custom-call | bytes 2097760 | tf_op jit(solution)/shard_map/pallas_call | solution.py:33
  2.2 3.0 %collective-permute-start = (bf16[128,1408]{1,0:T(8,128)(2,1)S(1)}, bf16[128,1408]{1,0:T(8,128)(2,1)S(1)}, u32[]{:S(2)}, u32[]{:S(2)}) collective-permute-start(bf16[128,1408]{1,0:T(8,128)(2,1)S(1)} %get-tuple-element.27), channel_id=1, source_target_pairs={{0,16},{1,17},{2,18},{3,19},{4,20},{5,21},{6,22},{7,23},{8,24},{9,... | collective-permute-start | bytes 1081352 | tf_op jit(solution)/shard_map/ppermute | solution.py:189
  5.2 1.5 %collective-permute-start.2 = (bf16[64,1280]{1,0:T(8,128)(2,1)S(1)}, bf16[64,1280]{1,0:T(8,128)(2,1)S(1)}, u32[]{:S(2)}, u32[]{:S(2)}) collective-permute-start(bf16[64,1280]{1,0:T(8,128)(2,1)S(1)} %get-tuple-element.29), channel_id=1, source_target_pairs={{0,2},{1,3},{2,0},{3,1},{4,6},{5,7},{6,4},{7,5},{8,10},{9,11},{10,... | collective-permute-start | bytes 491528 | tf_op jit(solution)/shard_map/ppermute | solution.py:178
  6.7 1.6 %collective-permute-start.1 = (bf16[64,1792]{1,0:T(8,128)(2,1)S(1)}, bf16[64,1792]{1,0:T(8,128)(2,1)S(1)}, u32[]{:S(2)}, u32[]{:S(2)}) collective-permute-start(bf16[64,1792]{1,0:T(8,128)(2,1)S(1)} %get-tuple-element.30.refs_6_), channel_id=1, source_target_pairs={{0,4},{1,5},{2,6},{3,7},{4,0},{5,1},{6,2},{7,3},{8,12},{9,13},{10,... | collective-permute-start | bytes 688136 | tf_op jit(solution)/shard_map/ppermute | solution.py:178
  8.3 2.6 %collective-permute-start.4 = (bf16[64,1792]{1,0:T(8,128)(2,1)S(1)}, bf16[64,1792]{1,0:T(8,128)(2,1)S(1)}, u32[]{:S(2)}, u32[]{:S(2)}) collective-permute-start(bf16[64,1792]{1,0:T(8,128)(2,1)S(1)} %get-tuple-element.30.refs_6_), channel_id=1, source_target_pairs={{0,8},{1,9},{2,10},{3,11},{4,12},{5,13},{6,14},{7,15},{8,0},{9,1},... | collective-permute-start | bytes 688136 | tf_op jit(solution)/shard_map/ppermute | solution.py:178
  10.9 0.0 collective-permute-done.2.refs_6_
  10.9 2.7 %collective-permute-done.refs_1_ = bf16[128,1408]{1,0:T(8,128)(2,1)S(1)} collective-permute-done((bf16[128,1408]{1,0:T(8,128)(2,1)S(1)}, bf16[128,1408]{1,0:T(8,128)(2,1)S(1)}, u32[]{:S(2)}, u32[]{:S(2)}) %collective-permute-start) | collective-permute-done | bytes 360480 | tf_op jit(solution)/shard_map/ppermute | solution.py:189
  13.6 2.7 %collective-permute-start.7 = (bf16[128,1408]{1,0:T(8,128)(2,1)S(1)}, bf16[128,1408]{1,0:T(8,128)(2,1)S(1)}, u32[]{:S(2)}, u32[]{:S(2)}) collective-permute-start(bf16[128,1408]{1,0:T(8,128)(2,1)S(1)} %get-tuple-element.32), channel_id=1, source_target_pairs={{0,18},{1,19},{2,16},{3,17},{4,22},{5,23},{6,20},{7,21},{8,26},{9,... | collective-permute-start | bytes 1081352 | tf_op jit(solution)/shard_map/ppermute | solution.py:189
  16.3 2.0 %collective-permute-done.1.refs_7_ = bf16[64,1792]{1,0:T(8,128)(2,1)S(1)} collective-permute-done((bf16[64,1792]{1,0:T(8,128)(2,1)S(1)}, bf16[64,1792]{1,0:T(8,128)(2,1)S(1)}, u32[]{:S(2)}, u32[]{:S(2)}) %collective-permute-start.1) | collective-permute-done | bytes 229408 | tf_op jit(solution)/shard_map/ppermute | solution.py:178
  18.3 0.7 %collective-permute-start.3 = (bf16[64,1792]{1,0:T(8,128)(2,1)S(1)}, bf16[64,1792]{1,0:T(8,128)(2,1)S(1)}, u32[]{:S(2)}, u32[]{:S(2)}) collective-permute-start(bf16[64,1792]{1,0:T(8,128)(2,1)S(1)} %get-tuple-element.30.refs_6_), channel_id=1, source_target_pairs={{4,8},{5,9},{6,10},{7,11},{8,4},{9,5},{10,6},{11,7},{20,24},{21,25... | collective-permute-start | bytes 688136 | tf_op jit(solution)/shard_map/ppermute | solution.py:181
  19.0 1.7 %collective-permute-done.4.refs_8_ = bf16[64,1792]{1,0:T(8,128)(2,1)S(1)} collective-permute-done((bf16[64,1792]{1,0:T(8,128)(2,1)S(1)}, bf16[64,1792]{1,0:T(8,128)(2,1)S(1)}, u32[]{:S(2)}, u32[]{:S(2)}) %collective-permute-start.4) | collective-permute-done | bytes 229408 | tf_op jit(solution)/shard_map/ppermute | solution.py:178
  20.7 1.3 %collective-permute-start.5 = (bf16[64,1792]{1,0:T(8,128)(2,1)S(1)}, bf16[64,1792]{1,0:T(8,128)(2,1)S(1)}, u32[]{:S(2)}, u32[]{:S(2)}) collective-permute-start(bf16[64,1792]{1,0:T(8,128)(2,1)S(1)} %collective-permute-done.4.refs_8_), channel_id=1, source_target_pairs={{4,0},{5,1},{6,2},{7,3},{8,12},{9,13},{10,14},{11,15},{20,16},{21,... | collective-permute-start | bytes 688136 | tf_op jit(solution)/shard_map/ppermute | solution.py:181
  22.0 3.8 %collective-permute-start.6 = (bf16[64,1280]{1,0:T(8,128)(2,1)S(1)}, bf16[64,1280]{1,0:T(8,128)(2,1)S(1)}, u32[]{:S(2)}, u32[]{:S(2)}) collective-permute-start(bf16[64,1280]{1,0:T(8,128)(2,1)S(1)} %collective-permute-done.2.refs_6_), channel_id=1, source_target_pairs={{0,8},{1,9},{2,10},{3,11},{4,12},{5,13},{6,14},{7,15},{8,0},{9,1},... | collective-permute-start | bytes 491528 | tf_op jit(solution)/shard_map/ppermute | solution.py:178
  25.8 0.5 collective-permute-start.9
  26.3 6.3 %collective-permute-done.6.refs_8_ = bf16[64,1280]{1,0:T(8,128)(2,1)S(1)} collective-permute-done((bf16[64,1280]{1,0:T(8,128)(2,1)S(1)}, bf16[64,1280]{1,0:T(8,128)(2,1)S(1)}, u32[]{:S(2)}, u32[]{:S(2)}) %collective-permute-start.6) | collective-permute-done | bytes 163872 | tf_op jit(solution)/shard_map/ppermute | solution.py:178
  32.6 0.0 collective-permute-done.3.refs_9_
  32.6 0.0 collective-permute-done.5.refs_10_
  32.6 0.0 collective-permute-done.7.refs_3_
  32.6 0.0 copy-start.1
  32.6 0.1 pad_maximum_fusion
  32.7 0.1 collective-permute-start.8
  32.8 0.4 collective-permute-done.9.refs_2_
  33.2 0.0 copy-start
  33.2 0.1 pad_maximum_fusion.1
  33.3 0.1 collective-permute-start.10
  33.5 0.6 %collective-permute-start.16 = (bf16[256,512]{1,0:T(8,128)(2,1)S(1)}, bf16[256,512]{1,0:T(8,128)(2,1)S(1)}, u32[]{:S(2)}, u32[]{:S(2)}) collective-permute-start(bf16[256,512]{1,0:T(8,128)(2,1)S(1)} %pad_maximum_fusion.2.refs_0_), channel_id=1, source_target_pairs={{0,16},{1,17},{2,18},{3,19},{4,20},{5,21},{6,22},{7,23},{8,24},{9,... | collective-permute-start | bytes 786440 | tf_op jit(solution)/shard_map/ppermute | solution.py:189
  34.1 1.1 %collective-permute-start.11 = (bf16[64,1280]{1,0:T(8,128)(2,1)S(1)}, bf16[64,1280]{1,0:T(8,128)(2,1)S(1)}, u32[]{:S(2)}, u32[]{:S(2)}) collective-permute-start(bf16[64,1280]{1,0:T(8,128)(2,1)S(1)} %collective-permute-done.2.refs_6_), channel_id=1, source_target_pairs={{0,4},{1,5},{2,6},{3,7},{4,0},{5,1},{6,2},{7,3},{8,12},{9,13},{10,... | collective-permute-start | bytes 491528 | tf_op jit(solution)/shard_map/ppermute | solution.py:178
  35.1 2.5 %collective-permute-start.12 = (bf16[64,1280]{1,0:T(8,128)(2,1)S(1)}, bf16[64,1280]{1,0:T(8,128)(2,1)S(1)}, u32[]{:S(2)}, u32[]{:S(2)}) collective-permute-start(bf16[64,1280]{1,0:T(8,128)(2,1)S(1)} %collective-permute-done.2.refs_6_), channel_id=1, source_target_pairs={{0,12},{1,13},{2,14},{3,15},{4,8},{5,9},{6,10},{7,11},{8,4},{9,5},... | collective-permute-start | bytes 491528 | tf_op jit(solution)/shard_map/ppermute | solution.py:178
  37.6 0.0 collective-permute-done.8.refs_4_.theirs
  37.6 1.5 %collective-permute-start.17 = (bf16[256,512]{1,0:T(8,128)(2,1)S(1)}, bf16[256,512]{1,0:T(8,128)(2,1)S(1)}, u32[]{:S(2)}, u32[]{:S(2)}) collective-permute-start(bf16[256,512]{1,0:T(8,128)(2,1)S(1)} %pad_maximum_fusion.2.refs_0_), channel_id=1, source_target_pairs={{0,2},{1,3},{2,0},{3,1},{4,6},{5,7},{6,4},{7,5},{8,10},{9,11},{10,... | collective-permute-start | bytes 786440 | tf_op jit(solution)/shard_map/ppermute | solution.py:178
  39.1 0.0 collective-permute-done.10.refs_5_
  39.1 0.5 collective-permute-start.18
  39.6 1.4 %shard_map.74.refs_10_ = f32[8,128,128]{2,1,0:T(8,128)S(1)} custom-call(s32[4]{0:T(128)S(1)} %pad_add_fusion.place, bf16[128,1408]{1,0:T(8,128)(2,1)S(1)} %get-tuple-element.33.refs_0_.mine, bf16[128,1408]{1,0:T(8,128)(2,1)S(1)} %collective-permute-done.refs_1_, bf16[128,1408]{1,0:T(8,128)(2,1)S(1)} %collective-permute-done.9.refs_2_, ...), custom_call_target="tpu_custom_call" | custom-call | flops 671088640 | bytes 4030480 | tf_op jit(solution)/shard_map/pallas_call | solution.py:33
  41.0 0.0 collective-permute-done.11.refs_7_
  41.1 4.4 %collective-permute-done.12.refs_9_ = bf16[64,1280]{1,0:T(8,128)(2,1)S(1)} collective-permute-done((bf16[64,1280]{1,0:T(8,128)(2,1)S(1)}, bf16[64,1280]{1,0:T(8,128)(2,1)S(1)}, u32[]{:S(2)}, u32[]{:S(2)}) %collective-permute-start.12) | collective-permute-done | bytes 163872 | tf_op jit(solution)/shard_map/ppermute | solution.py:178
  45.5 1.6 %shard_map.75 = (f32[128,128]{1,0:T(8,128)S(1)}, f32[128,128]{1,0:T(8,128)S(1)}, f32[128,128]{1,0:T(8,128)S(1)}, f32[128,128]{1,0:T(8,128)S(1)}) custom-call(s32[4]{0:T(128)S(1)} %pad_add_fusion.place, bf16[128,1408]{1,0:T(8,128)(2,1)S(1)} %get-tuple-element.33.refs_0_.mine, bf16[128,1408]{1,0:T(8,128)(2,1)S(1)} %collective-permute-done.refs_1_, ...), custom_call_target="tpu_custom_call" | custom-call | flops 671088640 | bytes 4063248 | tf_op jit(solution)/shard_map/pallas_call | solution.py:33
  47.1 0.6 %collective-permute-start.13 = (f32[128,128]{1,0:T(8,128)S(1)}, f32[128,128]{1,0:T(8,128)S(1)}, u32[]{:S(2)}, u32[]{:S(2)}) collective-permute-start(f32[128,128]{1,0:T(8,128)S(1)} %get-tuple-element.41), channel_id=1, source_target_pairs={{0,16},{1,17},{2,18},{3,19},{4,20},{5,21},{6,22},{7,23},{8,24},{9,... | collective-permute-start | bytes 196616 | tf_op jit(solution)/shard_map/ppermute | solution.py:189
  47.7 1.5 %collective-permute-start.14 = (f32[128,128]{1,0:T(8,128)S(1)}, f32[128,128]{1,0:T(8,128)S(1)}, u32[]{:S(2)}, u32[]{:S(2)}) collective-permute-start(f32[128,128]{1,0:T(8,128)S(1)} %get-tuple-element.42), channel_id=1, source_target_pairs={{0,2},{1,3},{2,0},{3,1},{4,6},{5,7},{6,4},{7,5},{8,10},{9,11},{10,... | collective-permute-start | bytes 196616 | tf_op jit(solution)/shard_map/ppermute | solution.py:178
  49.2 0.0 collective-permute-done.16.refs_1_
  49.2 1.4 %collective-permute-start.15 = (f32[128,128]{1,0:T(8,128)S(1)}, f32[128,128]{1,0:T(8,128)S(1)}, u32[]{:S(2)}, u32[]{:S(2)}) collective-permute-start(f32[128,128]{1,0:T(8,128)S(1)} %get-tuple-element.43), channel_id=1, source_target_pairs={{0,18},{1,19},{2,16},{3,17},{4,22},{5,23},{6,20},{7,21},{8,26},{9,... | collective-permute-start | bytes 196616 | tf_op jit(solution)/shard_map/ppermute | solution.py:189
  50.6 0.0 copy-done.1
  50.6 0.0 copy-done
  50.6 1.5 %fusion.base = f32[128,1024]{1,0:T(8,128)S(1)} fusion(bf16[128,5120]{1,0:T(8,128)(2,1)S(1)} %copy-done.1, bf16[5120,1024]{1,0:T(8,128)(2,1)S(1)} %copy-done), kind=kOutput, calls=%fused_computation.5 | convolution fusion | flops 1342177280 | bytes 12320768 | tf_op jit(solution)/shard_map/dot_general | solution.py:262
  52.2 0.2 collective-permute-done.17.refs_2_
  52.3 0.0 collective-permute-done.18.refs_3_
  52.3 0.0 collective-permute-done.13.z_x
  52.3 0.9 %collective-permute-done.14.z_y = f32[128,128]{1,0:T(8,128)S(1)} collective-permute-done((f32[128,128]{1,0:T(8,128)S(1)}, f32[128,128]{1,0:T(8,128)S(1)}, u32[]{:S(2)}, u32[]{:S(2)}) %collective-permute-start.14) | collective-permute-done | bytes 65568 | tf_op jit(solution)/shard_map/ppermute | solution.py:178
  53.2 1.2 %collective-permute-done.15.z_d = f32[128,128]{1,0:T(8,128)S(1)} collective-permute-done((f32[128,128]{1,0:T(8,128)S(1)}, f32[128,128]{1,0:T(8,128)S(1)}, u32[]{:S(2)}, u32[]{:S(2)}) %collective-permute-start.15) | collective-permute-done | bytes 65568 | tf_op jit(solution)/shard_map/ppermute | solution.py:189
  54.3 1.1 %shard_map.76 = (f32[128,1024]{1,0:T(8,128)S(1)}, f32[128,1024]{1,0:T(8,128)S(1)}) custom-call(s32[4]{0:T(128)S(1)} %pad_add_fusion.place, f32[128,1024]{1,0:T(8,128)S(1)} %fusion.base, bf16[128,1408]{1,0:T(8,128)(2,1)S(1)} %get-tuple-element.33.refs_0_.mine, bf16[256,1408]{1,0:T(8,128)(2,1)S(1)} %collective-permute-done.8.refs_4_.theirs, ...), custom_call_target="tpu_custom_call" | custom-call | flops 268435456 | bytes 2916368 | tf_op jit(solution)/shard_map/pallas_call | solution.py:33
  55.4 0.1 collective-permute-start.19
  55.5 1.9 %collective-permute-done.19.came = f32[128,1024]{1,0:T(8,128)S(1)} collective-permute-done((f32[128,1024]{1,0:T(8,128)S(1)}, f32[128,1024]{1,0:T(8,128)S(1)}, u32[]{:S(2)}, u32[]{:S(2)}) %collective-permute-start.19) | collective-permute-done | bytes 524320 | tf_op jit(solution)/shard_map/ppermute | solution.py:178
  57.4 0.8 %shard_map.77 = bf16[128,1024]{1,0:T(8,128)(2,1)} custom-call(f32[128,1024]{1,0:T(8,128)S(1)} %get-tuple-element.45.here, f32[128,1024]{1,0:T(8,128)S(1)} %collective-permute-done.19.came), custom_call_target="tpu_custom_call" | custom-call | flops 131072 | bytes 1048576 | tf_op jit(solution)/shard_map/pallas_call | solution.py:33
  (5 shorter events, 0.0 us)
Async XLA Ops:
  2.2 11.4 %collective-permute-start = (bf16[128,1408]{1,0:T(8,128)(2,1)S(1)}, bf16[128,1408]{1,0:T(8,128)(2,1)S(1)}, u32[]{:S(2)}, u32[]{:S(2)}) collective-permute-start(bf16[128,1408]{1,0:T(8,128)(2,1)S(1)} %get-tuple-element.27), channel_id=1, source_target_pairs={{0,16},{1,17},{2,18},{3,19},{4,20},{5,21},{6,22},{7,23},{8,24},{9,... | collective-permute-start | bytes 1081352 | tf_op jit(solution)/shard_map/ppermute | solution.py:189
  5.2 5.7 %collective-permute-start.2 = (bf16[64,1280]{1,0:T(8,128)(2,1)S(1)}, bf16[64,1280]{1,0:T(8,128)(2,1)S(1)}, u32[]{:S(2)}, u32[]{:S(2)}) collective-permute-start(bf16[64,1280]{1,0:T(8,128)(2,1)S(1)} %get-tuple-element.29), channel_id=1, source_target_pairs={{0,2},{1,3},{2,0},{3,1},{4,6},{5,7},{6,4},{7,5},{8,10},{9,11},{10,... | collective-permute-start | bytes 491528 | tf_op jit(solution)/shard_map/ppermute | solution.py:178
  6.7 11.6 %collective-permute-start.1 = (bf16[64,1792]{1,0:T(8,128)(2,1)S(1)}, bf16[64,1792]{1,0:T(8,128)(2,1)S(1)}, u32[]{:S(2)}, u32[]{:S(2)}) collective-permute-start(bf16[64,1792]{1,0:T(8,128)(2,1)S(1)} %get-tuple-element.30.refs_6_), channel_id=1, source_target_pairs={{0,4},{1,5},{2,6},{3,7},{4,0},{5,1},{6,2},{7,3},{8,12},{9,13},{10,... | collective-permute-start | bytes 688136 | tf_op jit(solution)/shard_map/ppermute | solution.py:178
  8.3 12.4 %collective-permute-start.4 = (bf16[64,1792]{1,0:T(8,128)(2,1)S(1)}, bf16[64,1792]{1,0:T(8,128)(2,1)S(1)}, u32[]{:S(2)}, u32[]{:S(2)}) collective-permute-start(bf16[64,1792]{1,0:T(8,128)(2,1)S(1)} %get-tuple-element.30.refs_6_), channel_id=1, source_target_pairs={{0,8},{1,9},{2,10},{3,11},{4,12},{5,13},{6,14},{7,15},{8,0},{9,1},... | collective-permute-start | bytes 688136 | tf_op jit(solution)/shard_map/ppermute | solution.py:178
  13.6 19.0 %collective-permute-start.7 = (bf16[128,1408]{1,0:T(8,128)(2,1)S(1)}, bf16[128,1408]{1,0:T(8,128)(2,1)S(1)}, u32[]{:S(2)}, u32[]{:S(2)}) collective-permute-start(bf16[128,1408]{1,0:T(8,128)(2,1)S(1)} %get-tuple-element.32), channel_id=1, source_target_pairs={{0,18},{1,19},{2,16},{3,17},{4,22},{5,23},{6,20},{7,21},{8,26},{9,... | collective-permute-start | bytes 1081352 | tf_op jit(solution)/shard_map/ppermute | solution.py:189
  18.3 14.3 %collective-permute-start.3 = (bf16[64,1792]{1,0:T(8,128)(2,1)S(1)}, bf16[64,1792]{1,0:T(8,128)(2,1)S(1)}, u32[]{:S(2)}, u32[]{:S(2)}) collective-permute-start(bf16[64,1792]{1,0:T(8,128)(2,1)S(1)} %get-tuple-element.30.refs_6_), channel_id=1, source_target_pairs={{4,8},{5,9},{6,10},{7,11},{8,4},{9,5},{10,6},{11,7},{20,24},{21,25... | collective-permute-start | bytes 688136 | tf_op jit(solution)/shard_map/ppermute | solution.py:181
  20.7 11.9 %collective-permute-start.5 = (bf16[64,1792]{1,0:T(8,128)(2,1)S(1)}, bf16[64,1792]{1,0:T(8,128)(2,1)S(1)}, u32[]{:S(2)}, u32[]{:S(2)}) collective-permute-start(bf16[64,1792]{1,0:T(8,128)(2,1)S(1)} %collective-permute-done.4.refs_8_), channel_id=1, source_target_pairs={{4,0},{5,1},{6,2},{7,3},{8,12},{9,13},{10,14},{11,15},{20,16},{21,... | collective-permute-start | bytes 688136 | tf_op jit(solution)/shard_map/ppermute | solution.py:181
  22.0 10.6 %collective-permute-start.6 = (bf16[64,1280]{1,0:T(8,128)(2,1)S(1)}, bf16[64,1280]{1,0:T(8,128)(2,1)S(1)}, u32[]{:S(2)}, u32[]{:S(2)}) collective-permute-start(bf16[64,1280]{1,0:T(8,128)(2,1)S(1)} %collective-permute-done.2.refs_6_), channel_id=1, source_target_pairs={{0,8},{1,9},{2,10},{3,11},{4,12},{5,13},{6,14},{7,15},{8,0},{9,1},... | collective-permute-start | bytes 491528 | tf_op jit(solution)/shard_map/ppermute | solution.py:178
  25.8 7.4 %collective-permute-start.9 = (bf16[128,1408]{1,0:T(8,128)(2,1)S(1)}, bf16[128,1408]{1,0:T(8,128)(2,1)S(1)}, u32[]{:S(2)}, u32[]{:S(2)}) collective-permute-start(bf16[128,1408]{1,0:T(8,128)(2,1)S(1)} %get-tuple-element.36), channel_id=1, source_target_pairs={{0,2},{1,3},{2,0},{3,1},{4,6},{5,7},{6,4},{7,5},{8,10},{9,11},{10,... | collective-permute-start | bytes 1081352 | tf_op jit(solution)/shard_map/ppermute | solution.py:178
  32.6 18.0 %copy-start.1 = (bf16[128,5120]{1,0:T(8,128)(2,1)S(1)}, bf16[128,5120]{1,0:T(8,128)(2,1)}, u32[]{:S(2)}) copy-start(bf16[128,5120]{1,0:T(8,128)(2,1)} %hidden.1) | copy-start | bytes 3932164
  32.7 4.9 %collective-permute-start.8 = (bf16[256,1408]{1,0:T(8,128)(2,1)S(1)}, bf16[256,1408]{1,0:T(8,128)(2,1)S(1)}, u32[]{:S(2)}, u32[]{:S(2)}) collective-permute-start(bf16[256,1408]{1,0:T(8,128)(2,1)S(1)} %pad_maximum_fusion), channel_id=1, source_target_pairs={{0,1},{1,0},{2,3},{3,2},{4,5},{5,4},{6,7},{7,6},{8,9},{9,8},{10,11... | collective-permute-start | bytes 2162696 | tf_op jit(solution)/shard_map/ppermute | solution.py:178
  33.2 17.4 %copy-start = (bf16[5120,1024]{1,0:T(8,128)(2,1)S(1)}, bf16[5120,1024]{1,0:T(8,128)(2,1)}, u32[]{:S(2)}) copy-start(bf16[5120,1024]{1,0:T(8,128)(2,1)} %param.8) | copy-start | bytes 31457284
  33.3 5.9 %collective-permute-start.10 = (bf16[256,1408]{1,0:T(8,128)(2,1)S(1)}, bf16[256,1408]{1,0:T(8,128)(2,1)S(1)}, u32[]{:S(2)}, u32[]{:S(2)}) collective-permute-start(bf16[256,1408]{1,0:T(8,128)(2,1)S(1)} %pad_maximum_fusion.1), channel_id=1, source_target_pairs={{0,1},{1,0},{2,3},{3,2},{4,5},{5,4},{6,7},{7,6},{8,9},{9,8},{10,11... | collective-permute-start | bytes 2162696 | tf_op jit(solution)/shard_map/ppermute | solution.py:178
  33.5 15.7 %collective-permute-start.16 = (bf16[256,512]{1,0:T(8,128)(2,1)S(1)}, bf16[256,512]{1,0:T(8,128)(2,1)S(1)}, u32[]{:S(2)}, u32[]{:S(2)}) collective-permute-start(bf16[256,512]{1,0:T(8,128)(2,1)S(1)} %pad_maximum_fusion.2.refs_0_), channel_id=1, source_target_pairs={{0,16},{1,17},{2,18},{3,19},{4,20},{5,21},{6,22},{7,23},{8,24},{9,... | collective-permute-start | bytes 786440 | tf_op jit(solution)/shard_map/ppermute | solution.py:189
  34.1 7.0 %collective-permute-start.11 = (bf16[64,1280]{1,0:T(8,128)(2,1)S(1)}, bf16[64,1280]{1,0:T(8,128)(2,1)S(1)}, u32[]{:S(2)}, u32[]{:S(2)}) collective-permute-start(bf16[64,1280]{1,0:T(8,128)(2,1)S(1)} %collective-permute-done.2.refs_6_), channel_id=1, source_target_pairs={{0,4},{1,5},{2,6},{3,7},{4,0},{5,1},{6,2},{7,3},{8,12},{9,13},{10,... | collective-permute-start | bytes 491528 | tf_op jit(solution)/shard_map/ppermute | solution.py:178
  35.1 10.4 %collective-permute-start.12 = (bf16[64,1280]{1,0:T(8,128)(2,1)S(1)}, bf16[64,1280]{1,0:T(8,128)(2,1)S(1)}, u32[]{:S(2)}, u32[]{:S(2)}) collective-permute-start(bf16[64,1280]{1,0:T(8,128)(2,1)S(1)} %collective-permute-done.2.refs_6_), channel_id=1, source_target_pairs={{0,12},{1,13},{2,14},{3,15},{4,8},{5,9},{6,10},{7,11},{8,4},{9,5},... | collective-permute-start | bytes 491528 | tf_op jit(solution)/shard_map/ppermute | solution.py:178
  37.6 14.7 %collective-permute-start.17 = (bf16[256,512]{1,0:T(8,128)(2,1)S(1)}, bf16[256,512]{1,0:T(8,128)(2,1)S(1)}, u32[]{:S(2)}, u32[]{:S(2)}) collective-permute-start(bf16[256,512]{1,0:T(8,128)(2,1)S(1)} %pad_maximum_fusion.2.refs_0_), channel_id=1, source_target_pairs={{0,2},{1,3},{2,0},{3,1},{4,6},{5,7},{6,4},{7,5},{8,10},{9,11},{10,... | collective-permute-start | bytes 786440 | tf_op jit(solution)/shard_map/ppermute | solution.py:178
  39.1 13.2 %collective-permute-start.18 = (bf16[256,512]{1,0:T(8,128)(2,1)S(1)}, bf16[256,512]{1,0:T(8,128)(2,1)S(1)}, u32[]{:S(2)}, u32[]{:S(2)}) collective-permute-start(bf16[256,512]{1,0:T(8,128)(2,1)S(1)} %pad_maximum_fusion.2.refs_0_), channel_id=1, source_target_pairs={{0,18},{1,19},{2,16},{3,17},{4,22},{5,23},{6,20},{7,21},{8,26},{9,... | collective-permute-start | bytes 786440 | tf_op jit(solution)/shard_map/ppermute | solution.py:189
  47.1 5.3 %collective-permute-start.13 = (f32[128,128]{1,0:T(8,128)S(1)}, f32[128,128]{1,0:T(8,128)S(1)}, u32[]{:S(2)}, u32[]{:S(2)}) collective-permute-start(f32[128,128]{1,0:T(8,128)S(1)} %get-tuple-element.41), channel_id=1, source_target_pairs={{0,16},{1,17},{2,18},{3,19},{4,20},{5,21},{6,22},{7,23},{8,24},{9,... | collective-permute-start | bytes 196616 | tf_op jit(solution)/shard_map/ppermute | solution.py:189
  47.7 5.5 %collective-permute-start.14 = (f32[128,128]{1,0:T(8,128)S(1)}, f32[128,128]{1,0:T(8,128)S(1)}, u32[]{:S(2)}, u32[]{:S(2)}) collective-permute-start(f32[128,128]{1,0:T(8,128)S(1)} %get-tuple-element.42), channel_id=1, source_target_pairs={{0,2},{1,3},{2,0},{3,1},{4,6},{5,7},{6,4},{7,5},{8,10},{9,11},{10,... | collective-permute-start | bytes 196616 | tf_op jit(solution)/shard_map/ppermute | solution.py:178
  49.2 5.2 %collective-permute-start.15 = (f32[128,128]{1,0:T(8,128)S(1)}, f32[128,128]{1,0:T(8,128)S(1)}, u32[]{:S(2)}, u32[]{:S(2)}) collective-permute-start(f32[128,128]{1,0:T(8,128)S(1)} %get-tuple-element.43), channel_id=1, source_target_pairs={{0,18},{1,19},{2,16},{3,17},{4,22},{5,23},{6,20},{7,21},{8,26},{9,... | collective-permute-start | bytes 196616 | tf_op jit(solution)/shard_map/ppermute | solution.py:189
  55.4 2.0 %collective-permute-start.19 = (f32[128,1024]{1,0:T(8,128)S(1)}, f32[128,1024]{1,0:T(8,128)S(1)}, u32[]{:S(2)}, u32[]{:S(2)}) collective-permute-start(f32[128,1024]{1,0:T(8,128)S(1)} %get-tuple-element.46), channel_id=1, source_target_pairs={{0,1},{1,0},{2,3},{3,2},{4,5},{5,4},{6,7},{7,6},{8,9},{9,8},{10,11... | collective-permute-start | bytes 1572872 | tf_op jit(solution)/shard_map/ppermute | solution.py:178
